TPU v7x, 256 devices: a whole 4x4x8 slice. The times are simulated.
256 devices in a mesh: grp: 8 (over z_lo, core), seq: 32 (over z_hi, y, x).
Axes of the slice: x: 4, y: 4, z: 8 (z_hi: 2, z_lo: 4; z = z_hi * 4 + z_lo), core: 2. Of those that a mesh axis runs over, the one named last changes fastest.
Arguments:
- q_resp: bfloat16 [8, 8192, 1280], P('grp', 'seq'), may hold values from -5 to 5
- resp_kv: bfloat16 [8, 8192, 512], P('grp', 'seq'), may hold values from -5 to 5
- prompt_kv: bfloat16 [8, 1024, 512], P(None, ('grp', 'seq')), may hold values from -5 to 5
- d_out: bfloat16 [8, 8192, 1280], P('grp', 'seq'), may hold values from -5 to 5
- resp_lengths: int32 [8, 32, 4], P('grp', 'seq'), may hold values from 1 to 128, 256 in all within a row
Outputs:
- attn_out: bfloat16 [8, 8192, 1280], P('grp', 'seq')
- d_query: bfloat16 [8, 8192, 1280], P('grp', 'seq')
- d_resp_kv: bfloat16 [8, 8192, 512], P('grp', 'seq')
- d_prompt_kv: bfloat16 [8, 1024, 512], P(None, ('grp', 'seq'))
Inputs may be any that keep to these rules, and one draw needn't show every extreme that they name: `resp_lengths`: on each device the lengths sum to 256; the longest response of a device has 128 tokens on some device.
All inputs are finite; a program needn't handle non-finite values.
Results may differ from a plain program's by a relative error of at most 0.03.
Values may be sent and summed in bfloat16 or wider, within the bound.
No kernel may reach another device: no remote copies, remote signals or barrier semaphores. Data moves between devices by JAX's collectives and lax.ppermute only.
A program may use at most 64 MiB of HBM per device.

v0:
```python
import jax
import jax.numpy as jnp
from jax import lax
from jax.sharding import PartitionSpec as P

HEADS = 10
KV_HEADS = 2
HEAD = 128


def segment_ids(lens, rows):
    ends = jnp.cumsum(lens)
    places = lax.iota(jnp.int32, rows)
    return jnp.sum((places[:, None] >= ends[None, :]).astype(jnp.int32), axis=1)


def on_device(q_resp, resp_kv, prompt_kv, d_out, resp_lengths):
    rows = q_resp.shape[1]
    width = KV_HEADS * HEAD
    repeat = HEADS // KV_HEADS
    scale = HEAD ** (-0.5)
    everything = lax.all_gather(prompt_kv, ("grp", "seq"), axis=1, tiled=True)
    own = lax.dynamic_index_in_dim(everything, lax.axis_index("grp"), 0, keepdims=False)
    own = own.reshape(lax.axis_size("grp"), lax.axis_size("seq"), -1, 2 * width).transpose(
        1, 0, 2, 3
    )
    gathered = own.reshape(-1, 2 * width)
    prompt_count = gathered.shape[0]
    seg = segment_ids(resp_lengths[0, 0], rows)
    places = lax.iota(jnp.int32, rows)
    self_ok = (seg[:, None] == seg[None, :]) & (places[None, :] <= places[:, None])
    allowed = jnp.concatenate([jnp.ones((rows, prompt_count), dtype=bool), self_ok], axis=1)
    resp_pair = resp_kv[0]
    keys_all = jnp.concatenate([gathered[:, :width], resp_pair[:, :width]], 0).reshape(
        -1, KV_HEADS, HEAD
    )
    vals_all = jnp.concatenate([gathered[:, width:], resp_pair[:, width:]], 0).reshape(
        -1, KV_HEADS, HEAD
    )
    queries = q_resp[0].reshape(rows, KV_HEADS, repeat, HEAD)
    grads_out = d_out[0].reshape(rows, KV_HEADS, repeat, HEAD)
    scores = (
        jnp.einsum("rgnd,jgd->gnrj", queries, keys_all, preferred_element_type=jnp.float32) * scale
    )
    scores = jnp.where(allowed[None, None], scores, -jnp.inf)
    top = jnp.max(scores, axis=-1, keepdims=True)
    weights = jnp.exp(scores - top)
    probs = weights / jnp.sum(weights, axis=-1, keepdims=True)
    probs_low = probs.astype(jnp.bfloat16)
    attn = jnp.einsum(
        "gnrj,jgd->rgnd", probs_low, vals_all, preferred_element_type=jnp.float32
    ).astype(jnp.bfloat16)
    delta = jnp.sum(grads_out.astype(jnp.float32) * attn.astype(jnp.float32), axis=-1).transpose(
        1, 2, 0
    )
    d_probs = jnp.einsum("rgnd,jgd->gnrj", grads_out, vals_all, preferred_element_type=jnp.float32)
    d_scores = (probs * (d_probs - delta[..., None])).astype(jnp.bfloat16)
    d_query = (
        scale * jnp.einsum("gnrj,jgd->rgnd", d_scores, keys_all, preferred_element_type=jnp.float32)
    ).astype(jnp.bfloat16)
    self_scores = d_scores[:, :, :, prompt_count:]
    self_probs = probs_low[:, :, :, prompt_count:]
    self_keys = scale * jnp.einsum(
        "gnrj,rgnd->jgd", self_scores, queries, preferred_element_type=jnp.float32
    )
    self_vals = jnp.einsum(
        "gnrj,rgnd->jgd", self_probs, grads_out, preferred_element_type=jnp.float32
    )
    d_self = jnp.concatenate(
        [self_keys.reshape(rows, width), self_vals.reshape(rows, width)], 1
    ).astype(jnp.bfloat16)
    count = prompt_count // lax.axis_size("seq") * lax.axis_size("seq")
    score_part = lax.slice_in_dim(d_scores, 0, count, axis=3)
    prob_part = lax.slice_in_dim(probs_low, 0, count, axis=3)
    part_keys = scale * jnp.einsum(
        "gnrj,rgnd->jgd", score_part, queries, preferred_element_type=jnp.float32
    )
    part_vals = jnp.einsum(
        "gnrj,rgnd->jgd", prob_part, grads_out, preferred_element_type=jnp.float32
    )
    summed = lax.psum_scatter(
        jnp.concatenate([part_keys.reshape(count, width), part_vals.reshape(count, width)], 1),
        "seq",
        scatter_dimension=0,
        tiled=True,
    )
    groups = lax.axis_size("grp")
    summed = summed.reshape(groups, 1, -1, 2 * width)
    returned = lax.all_to_all(summed, "grp", split_axis=0, concat_axis=1, tiled=True)
    d_prompt = returned.reshape(groups, -1, 2 * width).astype(jnp.bfloat16)
    return (
        attn.reshape(1, rows, HEADS * HEAD),
        d_query.reshape(1, rows, HEADS * HEAD),
        d_self.reshape(1, rows, 2 * width),
        d_prompt,
    )


def solution(mesh):
    in_specs = (
        P("grp", "seq", None),
        P("grp", "seq", None),
        P(None, ("grp", "seq"), None),
        P("grp", "seq", None),
        P("grp", "seq", None),
    )
    out_specs = (
        P("grp", "seq", None),
        P("grp", "seq", None),
        P("grp", "seq", None),
        P(None, ("grp", "seq"), None),
    )
    return jax.shard_map(
        on_device, mesh=mesh, in_specs=in_specs, out_specs=out_specs, check_vma=False
    )
```

profile of v0, /device:TPU:1, one launch (start us, length us, event | category | flops | bytes accessed | tf_op | source)
XLA Modules:
  0.0 1023.1 jit_solution(1801358041793836035)
XLA Ops:
  7.2 0.0 all-gather.2.cloned.1.call-start
  7.2 1.4 copy.92
  8.6 0.0 all-gather.2.cloned.1.call-update
  8.6 0.0 reduce-scatter.4.cloned.1.call-start
  8.7 0.8 reduce-window.8
  9.5 1.3 copy.96
  10.8 0.0 copy-start.5
  10.8 2.4 copy.100
  13.2 0.1 convert_reduce_fusion
  13.3 0.1 fusion.40
  13.4 0.1 concatenate.28
  13.5 1.0 fusion.44
  14.5 717.5 %all-gather.2.cloned.1.call-done = bf16[8,1024,512]{2,0,1:T(8,128)(2,1)} async-done(((bf16[8,4,512]{2,0,1:T(8,128)(2,1)}), bf16[8,1024,512]{2,0,1:T(8,128)(2,1)}) %all-gather.2.cloned.1.call-update) | async-done | bytes 8388624 | tf_op jit(solution)/shard_map/all_gather | solution.py:22
  732.0 9.8 dynamic-slice_reduce_fusion
  741.9 0.5 reshape.109
  742.3 0.5 copy.93
  742.9 0.3 reshape.110
  743.2 0.1 fusion.43
  743.3 0.1 pad_maximum_fusion.1
  743.3 0.2 copy.94
  743.6 0.2 copy.95
  743.8 0.0 copy-start.3
  743.9 7.2 fusion.45
  751.1 0.0 copy-done.3
  751.1 0.0 copy-start.2
  751.1 8.7 fusion.7
  759.8 0.0 copy-start
  759.8 0.0 copy-done.2
  759.8 4.4 fusion.8
  764.2 0.0 copy-done
  764.2 1.1 multiply_reduce_fusion
  765.3 5.8 fusion.2
  771.2 0.0 copy-done.5
  771.2 0.0 copy-start.1
  771.2 1.8 fusion.18
  773.0 0.9 copy-done.1
  773.9 0.1 pad_maximum_fusion
  774.0 1.9 copy.134
  775.9 0.0 copy-start.4
  775.9 0.0 reduce-scatter.4.cloned.1.call-update
  775.9 1.9 fusion.37
  777.9 0.1 copy.107
  778.0 2.0 fusion.34
  780.0 0.1 copy.106
  780.1 0.0 copy-done.4
  780.2 3.9 fusion.17
  784.1 195.9 %reduce-scatter.4.cloned.1.call-done = f32[32,512]{1,0:T(8,128)} async-done(((f32[1024,512]{1,0:T(8,128)}), f32[32,512]{1,0:T(8,128)}) %reduce-scatter.4.cloned.1.call-update) | async-done | bytes 65552 | tf_op jit(solution)/shard_map/reduce_scatter | solution.py:81
  979.9 1.5 reshape.119
  981.4 29.3 %all-to-all-start = ((bf16[8,1,4,512]{3,2,1,0:T(4,128)(2,1)}), bf16[8,1,4,512]{3,2,1,0:T(4,128)(2,1)S(1)}, u32[]{:S(2)}, u32[]{:S(2)}) async-start(bf16[8,1,4,512]{3,2,1,0:T(4,128)(2,1)} %bitcast.37), calls=%async_computation | async-start | bytes 65536 | tf_op jit(solution)/shard_map/all_to_all | solution.py:89
  1010.7 0.7 pad_maximum_fusion.3
  1011.4 1.1 copy.113
  1012.5 1.1 copy.112
  1013.6 2.1 all-to-all-done
  1015.7 0.6 copy.138
Async XLA Ops:
  7.2 724.9 %all-gather.2.cloned.1.call-start = ((), (), s32[]{:S(2)}) async-start(), calls=%async_computation.2 | async-start | bytes 8421376 | tf_op jit(solution)/shard_map/all_gather | solution.py:22
  8.6 971.3 %reduce-scatter.4.cloned.1.call-start = ((), (), s32[]{:S(2)}) async-start(), calls=%async_computation.3 | async-start | bytes 2162688 | tf_op jit(solution)/shard_map/reduce_scatter | solution.py:81
  10.8 760.3 %copy-start.5 = (bf16[1,256,1280]{1,2,0:T(8,128)(2,1)}, bf16[1,256,1280]{1,2,0:T(8,128)(2,1)S(1)}, u32[]{:S(2)}) copy-start(bf16[1,256,1280]{1,2,0:T(8,128)(2,1)S(1)} %copy.96) | copy-start | bytes 1966084
  743.8 7.2 copy-start.3
  751.1 8.7 copy-start.2
  759.8 4.4 copy-start
  771.2 2.7 copy-start.1
  775.9 4.2 copy-start.4
  981.4 34.3 %all-to-all-start = ((bf16[8,1,4,512]{3,2,1,0:T(4,128)(2,1)}), bf16[8,1,4,512]{3,2,1,0:T(4,128)(2,1)S(1)}, u32[]{:S(2)}, u32[]{:S(2)}) async-start(bf16[8,1,4,512]{3,2,1,0:T(4,128)(2,1)} %bitcast.37), calls=%async_computation | async-start | bytes 65536 | tf_op jit(solution)/shard_map/all_to_all | solution.py:89
Sparse Core Ops, SparseCore 0:
  10.4 721.5 all-gather.1
  776.1 203.8 reduce-scatter.3
where the time goes:
time: 1020 us
  waiting for transfers between devices  916 us (90%)
  starting transfers between devices  29.3 us (3%)
  matrix products  28.2 us (3%)
  local copies, waits for them, and re-layouts  25.1 us (2%)
  between operations  14.2 us (1%)
  other arithmetic  10.7 us (1%)
    all_gather x1, waiting for transfers between devices, on_device(): everything = lax.all_gather(prompt_kv, ('grp', 'seq'), axis=1, tiled=True)  718 us
    reduce_scatter x1, waiting for transfers between devices, on_device(): lax.psum_scatter(jnp.concatenate([part_keys.reshape(count, width), part_v...  196 us
    all_to_all x1, starting transfers between devices, on_device(): lax.all_to_all(summed, 'grp', split_axis=0, concat_axis=1, tiled=True)  29.3 us
  transfers between devices with their start and end apart: 3, of which 3 were waited for; matrix products, arithmetic and copies ran while one was open for 2% of the time, Pallas kernels for 0%

commit v1 on v0

v1 whole, which is shorter than its diff:
```python
import functools

import jax
import jax.numpy as jnp
from jax import lax
from jax.experimental import pallas as pl
from jax.experimental.pallas import tpu as pltpu
from jax.sharding import Mesh
from jax.sharding import PartitionSpec as P

HEADS = 10
KV_HEADS = 2
HEAD = 128
REPEAT = HEADS // KV_HEADS
SCALE = HEAD ** (-0.5)
LOG2E = 1.4426950408889634
MASKED = -1e30
bf16 = jnp.bfloat16
f32 = jnp.float32
ALONG_X = 4


def dot_nn(a, b):
    return lax.dot_general(a, b, (((1,), (0,)), ((), ())), preferred_element_type=f32)


def dot_nt(a, b):
    return lax.dot_general(a, b, (((1,), (1,)), ((), ())), preferred_element_type=f32)


def self_bias(lens_ref, rows):
    key = lax.broadcasted_iota(jnp.int32, (rows, rows), 0)
    row = lax.broadcasted_iota(jnp.int32, (rows, rows), 1)
    key_seg = jnp.zeros((rows, rows), jnp.int32)
    row_seg = jnp.zeros((rows, rows), jnp.int32)
    end = jnp.int32(0)
    for i in range(lens_ref.shape[-1]):
        end = end + lens_ref[0, 0, i]
        key_seg += (key >= end).astype(jnp.int32)
        row_seg += (row >= end).astype(jnp.int32)
    return jnp.where((key_seg == row_seg) & (key <= row), 0.0, MASKED).astype(f32)


def attention_kernel(has_earlier, lens_ref, q_ref, do_ref, resp_k_ref, resp_v_ref, *refs):
    parts = refs[:ALONG_X]
    refs = refs[ALONG_X:]
    if has_earlier:
        earlier_self, refs = refs[0], refs[3:]
    attn_ref, dq_ref, d_self_ref = refs[:3]
    d_parts = refs[3 : 3 + ALONG_X]
    bias_ref, k_t, v_t, acc = refs[3 + ALONG_X :]
    rows = q_ref.shape[1]
    step = pl.program_id(0)
    span = parts[0].shape[0]
    total = ALONG_X * span

    @pl.when(step == 0)
    def _():
        bias_ref[...] = self_bias(lens_ref, rows)
        for i, part in enumerate(parts):
            k_t[:, i * span : (i + 1) * span] = part[:, :HEAD].T
            v_t[:, i * span : (i + 1) * span] = part[:, HEAD:].T
        k_t[:, total:] = resp_k_ref[0].T
        v_t[:, total:] = resp_v_ref[0].T

    q_t = q_ref[0].T
    do_t = do_ref[0].T
    keys = [part[:, :HEAD] for part in parts] + [resp_k_ref[0]]
    vals = [part[:, HEAD:] for part in parts] + [resp_v_ref[0]]
    places = [slice(i * span, (i + 1) * span) for i in range(ALONG_X)] + [slice(total, total + rows)]
    scores = [dot_nn(k, q_t) for k in keys]
    scores[-1] = scores[-1] + bias_ref[...]
    top = functools.reduce(
        jnp.maximum, [jnp.max(s, axis=0, keepdims=True) for s in scores]
    ) * (SCALE * LOG2E)
    weights = [jnp.exp2(s * (SCALE * LOG2E) - top) for s in scores]
    inverse = 1.0 / sum(jnp.sum(w, axis=0, keepdims=True) for w in weights)
    low = [w.astype(bf16) for w in weights]
    out_t = sum(dot_nn(v_t[:, at], w) for at, w in zip(places, low)) * inverse
    attn_ref[0] = out_t.T.astype(bf16)
    delta = jnp.sum(do_t.astype(f32) * out_t.astype(bf16).astype(f32), axis=0, keepdims=True)
    d_scores = [
        (w * (dot_nn(v, do_t) - delta)).astype(bf16) for v, w in zip(vals, weights)
    ]
    dq_t = sum(dot_nn(k_t[:, at], d) for at, d in zip(places, d_scores)) * (inverse * SCALE)
    dq_ref[0] = dq_t.T.astype(bf16)
    q_scaled = (q_t.astype(f32) * (inverse * SCALE)).astype(bf16)
    do_scaled = (do_t.astype(f32) * inverse).astype(bf16)

    def add(first):
        for i, (mine, theirs) in enumerate(((q_scaled, d_scores), (do_scaled, low))):
            for at, t in zip(places, theirs):
                new = dot_nt(mine, t)
                acc[i, :, at] = new if first else acc[i, :, at] + new

    @pl.when(step == 0)
    def _():
        add(True)

    @pl.when(step > 0)
    def _():
        add(False)

    @pl.when(step == REPEAT - 1)
    def _():
        for i in range(2):
            cols = slice(i * HEAD, (i + 1) * HEAD)
            for at, d_part in zip(places, d_parts):
                d_part[:, cols] = acc[i, :, at].T.astype(bf16)
            if has_earlier:
                d_self_ref[0, :, 2 * i * HEAD : (2 * i + 1) * HEAD] = earlier_self[0, :, cols]
                d_self_ref[0, :, (2 * i + 1) * HEAD : (2 * i + 2) * HEAD] = acc[
                    i, :, total:
                ].T.astype(bf16)
            else:
                d_self_ref[0, :, cols] = acc[i, :, total:].T.astype(bf16)


def attention(head, lens, q, do, resp, parts, earlier):
    rows = q.shape[1]
    span = parts[0].shape[0]
    keys = ALONG_X * span + rows
    block = lambda place: pl.BlockSpec((1, rows, HEAD), lambda h, p=place: (0, 0, p(h)))
    whole = lambda *shape: pl.BlockSpec(shape, lambda h: (0,) * len(shape))
    of_head = lambda h: head * REPEAT + h
    pair = whole(span, 2 * HEAD)
    has_earlier = earlier is not None
    in_specs = [
        pl.BlockSpec(memory_space=pltpu.SMEM),
        block(of_head),
        block(of_head),
        block(lambda h: head),
        block(lambda h: KV_HEADS + head),
    ] + [pair] * ALONG_X
    args = [lens, q, do, resp, resp, *parts]
    width = 2 * HEAD
    aliases = {}
    if has_earlier:
        width = 2 * KV_HEADS * HEAD
        attn, dq, d_self = earlier
        in_specs += [whole(1, rows, 2 * HEAD)] + [pl.BlockSpec(memory_space=pl.ANY)] * 2
        aliases = {len(args) + 1: 0, len(args) + 2: 1}
        args += [d_self, attn, dq]
    full = jax.ShapeDtypeStruct((1, rows, HEADS * HEAD), bf16)
    out = pl.pallas_call(
        functools.partial(attention_kernel, has_earlier),
        grid=(REPEAT,),
        in_specs=in_specs,
        out_specs=[block(of_head), block(of_head), whole(1, rows, width)] + [pair] * ALONG_X,
        out_shape=[full, full, jax.ShapeDtypeStruct((1, rows, width), bf16)]
        + [jax.ShapeDtypeStruct((span, 2 * HEAD), bf16)] * ALONG_X,
        scratch_shapes=[
            pltpu.VMEM((rows, rows), f32),
            pltpu.VMEM((HEAD, keys), bf16),
            pltpu.VMEM((HEAD, keys), bf16),
            pltpu.VMEM((2, HEAD, keys), f32),
        ],
        input_output_aliases=aliases,
        compiler_params=pltpu.CompilerParams(vmem_limit_bytes=32 << 20),
        cost_estimate=pl.CostEstimate(
            flops=12 * REPEAT * rows * keys * HEAD,
            bytes_accessed=4 << 20,
            transcendentals=REPEAT * rows * keys,
        ),
        name=f"attention_{head}",
    )(*args)
    return out[:3], out[3:]


def shifted(by):
    return [(i, (i + by) % ALONG_X) for i in range(ALONG_X)]


def on_device(q_resp, resp_kv, prompt_kv, d_out, resp_lengths):
    groups, own_rows, width = prompt_kv.shape
    ring = ("zl", "c", "zh", "y")
    copies = lax.axis_size("zh") * lax.axis_size("y")
    mine = prompt_kv.reshape(groups, own_rows, 2, KV_HEADS, HEAD).transpose(0, 3, 1, 2, 4)
    mine = mine.reshape(groups, 1, KV_HEADS, own_rows, 2 * HEAD)
    sent = jnp.broadcast_to(mine, (groups, copies) + mine.shape[2:])
    sent = sent.reshape((groups * copies,) + mine.shape[2:])
    got = lax.all_to_all(sent, ring, split_axis=0, concat_axis=0, tiled=True)
    got = got.transpose(1, 0, 2, 3).reshape(KV_HEADS, -1, 2 * HEAD)
    earlier = None
    sums = []
    pairs = []
    for head in range(KV_HEADS):
        own = got[head]
        pairs.append([own] + [lax.ppermute(own, "x", shifted(-by)) for by in (1, 3, 2)])
    for head in range(KV_HEADS):
        earlier, partial = attention(
            head, resp_lengths, q_resp, d_out, resp_kv, pairs[head], earlier
        )
        back = [partial[0]] + [
            lax.ppermute(t, "x", shifted(by)) for t, by in zip(partial[1:], (1, 3, 2))
        ]
        sums.append(sum(t.astype(f32) for t in back).astype(bf16))
    attn, dq, d_self = earlier
    total = jnp.stack(sums).reshape(KV_HEADS, groups * copies, own_rows, 2 * HEAD)
    total = lax.all_to_all(
        total.transpose(1, 0, 2, 3), ring, split_axis=0, concat_axis=0, tiled=True
    )
    total = total.reshape(groups, copies, KV_HEADS, own_rows, 2, HEAD)
    d_prompt = jnp.sum(total.astype(f32), axis=1).astype(bf16)
    d_prompt = d_prompt.transpose(0, 2, 3, 1, 4).reshape(groups, own_rows, width)
    return attn, dq, d_self, d_prompt


def solution(mesh):
    fine = Mesh(mesh.devices.reshape(4, 2, 2, 4, 4), ("zl", "c", "zh", "y", "x"))
    grp, seq = ("zl", "c"), ("zh", "y", "x")
    rows = P(grp, seq, None)
    prompt = P(None, grp + seq, None)
    return jax.shard_map(
        on_device,
        mesh=fine,
        in_specs=(rows, rows, prompt, rows, rows),
        out_specs=(rows, rows, rows, prompt),
        check_vma=False,
    )
```

time: 1020 us -> 97.4 us (0.10)
  waiting for transfers between devices: 916 us -> 5.96 us
  blocking collectives: 0 us -> 49.3 us
  matrix products: 28.2 us -> 0 us
  Pallas kernels: 0 us -> 24.5 us
  local copies, waits for them, and re-layouts: 25.1 us -> 1.93 us
  starting transfers between devices: 29.3 us -> 14.2 us
  between operations: 14.2 us -> 0.77 us
    all_gather x1 -> x0, waiting for transfers between devices: 718 us -> none  [on_device(): everything = lax.all_gather(prompt_kv, ('grp', 'seq'), axis=1, tiled=True)]
    reduce_scatter x1 -> x0, waiting for transfers between devices: 196 us -> none  [on_device(): lax.psum_scatter(jnp.concatenate([part_keys.reshape(count, width), part_v...]
    all_to_all x0 -> x2, blocking collectives: none -> 49.3 us  [the longest x1 25.5 us: on_device(): got = lax.all_to_all(sent, ring, split_axis=0, concat_axis=0, tiled=True)]
    all_to_all x1 -> x0, starting transfers between devices: 29.3 us -> none  [on_device(): lax.all_to_all(summed, 'grp', split_axis=0, concat_axis=1, tiled=True)]
    pallas_call x0 -> x2, Pallas kernels: none -> 24.5 us  [attention(): pl.pallas_call(functools.partial(attention_kernel, has_earlier), grid=(RE...]
    dot_general x7 -> x0, matrix products: 21 us -> none  [the longest x1 5.84 us: on_device(): jnp.einsum('rgnd,jgd->gnrj', grads_out, vals_all, preferred_element_type=...]
    ppermute x0 -> x12, starting transfers between devices: none -> 14.2 us  [the longest x6 7.68 us: on_device(): lax.ppermute(own, 'x', shifted(-by))]
  transfers between devices with their start and end apart: 3 -> 12, of which waited for: 3 -> 3; matrix products, arithmetic and copies ran while one was open for 2% -> 0% of each run, Pallas kernels for 0% -> 25%
where the time goes in v1:
time: 97.4 us; the launch traced here: 97.2 us
  blocking collectives  49.3 us (51%)
  Pallas kernels  24.5 us (25%)
  starting transfers between devices  14.2 us (15%)
  waiting for transfers between devices  5.96 us (6%)
  local copies, waits for them, and re-layouts  1.93 us (2%)
    all_to_all x1, blocking collectives, on_device(): got = lax.all_to_all(sent, ring, split_axis=0, concat_axis=0, tiled=True)  25.5 us
    pallas_call x2, Pallas kernels, attention(): pl.pallas_call(functools.partial(attention_kernel, has_earlier), grid=(RE...  24.5 us
    all_to_all x1, blocking collectives, on_device(): lax.all_to_all(total.transpose(1, 0, 2, 3), ring, split_axis=0, concat_ax...  23.8 us
    ppermute x6, starting transfers between devices, on_device(): lax.ppermute(own, 'x', shifted(-by))  7.68 us
    ppermute x6, starting transfers between devices, on_device(): lax.ppermute(t, 'x', shifted(by))  6.49 us
    ppermute x6, waiting for transfers between devices, on_device(): lax.ppermute(t, 'x', shifted(by))  4.14 us
  transfers between devices with their start and end apart: 12, of which 3 were waited for; matrix products, arithmetic and copies ran while one was open for 0% of the time, Pallas kernels for 25%

profile of v1, /device:TPU:1, one launch (start us, length us, event | category | flops | bytes accessed | tf_op | source)
XLA Modules:
  0.0 97.2 jit_solution(10144710360750291641)
XLA Ops:
  0.6 0.8 reshape.32
  1.5 0.1 broadcast_in_dim.8
  1.6 0.0 copy-start.1
  1.6 25.5 %all_to_all.10 = bf16[64,2,4,256]{3,2,1,0:T(4,128)(2,1)S(1)} all-to-all(bf16[64,2,4,256]{3,2,1,0:T(4,128)(2,1)S(1)} %bitcast.18), channel_id=1, replica_groups=mesh['zl'=4,'c'=2,'zh'=2,'y'=4,'x'=4] {'zl','c','zh','y'}, dimensions={0} | all-to-all | bytes 524288 | tf_op jit(solution)/shard_map/all_to_all | solution.py:182
  27.1 0.0 copy-start
  27.1 0.1 fusion
  27.2 0.0 copy-start.2
  27.2 2.6 %collective-permute-start.3 = (bf16[256,256]{1,0:T(8,128)(2,1)S(1)}, bf16[256,256]{1,0:T(8,128)(2,1)S(1)}, u32[]{:S(2)}, u32[]{:S(2)}) collective-permute-start(bf16[256,256]{1,0:T(8,128)(2,1)S(1)} %squeeze.7.refs_0_), channel_id=1, source_target_pairs={{0,3},{1,0},{2,1},{3,2},{4,7},{5,4},{6,5},{7,6},{8,11},{9,8},{10,9... | collective-permute-start | bytes 393224 | tf_op jit(solution)/shard_map/ppermute | solution.py:189
  29.8 0.0 collective-permute-start.4
  29.8 1.7 %collective-permute-start.5 = (bf16[256,256]{1,0:T(8,128)(2,1)S(1)}, bf16[256,256]{1,0:T(8,128)(2,1)S(1)}, u32[]{:S(2)}, u32[]{:S(2)}) collective-permute-start(bf16[256,256]{1,0:T(8,128)(2,1)S(1)} %squeeze.7.refs_0_), channel_id=1, source_target_pairs={{0,2},{1,3},{2,0},{3,1},{4,6},{5,7},{6,4},{7,5},{8,10},{9,11},{10,... | collective-permute-start | bytes 393224 | tf_op jit(solution)/shard_map/ppermute | solution.py:189
  31.5 0.0 copy-start.3
  31.6 1.0 %collective-permute-start = (bf16[256,256]{1,0:T(8,128)(2,1)S(1)}, bf16[256,256]{1,0:T(8,128)(2,1)S(1)}, u32[]{:S(2)}, u32[]{:S(2)}) collective-permute-start(bf16[256,256]{1,0:T(8,128)(2,1)S(1)} %squeeze.6.refs_0_), channel_id=1, source_target_pairs={{0,3},{1,0},{2,1},{3,2},{4,7},{5,4},{6,5},{7,6},{8,11},{9,8},{10,9... | collective-permute-start | bytes 393224 | tf_op jit(solution)/shard_map/ppermute | solution.py:189
  32.6 0.7 collective-permute-start.1
  33.3 0.0 collective-permute-done.3.refs_1_
  33.3 1.7 %collective-permute-start.2 = (bf16[256,256]{1,0:T(8,128)(2,1)S(1)}, bf16[256,256]{1,0:T(8,128)(2,1)S(1)}, u32[]{:S(2)}, u32[]{:S(2)}) collective-permute-start(bf16[256,256]{1,0:T(8,128)(2,1)S(1)} %squeeze.6.refs_0_), channel_id=1, source_target_pairs={{0,2},{1,3},{2,0},{3,1},{4,6},{5,7},{6,4},{7,5},{8,10},{9,11},{10,... | collective-permute-start | bytes 393224 | tf_op jit(solution)/shard_map/ppermute | solution.py:189
  35.0 1.8 %collective-permute-done.4.refs_2_ = bf16[256,256]{1,0:T(8,128)(2,1)S(1)} collective-permute-done((bf16[256,256]{1,0:T(8,128)(2,1)S(1)}, bf16[256,256]{1,0:T(8,128)(2,1)S(1)}, u32[]{:S(2)}, u32[]{:S(2)}) %collective-permute-start.4) | collective-permute-done | bytes 131104 | tf_op jit(solution)/shard_map/ppermute | solution.py:189
  36.8 0.0 collective-permute-done.5.refs_3_
  36.8 0.0 copy-done.1
  36.8 0.0 copy-done
  36.8 0.0 copy-done.2
  36.8 0.0 copy-done.3
  36.8 12.2 %attention_0.1 = (bf16[1,256,1280]{2,1,0:T(8,128)(2,1)}, bf16[1,256,1280]{2,1,0:T(8,128)(2,1)}, bf16[1,256,256]{2,1,0:T(8,128)(2,1)S(1)}, bf16[256,256]{1,0:T(8,...) custom-call(s32[1,1,4]{2,1,0:T(1,128)S(1)} %copy-done.3, ...), custom_call_target="tpu_custom_call" | custom-call | flops 2516582400 | bytes 4194304 | tf_op jit(solution)/shard_map/attention_0/pallas_call | solution.py:145
  49.0 0.0 collective-permute-start.6
  49.0 2.7 %collective-permute-start.7 = (bf16[256,256]{1,0:T(8,128)(2,1)S(1)}, bf16[256,256]{1,0:T(8,128)(2,1)S(1)}, u32[]{:S(2)}, u32[]{:S(2)}) collective-permute-start(bf16[256,256]{1,0:T(8,128)(2,1)S(1)} %get-tuple-element.26), channel_id=1, source_target_pairs={{0,3},{1,0},{2,1},{3,2},{4,7},{5,4},{6,5},{7,6},{8,11},{9,8},{10,9... | collective-permute-start | bytes 393224 | tf_op jit(solution)/shard_map/ppermute | solution.py:195
  51.6 0.0 collective-permute-done.refs_1_
  51.6 0.0 collective-permute-start.8
  51.6 0.0 collective-permute-done.1.refs_2_
  51.6 0.0 collective-permute-done.2.refs_3_
  51.7 12.3 %attention_1.1 = (bf16[1,256,1280]{2,1,0:T(8,128)(2,1)}, bf16[1,256,1280]{2,1,0:T(8,128)(2,1)}, bf16[1,256,512]{2,1,0:T(8,128)(2,1)}, bf16[256,256]{1,0:T(8,128)...) custom-call(s32[1,1,4]{2,1,0:T(1,128)S(1)} %copy-done.3, ...), custom_call_target="tpu_custom_call", output_to_operand_aliasing={{0}: (10, {}), {1}: (11, {})} | custom-call | flops 2516582400 | bytes 4194304 | tf_op jit(solution)/shard_map/attention_1/pallas_call | solution.py:145
  64.0 1.2 %collective-permute-start.10 = (bf16[256,256]{1,0:T(8,128)(2,1)S(1)}, bf16[256,256]{1,0:T(8,128)(2,1)S(1)}, u32[]{:S(2)}, u32[]{:S(2)}) collective-permute-start(bf16[256,256]{1,0:T(8,128)(2,1)S(1)} %get-tuple-element.30), channel_id=1, source_target_pairs={{0,3},{1,0},{2,1},{3,2},{4,7},{5,4},{6,5},{7,6},{8,11},{9,8},{10,9... | collective-permute-start | bytes 393224 | tf_op jit(solution)/shard_map/ppermute | solution.py:195
  65.1 1.9 %collective-permute-start.11 = (bf16[256,256]{1,0:T(8,128)(2,1)S(1)}, bf16[256,256]{1,0:T(8,128)(2,1)S(1)}, u32[]{:S(2)}, u32[]{:S(2)}) collective-permute-start(bf16[256,256]{1,0:T(8,128)(2,1)S(1)} %get-tuple-element.31), channel_id=1, source_target_pairs={{0,2},{1,3},{2,0},{3,1},{4,6},{5,7},{6,4},{7,5},{8,10},{9,11},{10,... | collective-permute-start | bytes 393224 | tf_op jit(solution)/shard_map/ppermute | solution.py:195
  67.0 0.0 collective-permute-done.6
  67.0 0.8 collective-permute-start.9
  67.8 0.0 collective-permute-done.7
  67.8 0.0 collective-permute-done.8
  67.8 0.1 add_convert_fusion.1
  67.9 0.0 collective-permute-done.10
  67.9 2.5 %collective-permute-done.11 = bf16[256,256]{1,0:T(8,128)(2,1)S(1)} collective-permute-done((bf16[256,256]{1,0:T(8,128)(2,1)S(1)}, bf16[256,256]{1,0:T(8,128)(2,1)S(1)}, u32[]{:S(2)}, u32[]{:S(2)}) %collective-permute-start.11) | collective-permute-done | bytes 131104 | tf_op jit(solution)/shard_map/ppermute | solution.py:195
  70.4 1.6 %collective-permute-done.9 = bf16[256,256]{1,0:T(8,128)(2,1)S(1)} collective-permute-done((bf16[256,256]{1,0:T(8,128)(2,1)S(1)}, bf16[256,256]{1,0:T(8,128)(2,1)S(1)}, u32[]{:S(2)}, u32[]{:S(2)}) %collective-permute-start.9) | collective-permute-done | bytes 131104 | tf_op jit(solution)/shard_map/ppermute | solution.py:195
  72.0 0.1 add_convert_fusion
  72.2 0.2 maximum_bitcast_fusion
  72.3 23.8 %all_to_all.11 = bf16[64,2,4,256]{3,2,1,0:T(4,128)(2,1)S(1)} all-to-all(bf16[64,2,4,256]{3,2,1,0:T(4,128)(2,1)S(1)} %maximum_bitcast_fusion), channel_id=1, replica_groups=mesh['zl'=4,'c'=2,'zh'=2,'y'=4,'x'=4] {'zl','c','zh','y'}, dimensions={0} | all-to-all | bytes 524288 | tf_op jit(solution)/shard_map/all_to_all | solution.py:200
  96.2 0.1 reshape.34
  96.3 0.2 reduce_sum.12
  96.6 0.6 reshape.36
  (8 shorter events, 0.2 us)
Async XLA Ops:
  1.6 35.2 %copy-start.1 = (bf16[1,256,1280]{2,1,0:T(8,128)(2,1)S(1)}, bf16[1,256,1280]{2,1,0:T(8,128)(2,1)}, u32[]{:S(2)}) copy-start(bf16[1,256,1280]{2,1,0:T(8,128)(2,1)} %do_ref.3) | copy-start | bytes 1966084
  27.1 9.7 %copy-start = (bf16[1,256,1280]{2,1,0:T(8,128)(2,1)S(1)}, bf16[1,256,1280]{2,1,0:T(8,128)(2,1)}, u32[]{:S(2)}) copy-start(bf16[1,256,1280]{2,1,0:T(8,128)(2,1)} %q_ref.3) | copy-start | bytes 1966084
  27.2 9.6 %copy-start.2 = (bf16[1,256,512]{2,1,0:T(8,128)(2,1)S(1)}, bf16[1,256,512]{2,1,0:T(8,128)(2,1)}, u32[]{:S(2)}) copy-start(bf16[1,256,512]{2,1,0:T(8,128)(2,1)} %resp_v_ref.3) | copy-start | bytes 786436
  27.2 6.0 %collective-permute-start.3 = (bf16[256,256]{1,0:T(8,128)(2,1)S(1)}, bf16[256,256]{1,0:T(8,128)(2,1)S(1)}, u32[]{:S(2)}, u32[]{:S(2)}) collective-permute-start(bf16[256,256]{1,0:T(8,128)(2,1)S(1)} %squeeze.7.refs_0_), channel_id=1, source_target_pairs={{0,3},{1,0},{2,1},{3,2},{4,7},{5,4},{6,5},{7,6},{8,11},{9,8},{10,9... | collective-permute-start | bytes 393224 | tf_op jit(solution)/shard_map/ppermute | solution.py:189
  29.8 7.0 %collective-permute-start.4 = (bf16[256,256]{1,0:T(8,128)(2,1)S(1)}, bf16[256,256]{1,0:T(8,128)(2,1)S(1)}, u32[]{:S(2)}, u32[]{:S(2)}) collective-permute-start(bf16[256,256]{1,0:T(8,128)(2,1)S(1)} %squeeze.7.refs_0_), channel_id=1, source_target_pairs={{0,1},{1,2},{2,3},{3,0},{4,5},{5,6},{6,7},{7,4},{8,9},{9,10},{10,1... | collective-permute-start | bytes 393224 | tf_op jit(solution)/shard_map/ppermute | solution.py:189
  29.8 7.0 %collective-permute-start.5 = (bf16[256,256]{1,0:T(8,128)(2,1)S(1)}, bf16[256,256]{1,0:T(8,128)(2,1)S(1)}, u32[]{:S(2)}, u32[]{:S(2)}) collective-permute-start(bf16[256,256]{1,0:T(8,128)(2,1)S(1)} %squeeze.7.refs_0_), channel_id=1, source_target_pairs={{0,2},{1,3},{2,0},{3,1},{4,6},{5,7},{6,4},{7,5},{8,10},{9,11},{10,... | collective-permute-start | bytes 393224 | tf_op jit(solution)/shard_map/ppermute | solution.py:189
  31.5 5.3 %copy-start.3 = (s32[1,1,4]{2,1,0:T(1,128)S(1)}, s32[1,1,4]{2,1,0:T(1,128)}, u32[]{:S(2)}) copy-start(s32[1,1,4]{2,1,0:T(1,128)} %lens_ref.3) | copy-start | bytes 52
  31.6 20.1 %collective-permute-start = (bf16[256,256]{1,0:T(8,128)(2,1)S(1)}, bf16[256,256]{1,0:T(8,128)(2,1)S(1)}, u32[]{:S(2)}, u32[]{:S(2)}) collective-permute-start(bf16[256,256]{1,0:T(8,128)(2,1)S(1)} %squeeze.6.refs_0_), channel_id=1, source_target_pairs={{0,3},{1,0},{2,1},{3,2},{4,7},{5,4},{6,5},{7,6},{8,11},{9,8},{10,9... | collective-permute-start | bytes 393224 | tf_op jit(solution)/shard_map/ppermute | solution.py:189
  32.6 19.1 %collective-permute-start.1 = (bf16[256,256]{1,0:T(8,128)(2,1)S(1)}, bf16[256,256]{1,0:T(8,128)(2,1)S(1)}, u32[]{:S(2)}, u32[]{:S(2)}) collective-permute-start(bf16[256,256]{1,0:T(8,128)(2,1)S(1)} %squeeze.6.refs_0_), channel_id=1, source_target_pairs={{0,1},{1,2},{2,3},{3,0},{4,5},{5,6},{6,7},{7,4},{8,9},{9,10},{10,1... | collective-permute-start | bytes 393224 | tf_op jit(solution)/shard_map/ppermute | solution.py:189
  33.3 18.4 %collective-permute-start.2 = (bf16[256,256]{1,0:T(8,128)(2,1)S(1)}, bf16[256,256]{1,0:T(8,128)(2,1)S(1)}, u32[]{:S(2)}, u32[]{:S(2)}) collective-permute-start(bf16[256,256]{1,0:T(8,128)(2,1)S(1)} %squeeze.6.refs_0_), channel_id=1, source_target_pairs={{0,2},{1,3},{2,0},{3,1},{4,6},{5,7},{6,4},{7,5},{8,10},{9,11},{10,... | collective-permute-start | bytes 393224 | tf_op jit(solution)/shard_map/ppermute | solution.py:189
  49.0 18.1 %collective-permute-start.6 = (bf16[256,256]{1,0:T(8,128)(2,1)S(1)}, bf16[256,256]{1,0:T(8,128)(2,1)S(1)}, u32[]{:S(2)}, u32[]{:S(2)}) collective-permute-start(bf16[256,256]{1,0:T(8,128)(2,1)S(1)} %get-tuple-element.25), channel_id=1, source_target_pairs={{0,1},{1,2},{2,3},{3,0},{4,5},{5,6},{6,7},{7,4},{8,9},{9,10},{10,1... | collective-permute-start | bytes 393224 | tf_op jit(solution)/shard_map/ppermute | solution.py:195
  49.0 18.8 %collective-permute-start.7 = (bf16[256,256]{1,0:T(8,128)(2,1)S(1)}, bf16[256,256]{1,0:T(8,128)(2,1)S(1)}, u32[]{:S(2)}, u32[]{:S(2)}) collective-permute-start(bf16[256,256]{1,0:T(8,128)(2,1)S(1)} %get-tuple-element.26), channel_id=1, source_target_pairs={{0,3},{1,0},{2,1},{3,2},{4,7},{5,4},{6,5},{7,6},{8,11},{9,8},{10,9... | collective-permute-start | bytes 393224 | tf_op jit(solution)/shard_map/ppermute | solution.py:195
  51.6 16.1 %collective-permute-start.8 = (bf16[256,256]{1,0:T(8,128)(2,1)S(1)}, bf16[256,256]{1,0:T(8,128)(2,1)S(1)}, u32[]{:S(2)}, u32[]{:S(2)}) collective-permute-start(bf16[256,256]{1,0:T(8,128)(2,1)S(1)} %get-tuple-element.27), channel_id=1, source_target_pairs={{0,2},{1,3},{2,0},{3,1},{4,6},{5,7},{6,4},{7,5},{8,10},{9,11},{10,... | collective-permute-start | bytes 393224 | tf_op jit(solution)/shard_map/ppermute | solution.py:195
  64.0 3.9 %collective-permute-start.10 = (bf16[256,256]{1,0:T(8,128)(2,1)S(1)}, bf16[256,256]{1,0:T(8,128)(2,1)S(1)}, u32[]{:S(2)}, u32[]{:S(2)}) collective-permute-start(bf16[256,256]{1,0:T(8,128)(2,1)S(1)} %get-tuple-element.30), channel_id=1, source_target_pairs={{0,3},{1,0},{2,1},{3,2},{4,7},{5,4},{6,5},{7,6},{8,11},{9,8},{10,9... | collective-permute-start | bytes 393224 | tf_op jit(solution)/shard_map/ppermute | solution.py:195
  65.1 5.3 %collective-permute-start.11 = (bf16[256,256]{1,0:T(8,128)(2,1)S(1)}, bf16[256,256]{1,0:T(8,128)(2,1)S(1)}, u32[]{:S(2)}, u32[]{:S(2)}) collective-permute-start(bf16[256,256]{1,0:T(8,128)(2,1)S(1)} %get-tuple-element.31), channel_id=1, source_target_pairs={{0,2},{1,3},{2,0},{3,1},{4,6},{5,7},{6,4},{7,5},{8,10},{9,11},{10,... | collective-permute-start | bytes 393224 | tf_op jit(solution)/shard_map/ppermute | solution.py:195
  67.0 5.0 %collective-permute-start.9 = (bf16[256,256]{1,0:T(8,128)(2,1)S(1)}, bf16[256,256]{1,0:T(8,128)(2,1)S(1)}, u32[]{:S(2)}, u32[]{:S(2)}) collective-permute-start(bf16[256,256]{1,0:T(8,128)(2,1)S(1)} %get-tuple-element.29), channel_id=1, source_target_pairs={{0,1},{1,2},{2,3},{3,0},{4,5},{5,6},{6,7},{7,4},{8,9},{9,10},{10,1... | collective-permute-start | bytes 393224 | tf_op jit(solution)/shard_map/ppermute | solution.py:195

commit v2 on v1

v2 whole, which is shorter than its diff:
```python
import functools

import jax
import jax.numpy as jnp
from jax import lax
from jax.experimental import pallas as pl
from jax.experimental.pallas import tpu as pltpu
from jax.sharding import Mesh
from jax.sharding import PartitionSpec as P

HEADS = 10
KV_HEADS = 2
HEAD = 128
REPEAT = HEADS // KV_HEADS
SCALE = HEAD ** (-0.5)
LOG2E = 1.4426950408889634
MASKED = -1e30
bf16 = jnp.bfloat16
f32 = jnp.float32
ALONG_X = 4


def dot_nn(a, b):
    return lax.dot_general(a, b, (((1,), (0,)), ((), ())), preferred_element_type=f32)


def dot_nt(a, b):
    return lax.dot_general(a, b, (((1,), (1,)), ((), ())), preferred_element_type=f32)


def self_bias(lens_ref, rows):
    key = lax.broadcasted_iota(jnp.int32, (rows, rows), 0)
    row = lax.broadcasted_iota(jnp.int32, (rows, rows), 1)
    key_seg = jnp.zeros((rows, rows), jnp.int32)
    row_seg = jnp.zeros((rows, rows), jnp.int32)
    end = jnp.int32(0)
    for i in range(lens_ref.shape[-1]):
        end = end + lens_ref[0, 0, i]
        key_seg += (key >= end).astype(jnp.int32)
        row_seg += (row >= end).astype(jnp.int32)
    return jnp.where((key_seg == row_seg) & (key <= row), 0.0, MASKED).astype(f32)


def attention_kernel(has_earlier, lens_ref, q_ref, do_ref, resp_k_ref, resp_v_ref, *refs):
    parts = refs[:ALONG_X]
    refs = refs[ALONG_X:]
    if has_earlier:
        earlier_self, refs = refs[0], refs[3:]
    attn_ref, dq_ref, d_self_ref = refs[:3]
    d_parts = refs[3 : 3 + ALONG_X]
    bias_ref, k_t, v_t, acc, scores_ref, low_ref, d_probs_ref = refs[3 + ALONG_X :]
    rows = q_ref.shape[1]
    span = parts[0].shape[0]
    total = ALONG_X * span
    places = [slice(i * span, (i + 1) * span) for i in range(ALONG_X)] + [slice(total, total + rows)]
    keys = [part[:, :HEAD] for part in parts] + [resp_k_ref[0]]
    vals = [part[:, HEAD:] for part in parts] + [resp_v_ref[0]]
    last = len(keys) - 1
    bias_ref[...] = self_bias(lens_ref, rows)
    for at, k, v in zip(places, keys, vals):
        k_t[:, at] = k.T
        v_t[:, at] = v.T
    state = [{} for _ in range(REPEAT)]

    def over_keys(op, t):
        return op(t.reshape(t.shape[0] // 8, 8, rows), axis=0)

    def score_pass(h):
        q_t = q_ref[0, :, h * HEAD : (h + 1) * HEAD].T
        tops = []
        for i, (at, k) in enumerate(zip(places, keys)):
            s = dot_nn(k, q_t)
            if i == last:
                s = s + bias_ref[...]
            scores_ref[h % 2, at, :] = s
            tops.append(over_keys(jnp.max, s))
        top = jnp.max(functools.reduce(jnp.maximum, tops), axis=0, keepdims=True)
        state[h].update(q_t=q_t, top=top * (SCALE * LOG2E))

    def forward_pass(h):
        cols = slice(h * HEAD, (h + 1) * HEAD)
        top = state[h]["top"]
        do_t = do_ref[0, :, cols].T
        sums, out_t = [], 0.0
        for at, v in zip(places, vals):
            w = jnp.exp2(scores_ref[h % 2, at, :] * (SCALE * LOG2E) - top)
            sums.append(over_keys(jnp.sum, w))
            low = w.astype(bf16)
            low_ref[h % 2, at, :] = low
            d_probs_ref[h % 2, at, :] = dot_nn(v, do_t)
            out_t = out_t + dot_nn(v_t[:, at], low)
        inverse = 1.0 / jnp.sum(sum(sums), axis=0, keepdims=True)
        out_t = out_t * inverse
        attn_ref[0, :, cols] = out_t.T.astype(bf16)
        delta = jnp.sum(
            do_t.astype(f32) * out_t.astype(bf16).astype(f32), axis=0, keepdims=True
        )
        state[h].update(do_t=do_t, inverse=inverse, delta=delta)

    def backward_pass(h):
        inverse, delta = state[h]["inverse"], state[h]["delta"]
        q_scaled = (state[h]["q_t"].astype(f32) * (inverse * SCALE)).astype(bf16)
        do_scaled = (state[h]["do_t"].astype(f32) * inverse).astype(bf16)
        dq_t = 0.0
        for at in places:
            low = low_ref[h % 2, at, :]
            d_scores = (low.astype(f32) * (d_probs_ref[h % 2, at, :] - delta)).astype(bf16)
            dq_t = dq_t + dot_nn(k_t[:, at], d_scores)
            for j, (mine, theirs) in enumerate(((q_scaled, d_scores), (do_scaled, low))):
                new = dot_nt(mine, theirs)
                acc[j, :, at] = new if h == 0 else acc[j, :, at] + new
        dq_ref[0, :, h * HEAD : (h + 1) * HEAD] = (dq_t * (inverse * SCALE)).T.astype(bf16)

    score_pass(0)
    for h in range(REPEAT):
        forward_pass(h)
        if h + 1 < REPEAT:
            score_pass(h + 1)
        backward_pass(h)
    for j in range(2):
        cols = slice(j * HEAD, (j + 1) * HEAD)
        for at, d_part in zip(places, d_parts):
            d_part[:, cols] = acc[j, :, at].T.astype(bf16)
        own = acc[j, :, total:].T.astype(bf16)
        if has_earlier:
            d_self_ref[0, :, 2 * j * HEAD : (2 * j + 1) * HEAD] = earlier_self[0, :, cols]
            d_self_ref[0, :, (2 * j + 1) * HEAD : (2 * j + 2) * HEAD] = own
        else:
            d_self_ref[0, :, cols] = own


def attention(head, lens, q, do, resp, parts, earlier):
    rows = q.shape[1]
    span = parts[0].shape[0]
    keys = ALONG_X * span + rows
    block = lambda n, at: pl.BlockSpec((1, rows, n), lambda i: (0, 0, at))
    whole = lambda *shape: pl.BlockSpec(shape, lambda i: (0,) * len(shape))
    of_heads = block(REPEAT * HEAD, head)
    pair = whole(span, 2 * HEAD)
    has_earlier = earlier is not None
    in_specs = [
        pl.BlockSpec(memory_space=pltpu.SMEM),
        of_heads,
        of_heads,
        block(HEAD, head),
        block(HEAD, KV_HEADS + head),
    ] + [pair] * ALONG_X
    args = [lens, q, do, resp, resp, *parts]
    width = 2 * HEAD
    aliases = {}
    if has_earlier:
        width = 2 * KV_HEADS * HEAD
        attn, dq, d_self = earlier
        in_specs += [whole(1, rows, 2 * HEAD)] + [pl.BlockSpec(memory_space=pl.ANY)] * 2
        aliases = {len(args) + 1: 0, len(args) + 2: 1}
        args += [d_self, attn, dq]
    full = jax.ShapeDtypeStruct((1, rows, HEADS * HEAD), bf16)
    out = pl.pallas_call(
        functools.partial(attention_kernel, has_earlier),
        grid=(1,),
        in_specs=in_specs,
        out_specs=[of_heads, of_heads, whole(1, rows, width)] + [pair] * ALONG_X,
        out_shape=[full, full, jax.ShapeDtypeStruct((1, rows, width), bf16)]
        + [jax.ShapeDtypeStruct((span, 2 * HEAD), bf16)] * ALONG_X,
        scratch_shapes=[
            pltpu.VMEM((rows, rows), f32),
            pltpu.VMEM((HEAD, keys), bf16),
            pltpu.VMEM((HEAD, keys), bf16),
            pltpu.VMEM((2, HEAD, keys), f32),
            pltpu.VMEM((2, keys, rows), f32),
            pltpu.VMEM((2, keys, rows), bf16),
            pltpu.VMEM((2, keys, rows), f32),
        ],
        input_output_aliases=aliases,
        compiler_params=pltpu.CompilerParams(vmem_limit_bytes=32 << 20),
        cost_estimate=pl.CostEstimate(
            flops=12 * REPEAT * rows * keys * HEAD,
            bytes_accessed=4 << 20,
            transcendentals=REPEAT * rows * keys,
        ),
        name=f"attention_{head}",
    )(*args)
    return out[:3], out[3:]


def partner(by):
    return [(i, i ^ by) for i in range(ALONG_X)]


def on_device(q_resp, resp_kv, prompt_kv, d_out, resp_lengths):
    groups, own_rows, width = prompt_kv.shape
    ring = ("zl", "c", "zh", "y")
    copies = lax.axis_size("zh") * lax.axis_size("y")
    mine = prompt_kv.reshape(groups, own_rows, 2, KV_HEADS, HEAD).transpose(0, 3, 1, 2, 4)
    mine = mine.reshape(groups, 1, KV_HEADS, own_rows, 2 * HEAD)
    sent = jnp.broadcast_to(mine, (groups, copies) + mine.shape[2:])
    sent = sent.reshape((groups * copies,) + mine.shape[2:])
    got = lax.all_to_all(sent, ring, split_axis=0, concat_axis=0, tiled=True)
    got = got.transpose(1, 0, 2, 3).reshape(KV_HEADS, -1, 2 * HEAD)
    earlier = None
    sums = []
    pairs = []
    for head in range(KV_HEADS):
        own = got[head]
        pairs.append([own] + [lax.ppermute(own, "x", partner(by)) for by in (2, 1, 3)])
    for head in range(KV_HEADS):
        earlier, partial = attention(
            head, resp_lengths, q_resp, d_out, resp_kv, pairs[head], earlier
        )
        back = [partial[0]] + [
            lax.ppermute(t, "x", partner(by)) for t, by in zip(partial[1:], (2, 1, 3))
        ]
        sums.append(sum(t.astype(f32) for t in back).astype(bf16))
    attn, dq, d_self = earlier
    total = jnp.stack(sums).reshape(KV_HEADS, groups * copies, own_rows, 2 * HEAD)
    total = lax.all_to_all(
        total.transpose(1, 0, 2, 3), ring, split_axis=0, concat_axis=0, tiled=True
    )
    total = total.reshape(groups, copies, KV_HEADS, own_rows, 2, HEAD)
    d_prompt = jnp.sum(total.astype(f32), axis=1).astype(bf16)
    d_prompt = d_prompt.transpose(0, 2, 3, 1, 4).reshape(groups, own_rows, width)
    return attn, dq, d_self, d_prompt


def solution(mesh):
    fine = Mesh(mesh.devices.reshape(4, 2, 2, 4, 4), ("zl", "c", "zh", "y", "x"))
    grp, seq = ("zl", "c"), ("zh", "y", "x")
    rows = P(grp, seq, None)
    prompt = P(None, grp + seq, None)
    return jax.shard_map(
        on_device,
        mesh=fine,
        in_specs=(rows, rows, prompt, rows, rows),
        out_specs=(rows, rows, rows, prompt),
        check_vma=False,
    )
```

time: 97.4 us -> 87.9 us (0.902)
  Pallas kernels: 24.5 us -> 15.2 us
    pallas_call x2, Pallas kernels: 24.5 us -> 15.2 us  [attention(): pl.pallas_call(functools.partial(attention_kernel, has_earlier), grid=(1,...]
  transfers between devices with their start and end apart: 12 -> 12, of which waited for: 3 -> 3; matrix products, arithmetic and copies ran while one was open for 0% -> 0% of each run, Pallas kernels for 25% -> 17%
where the time goes in v2:
time: 87.9 us; the launch traced here: 87.7 us
  blocking collectives  48.7 us (55%)
  Pallas kernels  15.2 us (17%)
  starting transfers between devices  14.4 us (16%)
  waiting for transfers between devices  6.16 us (7%)
  local copies, waits for them, and re-layouts  1.93 us (2%)
    all_to_all x1, blocking collectives, on_device(): got = lax.all_to_all(sent, ring, split_axis=0, concat_axis=0, tiled=True)  25.5 us
    all_to_all x1, blocking collectives, on_device(): lax.all_to_all(total.transpose(1, 0, 2, 3), ring, split_axis=0, concat_ax...  23.2 us
    pallas_call x2, Pallas kernels, attention(): pl.pallas_call(functools.partial(attention_kernel, has_earlier), grid=(1,...  15.2 us
    ppermute x6, starting transfers between devices, on_device(): lax.ppermute(own, 'x', partner(by))  7.9 us
    ppermute x6, starting transfers between devices, on_device(): lax.ppermute(t, 'x', partner(by))  6.51 us
    ppermute x6, waiting for transfers between devices, on_device(): lax.ppermute(own, 'x', partner(by))  3.09 us
    ppermute x6, waiting for transfers between devices, on_device(): lax.ppermute(t, 'x', partner(by))  3.07 us
  transfers between devices with their start and end apart: 12, of which 3 were waited for; matrix products, arithmetic and copies ran while one was open for 0% of the time, Pallas kernels for 17%

profile of v2, /device:TPU:1, one launch (start us, length us, event | category | flops | bytes accessed | tf_op | source)
XLA Modules:
  0.0 87.7 jit_solution(5162877803223440199)
XLA Ops:
  0.6 0.8 reshape.32
  1.5 0.1 broadcast_in_dim.8
  1.6 0.0 copy-start.1
  1.6 25.5 %all_to_all.10 = bf16[64,2,4,256]{3,2,1,0:T(4,128)(2,1)S(1)} all-to-all(bf16[64,2,4,256]{3,2,1,0:T(4,128)(2,1)S(1)} %bitcast.18), channel_id=1, replica_groups=mesh['zl'=4,'c'=2,'zh'=2,'y'=4,'x'=4] {'zl','c','zh','y'}, dimensions={0} | all-to-all | bytes 524288 | tf_op jit(solution)/shard_map/all_to_all | solution.py:198
  27.1 0.0 copy-start
  27.1 0.1 fusion
  27.2 0.0 copy-start.2
  27.2 2.8 %collective-permute-start.3 = (bf16[256,256]{1,0:T(8,128)(2,1)S(1)}, bf16[256,256]{1,0:T(8,128)(2,1)S(1)}, u32[]{:S(2)}, u32[]{:S(2)}) collective-permute-start(bf16[256,256]{1,0:T(8,128)(2,1)S(1)} %squeeze.7.refs_0_), channel_id=1, source_target_pairs={{0,2},{1,3},{2,0},{3,1},{4,6},{5,7},{6,4},{7,5},{8,10},{9,11},{10,... | collective-permute-start | bytes 393224 | tf_op jit(solution)/shard_map/ppermute | solution.py:205
  30.1 0.3 collective-permute-start.4
  30.4 0.6 collective-permute-start.5
  30.9 0.0 copy-start.3
  31.0 2.5 %collective-permute-start = (bf16[256,256]{1,0:T(8,128)(2,1)S(1)}, bf16[256,256]{1,0:T(8,128)(2,1)S(1)}, u32[]{:S(2)}, u32[]{:S(2)}) collective-permute-start(bf16[256,256]{1,0:T(8,128)(2,1)S(1)} %squeeze.6.refs_0_), channel_id=1, source_target_pairs={{0,2},{1,3},{2,0},{3,1},{4,6},{5,7},{6,4},{7,5},{8,10},{9,11},{10,... | collective-permute-start | bytes 393224 | tf_op jit(solution)/shard_map/ppermute | solution.py:205
  33.5 0.3 collective-permute-start.1
  33.8 0.0 collective-permute-done.3.refs_1_
  33.8 1.4 %collective-permute-start.2 = (bf16[256,256]{1,0:T(8,128)(2,1)S(1)}, bf16[256,256]{1,0:T(8,128)(2,1)S(1)}, u32[]{:S(2)}, u32[]{:S(2)}) collective-permute-start(bf16[256,256]{1,0:T(8,128)(2,1)S(1)} %squeeze.6.refs_0_), channel_id=1, source_target_pairs={{0,3},{1,2},{2,1},{3,0},{4,7},{5,6},{6,5},{7,4},{8,11},{9,10},{10,... | collective-permute-start | bytes 393224 | tf_op jit(solution)/shard_map/ppermute | solution.py:205
  35.2 0.0 collective-permute-done.4.refs_2_
  35.2 3.1 %collective-permute-done.5.refs_3_ = bf16[256,256]{1,0:T(8,128)(2,1)S(1)} collective-permute-done((bf16[256,256]{1,0:T(8,128)(2,1)S(1)}, bf16[256,256]{1,0:T(8,128)(2,1)S(1)}, u32[]{:S(2)}, u32[]{:S(2)}) %collective-permute-start.5) | collective-permute-done | bytes 131104 | tf_op jit(solution)/shard_map/ppermute | solution.py:205
  38.3 0.0 copy-done.1
  38.3 0.0 copy-done
  38.3 0.0 copy-done.2
  38.3 0.0 copy-done.3
  38.3 7.5 %attention_0.1 = (bf16[1,256,1280]{2,1,0:T(8,128)(2,1)}, bf16[1,256,1280]{2,1,0:T(8,128)(2,1)}, bf16[1,256,256]{2,1,0:T(8,128)(2,1)S(1)}, bf16[256,256]{1,0:T(8,...) custom-call(s32[1,1,4]{2,1,0:T(1,128)S(1)} %copy-done.3, ...), custom_call_target="tpu_custom_call" | custom-call | flops 2516582400 | bytes 4194304 | tf_op jit(solution)/shard_map/attention_0/pallas_call | solution.py:158
  45.8 0.0 collective-permute-start.6
  45.8 0.0 collective-permute-start.7
  45.8 0.0 collective-permute-done.refs_1_
  45.8 3.2 %collective-permute-start.8 = (bf16[256,256]{1,0:T(8,128)(2,1)S(1)}, bf16[256,256]{1,0:T(8,128)(2,1)S(1)}, u32[]{:S(2)}, u32[]{:S(2)}) collective-permute-start(bf16[256,256]{1,0:T(8,128)(2,1)S(1)} %get-tuple-element.27), channel_id=1, source_target_pairs={{0,3},{1,2},{2,1},{3,0},{4,7},{5,6},{6,5},{7,4},{8,11},{9,10},{10,... | collective-permute-start | bytes 393224 | tf_op jit(solution)/shard_map/ppermute | solution.py:211
  49.1 0.0 collective-permute-done.1.refs_2_
  49.1 0.0 collective-permute-done.2.refs_3_
  49.1 7.7 %attention_1.1 = (bf16[1,256,1280]{2,1,0:T(8,128)(2,1)}, bf16[1,256,1280]{2,1,0:T(8,128)(2,1)}, bf16[1,256,512]{2,1,0:T(8,128)(2,1)}, bf16[256,256]{1,0:T(8,128)...) custom-call(s32[1,1,4]{2,1,0:T(1,128)S(1)} %copy-done.3, ...), custom_call_target="tpu_custom_call", output_to_operand_aliasing={{0}: (10, {}), {1}: (11, {})} | custom-call | flops 2516582400 | bytes 4194304 | tf_op jit(solution)/shard_map/attention_1/pallas_call | solution.py:158
  56.7 0.0 collective-permute-start.10
  56.7 0.3 collective-permute-start.11
  57.0 0.0 collective-permute-done.6
  57.0 3.0 %collective-permute-start.9 = (bf16[256,256]{1,0:T(8,128)(2,1)S(1)}, bf16[256,256]{1,0:T(8,128)(2,1)S(1)}, u32[]{:S(2)}, u32[]{:S(2)}) collective-permute-start(bf16[256,256]{1,0:T(8,128)(2,1)S(1)} %get-tuple-element.29), channel_id=1, source_target_pairs={{0,2},{1,3},{2,0},{3,1},{4,6},{5,7},{6,4},{7,5},{8,10},{9,11},{10,... | collective-permute-start | bytes 393224 | tf_op jit(solution)/shard_map/ppermute | solution.py:211
  60.0 0.0 collective-permute-done.7
  60.0 0.0 collective-permute-done.8
  60.0 0.1 add_convert_fusion.1
  60.1 0.4 collective-permute-done.10
  60.5 2.6 %collective-permute-done.11 = bf16[256,256]{1,0:T(8,128)(2,1)S(1)} collective-permute-done((bf16[256,256]{1,0:T(8,128)(2,1)S(1)}, bf16[256,256]{1,0:T(8,128)(2,1)S(1)}, u32[]{:S(2)}, u32[]{:S(2)}) %collective-permute-start.11) | collective-permute-done | bytes 131104 | tf_op jit(solution)/shard_map/ppermute | solution.py:211
  63.2 0.0 collective-permute-done.9
  63.2 0.1 add_convert_fusion
  63.3 0.2 maximum_bitcast_fusion
  63.5 23.2 %all_to_all.11 = bf16[64,2,4,256]{3,2,1,0:T(4,128)(2,1)S(1)} all-to-all(bf16[64,2,4,256]{3,2,1,0:T(4,128)(2,1)S(1)} %maximum_bitcast_fusion), channel_id=1, replica_groups=mesh['zl'=4,'c'=2,'zh'=2,'y'=4,'x'=4] {'zl','c','zh','y'}, dimensions={0} | all-to-all | bytes 524288 | tf_op jit(solution)/shard_map/all_to_all | solution.py:216
  86.6 0.1 reshape.34
  86.7 0.2 reduce_sum.12
  87.0 0.6 reshape.36
  (8 shorter events, 0.2 us)
Async XLA Ops:
  1.6 36.7 %copy-start.1 = (bf16[1,256,1280]{2,1,0:T(8,128)(2,1)S(1)}, bf16[1,256,1280]{2,1,0:T(8,128)(2,1)}, u32[]{:S(2)}) copy-start(bf16[1,256,1280]{2,1,0:T(8,128)(2,1)} %do_ref.3) | copy-start | bytes 1966084
  27.1 11.2 %copy-start = (bf16[1,256,1280]{2,1,0:T(8,128)(2,1)S(1)}, bf16[1,256,1280]{2,1,0:T(8,128)(2,1)}, u32[]{:S(2)}) copy-start(bf16[1,256,1280]{2,1,0:T(8,128)(2,1)} %q_ref.3) | copy-start | bytes 1966084
  27.2 11.1 %copy-start.2 = (bf16[1,256,512]{2,1,0:T(8,128)(2,1)S(1)}, bf16[1,256,512]{2,1,0:T(8,128)(2,1)}, u32[]{:S(2)}) copy-start(bf16[1,256,512]{2,1,0:T(8,128)(2,1)} %resp_v_ref.3) | copy-start | bytes 786436
  27.2 6.5 %collective-permute-start.3 = (bf16[256,256]{1,0:T(8,128)(2,1)S(1)}, bf16[256,256]{1,0:T(8,128)(2,1)S(1)}, u32[]{:S(2)}, u32[]{:S(2)}) collective-permute-start(bf16[256,256]{1,0:T(8,128)(2,1)S(1)} %squeeze.7.refs_0_), channel_id=1, source_target_pairs={{0,2},{1,3},{2,0},{3,1},{4,6},{5,7},{6,4},{7,5},{8,10},{9,11},{10,... | collective-permute-start | bytes 393224 | tf_op jit(solution)/shard_map/ppermute | solution.py:205
  30.1 5.1 %collective-permute-start.4 = (bf16[256,256]{1,0:T(8,128)(2,1)S(1)}, bf16[256,256]{1,0:T(8,128)(2,1)S(1)}, u32[]{:S(2)}, u32[]{:S(2)}) collective-permute-start(bf16[256,256]{1,0:T(8,128)(2,1)S(1)} %squeeze.7.refs_0_), channel_id=1, source_target_pairs={{0,1},{1,0},{2,3},{3,2},{4,5},{5,4},{6,7},{7,6},{8,9},{9,8},{10,11... | collective-permute-start | bytes 393224 | tf_op jit(solution)/shard_map/ppermute | solution.py:205
  30.4 7.9 %collective-permute-start.5 = (bf16[256,256]{1,0:T(8,128)(2,1)S(1)}, bf16[256,256]{1,0:T(8,128)(2,1)S(1)}, u32[]{:S(2)}, u32[]{:S(2)}) collective-permute-start(bf16[256,256]{1,0:T(8,128)(2,1)S(1)} %squeeze.7.refs_0_), channel_id=1, source_target_pairs={{0,3},{1,2},{2,1},{3,0},{4,7},{5,6},{6,5},{7,4},{8,11},{9,10},{10,... | collective-permute-start | bytes 393224 | tf_op jit(solution)/shard_map/ppermute | solution.py:205
  30.9 7.3 %copy-start.3 = (s32[1,1,4]{2,1,0:T(1,128)S(1)}, s32[1,1,4]{2,1,0:T(1,128)}, u32[]{:S(2)}) copy-start(s32[1,1,4]{2,1,0:T(1,128)} %lens_ref.3) | copy-start | bytes 52
  31.0 14.8 %collective-permute-start = (bf16[256,256]{1,0:T(8,128)(2,1)S(1)}, bf16[256,256]{1,0:T(8,128)(2,1)S(1)}, u32[]{:S(2)}, u32[]{:S(2)}) collective-permute-start(bf16[256,256]{1,0:T(8,128)(2,1)S(1)} %squeeze.6.refs_0_), channel_id=1, source_target_pairs={{0,2},{1,3},{2,0},{3,1},{4,6},{5,7},{6,4},{7,5},{8,10},{9,11},{10,... | collective-permute-start | bytes 393224 | tf_op jit(solution)/shard_map/ppermute | solution.py:205
  33.5 15.6 %collective-permute-start.1 = (bf16[256,256]{1,0:T(8,128)(2,1)S(1)}, bf16[256,256]{1,0:T(8,128)(2,1)S(1)}, u32[]{:S(2)}, u32[]{:S(2)}) collective-permute-start(bf16[256,256]{1,0:T(8,128)(2,1)S(1)} %squeeze.6.refs_0_), channel_id=1, source_target_pairs={{0,1},{1,0},{2,3},{3,2},{4,5},{5,4},{6,7},{7,6},{8,9},{9,8},{10,11... | collective-permute-start | bytes 393224 | tf_op jit(solution)/shard_map/ppermute | solution.py:205
  33.8 15.3 %collective-permute-start.2 = (bf16[256,256]{1,0:T(8,128)(2,1)S(1)}, bf16[256,256]{1,0:T(8,128)(2,1)S(1)}, u32[]{:S(2)}, u32[]{:S(2)}) collective-permute-start(bf16[256,256]{1,0:T(8,128)(2,1)S(1)} %squeeze.6.refs_0_), channel_id=1, source_target_pairs={{0,3},{1,2},{2,1},{3,0},{4,7},{5,6},{6,5},{7,4},{8,11},{9,10},{10,... | collective-permute-start | bytes 393224 | tf_op jit(solution)/shard_map/ppermute | solution.py:205
  45.8 11.2 %collective-permute-start.6 = (bf16[256,256]{1,0:T(8,128)(2,1)S(1)}, bf16[256,256]{1,0:T(8,128)(2,1)S(1)}, u32[]{:S(2)}, u32[]{:S(2)}) collective-permute-start(bf16[256,256]{1,0:T(8,128)(2,1)S(1)} %get-tuple-element.25), channel_id=1, source_target_pairs={{0,2},{1,3},{2,0},{3,1},{4,6},{5,7},{6,4},{7,5},{8,10},{9,11},{10,... | collective-permute-start | bytes 393224 | tf_op jit(solution)/shard_map/ppermute | solution.py:211
  45.8 14.2 %collective-permute-start.7 = (bf16[256,256]{1,0:T(8,128)(2,1)S(1)}, bf16[256,256]{1,0:T(8,128)(2,1)S(1)}, u32[]{:S(2)}, u32[]{:S(2)}) collective-permute-start(bf16[256,256]{1,0:T(8,128)(2,1)S(1)} %get-tuple-element.26), channel_id=1, source_target_pairs={{0,1},{1,0},{2,3},{3,2},{4,5},{5,4},{6,7},{7,6},{8,9},{9,8},{10,11... | collective-permute-start | bytes 393224 | tf_op jit(solution)/shard_map/ppermute | solution.py:211
  45.8 14.2 %collective-permute-start.8 = (bf16[256,256]{1,0:T(8,128)(2,1)S(1)}, bf16[256,256]{1,0:T(8,128)(2,1)S(1)}, u32[]{:S(2)}, u32[]{:S(2)}) collective-permute-start(bf16[256,256]{1,0:T(8,128)(2,1)S(1)} %get-tuple-element.27), channel_id=1, source_target_pairs={{0,3},{1,2},{2,1},{3,0},{4,7},{5,6},{6,5},{7,4},{8,11},{9,10},{10,... | collective-permute-start | bytes 393224 | tf_op jit(solution)/shard_map/ppermute | solution.py:211
  56.7 3.8 %collective-permute-start.10 = (bf16[256,256]{1,0:T(8,128)(2,1)S(1)}, bf16[256,256]{1,0:T(8,128)(2,1)S(1)}, u32[]{:S(2)}, u32[]{:S(2)}) collective-permute-start(bf16[256,256]{1,0:T(8,128)(2,1)S(1)} %get-tuple-element.30), channel_id=1, source_target_pairs={{0,1},{1,0},{2,3},{3,2},{4,5},{5,4},{6,7},{7,6},{8,9},{9,8},{10,11... | collective-permute-start | bytes 393224 | tf_op jit(solution)/shard_map/ppermute | solution.py:211
  56.7 6.4 %collective-permute-start.11 = (bf16[256,256]{1,0:T(8,128)(2,1)S(1)}, bf16[256,256]{1,0:T(8,128)(2,1)S(1)}, u32[]{:S(2)}, u32[]{:S(2)}) collective-permute-start(bf16[256,256]{1,0:T(8,128)(2,1)S(1)} %get-tuple-element.31), channel_id=1, source_target_pairs={{0,3},{1,2},{2,1},{3,0},{4,7},{5,6},{6,5},{7,4},{8,11},{9,10},{10,... | collective-permute-start | bytes 393224 | tf_op jit(solution)/shard_map/ppermute | solution.py:211
  57.0 6.1 %collective-permute-start.9 = (bf16[256,256]{1,0:T(8,128)(2,1)S(1)}, bf16[256,256]{1,0:T(8,128)(2,1)S(1)}, u32[]{:S(2)}, u32[]{:S(2)}) collective-permute-start(bf16[256,256]{1,0:T(8,128)(2,1)S(1)} %get-tuple-element.29), channel_id=1, source_target_pairs={{0,2},{1,3},{2,0},{3,1},{4,6},{5,7},{6,4},{7,5},{8,10},{9,11},{10,... | collective-permute-start | bytes 393224 | tf_op jit(solution)/shard_map/ppermute | solution.py:211

commit v3 on v2

v3 whole, which is shorter than its diff:
```python
import functools

import jax
import jax.numpy as jnp
from jax import lax
from jax.experimental import pallas as pl
from jax.experimental.pallas import tpu as pltpu
from jax.sharding import Mesh
from jax.sharding import PartitionSpec as P

HEADS = 10
KV_HEADS = 2
HEAD = 128
REPEAT = HEADS // KV_HEADS
SCALE = HEAD ** (-0.5)
LOG2E = 1.4426950408889634
MASKED = -1e30
PARTNERS = 3
SHIFTS = (2, 1, 3)
WIDTH = KV_HEADS * HEAD
bf16 = jnp.bfloat16
f32 = jnp.float32


def dot_nn(a, b):
    return lax.dot_general(a, b, (((1,), (0,)), ((), ())), preferred_element_type=f32)


def dot_nt(a, b):
    return lax.dot_general(a, b, (((1,), (1,)), ((), ())), preferred_element_type=f32)


def by_eights(op, t):
    return op(t.reshape(t.shape[0] // 8, 8, t.shape[1]), axis=0)


def of_keys(head):
    at = head // REPEAT * HEAD
    return slice(at, at + HEAD)


def of_vals(head):
    at = WIDTH + head // REPEAT * HEAD
    return slice(at, at + HEAD)


def of_head(head):
    return slice(head * HEAD, (head + 1) * HEAD)


def self_bias(lens_ref, rows):
    key = lax.broadcasted_iota(jnp.int32, (rows, rows), 0)
    row = lax.broadcasted_iota(jnp.int32, (rows, rows), 1)
    key_seg = jnp.zeros((rows, rows), jnp.int32)
    row_seg = jnp.zeros((rows, rows), jnp.int32)
    end = jnp.int32(0)
    for i in range(lens_ref.shape[-1]):
        end = end + lens_ref[0, 0, i]
        key_seg += (key >= end).astype(jnp.int32)
        row_seg += (row >= end).astype(jnp.int32)
    return jnp.where((key_seg == row_seg) & (key <= row), 0.0, MASKED).astype(f32)


def scaled(t, factor):
    return (t.astype(f32) * factor).astype(bf16)


def near_forward_kernel(
    lens_hbm, q_hbm, resp_hbm, own_ref, low_ref, out_ref, stat_ref,
    lens_ref, q_ref, resp_ref, bias_ref, scores_ref, arrived,
):
    rows, span = q_ref.shape[1], own_ref.shape[0]
    arriving = [
        pltpu.make_async_copy(source, target, arrived.at[i])
        for i, (source, target) in enumerate(
            ((lens_hbm, lens_ref), (resp_hbm, resp_ref), (q_hbm, q_ref))
        )
    ]
    for copy in arriving:
        copy.start()
    arriving[0].wait()
    bias_ref[...] = self_bias(lens_ref, rows)
    arriving[1].wait()
    arriving[2].wait()
    places = [slice(0, span), slice(span, span + rows)]
    vals_t = [
        (own_ref[:, of_vals(g * REPEAT)].T, resp_ref[0, :, of_vals(g * REPEAT)].T)
        for g in range(KV_HEADS)
    ]
    tops = {}

    def score_pass(h):
        q_t = q_ref[0, :, of_head(h)].T
        own = dot_nn(own_ref[:, of_keys(h)], q_t)
        resp = dot_nn(resp_ref[0, :, of_keys(h)], q_t) + bias_ref[...]
        scores_ref[h % 2, places[0]] = own
        scores_ref[h % 2, places[1]] = resp
        top = jnp.maximum(by_eights(jnp.max, own), by_eights(jnp.max, resp))
        tops[h] = jnp.max(top, axis=0, keepdims=True) * (SCALE * LOG2E)

    def forward_pass(h):
        sums, out_t = 0.0, 0.0
        for at, v_t in zip(places, vals_t[h // REPEAT]):
            weights = jnp.exp2(scores_ref[h % 2, at] * (SCALE * LOG2E) - tops[h])
            low = weights.astype(bf16)
            low_ref[h, at] = low
            sums = sums + by_eights(jnp.sum, weights)
            out_t = out_t + dot_nn(v_t, low)
        stat_ref[h, 0:8] = jnp.broadcast_to(tops[h], (8, rows))
        stat_ref[h, 8:16] = sums
        out_ref[h] = out_t.astype(bf16)

    score_pass(0)
    for h in range(HEADS):
        if h + 1 < HEADS:
            score_pass(h + 1)
        forward_pass(h)


def far_kernel(has_earlier, q_ref, do_ref, near_out_ref, near_stat_ref, *refs):
    pairs, refs = refs[:PARTNERS], refs[PARTNERS + has_earlier :]
    attn_ref, dq_ref, stat_ref = refs[:3]
    d_pairs, refs = refs[3 : 3 + PARTNERS], refs[3 + PARTNERS :]
    pair_t, acc, scores_ref, low_ref, d_probs_ref = refs
    rows, span = q_ref.shape[1], pairs[0].shape[0]
    places = [slice(i * span, (i + 1) * span) for i in range(PARTNERS)]
    for at, pair in zip(places, pairs):
        pair_t[:HEAD, at] = pair[:, :HEAD].T
        pair_t[HEAD:, at] = pair[:, HEAD:].T
    state = [{} for _ in range(REPEAT)]

    def score_pass(h):
        q_t = q_ref[0, :, of_head(h)].T
        tops = [near_stat_ref[h, 0:8]]
        for at, pair in zip(places, pairs):
            s = dot_nn(pair[:, :HEAD], q_t)
            scores_ref[h % 2, at] = s
            tops.append(by_eights(jnp.max, s) * (SCALE * LOG2E))
        top = jnp.max(functools.reduce(jnp.maximum, tops), axis=0, keepdims=True)
        state[h].update(q_t=q_t, top=top)

    def forward_pass(h):
        top = state[h]["top"]
        do_t = do_ref[0, :, of_head(h)].T
        before = jnp.exp2(near_stat_ref[h, 0:1] - top)
        sums = near_stat_ref[h, 8:16] * before
        out_t = near_out_ref[h].astype(f32) * before
        for at, pair in zip(places, pairs):
            w = jnp.exp2(scores_ref[h % 2, at] * (SCALE * LOG2E) - top)
            sums = sums + by_eights(jnp.sum, w)
            low = w.astype(bf16)
            low_ref[h % 2, at] = low
            d_probs_ref[h % 2, at] = dot_nn(pair[:, HEAD:], do_t)
            out_t = out_t + dot_nn(pair_t[HEAD:, at], low)
        inverse = 1.0 / jnp.sum(sums, axis=0, keepdims=True)
        out_t = out_t * inverse
        attn_ref[0, :, of_head(h)] = out_t.T.astype(bf16)
        delta = jnp.sum(
            do_t.astype(f32) * out_t.astype(bf16).astype(f32), axis=0, keepdims=True
        )
        stat_ref[h, 0:8] = jnp.broadcast_to(delta, (8, rows))
        stat_ref[h, 8:16] = jnp.broadcast_to(inverse * before, (8, rows))
        state[h].update(do_t=do_t, inverse=inverse, delta=delta)

    def backward_pass(h):
        inverse, delta = state[h]["inverse"], state[h]["delta"]
        q_scaled = scaled(state[h]["q_t"], inverse * SCALE)
        do_scaled = scaled(state[h]["do_t"], inverse)
        dq_t = 0.0
        for at in places:
            low = low_ref[h % 2, at]
            d_scores = (low.astype(f32) * (d_probs_ref[h % 2, at] - delta)).astype(bf16)
            dq_t = dq_t + dot_nn(pair_t[:HEAD, at], d_scores)
            for j, (mine, theirs) in enumerate(((q_scaled, d_scores), (do_scaled, low))):
                new = dot_nt(mine, theirs)
                acc[j, :, at] = new if h == 0 else acc[j, :, at] + new
        dq_ref[h] = (dq_t * (inverse * SCALE)).astype(bf16)

    score_pass(0)
    for h in range(REPEAT):
        forward_pass(h)
        if h + 1 < REPEAT:
            score_pass(h + 1)
        backward_pass(h)
    for at, d_pair in zip(places, d_pairs):
        d_pair[:, :HEAD] = acc[0, :, at].T.astype(bf16)
        d_pair[:, HEAD:] = acc[1, :, at].T.astype(bf16)


def near_backward_kernel(
    q_ref, do_ref, own_ref, resp_ref, low_ref, dq_0_ref, dq_1_ref, stat_0_ref, stat_1_ref,
    d_own_ref, d_resp_ref, dq_ref, acc, d_probs_ref,
):
    rows, span = q_ref.shape[1], own_ref.shape[0]
    places = [slice(0, span), slice(span, span + rows)]
    keys_t = [
        (own_ref[:, of_keys(g * REPEAT)].T, resp_ref[0, :, of_keys(g * REPEAT)].T)
        for g in range(KV_HEADS)
    ]
    d_outs = {}

    def d_probs_pass(h):
        d_outs[h] = do_ref[0, :, of_head(h)].T
        d_probs_ref[h % 2, places[0]] = dot_nn(own_ref[:, of_vals(h)], d_outs[h])
        d_probs_ref[h % 2, places[1]] = dot_nn(resp_ref[0, :, of_vals(h)], d_outs[h])

    def backward_pass(h):
        stat_ref, dq_part_ref = ((stat_0_ref, dq_0_ref), (stat_1_ref, dq_1_ref))[h // REPEAT]
        delta, share = stat_ref[h % REPEAT, 0:1], stat_ref[h % REPEAT, 8:9]
        q_scaled = scaled(q_ref[0, :, of_head(h)].T, share * SCALE)
        do_scaled = scaled(d_outs[h], share)
        dq_t = 0.0
        for at, k_t in zip(places, keys_t[h // REPEAT]):
            low = low_ref[h, at]
            d_scores = (low.astype(f32) * (d_probs_ref[h % 2, at] - delta)).astype(bf16)
            dq_t = dq_t + dot_nn(k_t, d_scores)
            for j, (mine, theirs) in enumerate(((q_scaled, d_scores), (do_scaled, low))):
                new = dot_nt(mine, theirs)
                acc[j, :, at] = new if h % REPEAT == 0 else acc[j, :, at] + new
        dq_t = dq_part_ref[h % REPEAT].astype(f32) + dq_t * (share * SCALE)
        dq_ref[0, :, of_head(h)] = dq_t.T.astype(bf16)
        if h % REPEAT == REPEAT - 1:
            for j, cols in enumerate((of_keys(h), of_vals(h))):
                d_own_ref[:, cols] = acc[j, :, places[0]].T
                d_resp_ref[0, :, cols] = acc[j, :, places[1]].T.astype(bf16)

    d_probs_pass(0)
    for h in range(HEADS):
        if h + 1 < HEADS:
            d_probs_pass(h + 1)
        backward_pass(h)


def whole(shape):
    return pl.BlockSpec(shape, lambda i: (0,) * len(shape))


def call(kernel, name, limit, outs, scratch, flops, exps, args, specs=(), out_specs=(), **kwargs):
    specs = list(specs) or [whole(t.shape) for t in args]
    return pl.pallas_call(
        kernel,
        grid=(1,),
        in_specs=specs,
        out_specs=list(out_specs) or [whole(shape) for shape, _ in outs],
        out_shape=[jax.ShapeDtypeStruct(shape, dtype) for shape, dtype in outs],
        scratch_shapes=[pltpu.VMEM(*t) if isinstance(t, tuple) else t for t in scratch],
        compiler_params=pltpu.CompilerParams(vmem_limit_bytes=limit << 20),
        cost_estimate=pl.CostEstimate(flops=flops, bytes_accessed=1 << 20, transcendentals=exps),
        name=name,
        **kwargs,
    )(*args)


def partner(by):
    return [(i, i ^ by) for i in range(PARTNERS + 1)]


def on_device(q_resp, resp_kv, prompt_kv, d_out, resp_lengths):
    groups, own_rows, width = prompt_kv.shape
    rows = q_resp.shape[1]
    ring = ("zl", "c", "zh", "y")
    copies = lax.axis_size(("zh", "y"))
    sent = jnp.broadcast_to(prompt_kv[:, None], (groups, copies, own_rows, width))
    sent = sent.reshape(-1, own_rows, width)
    own = lax.all_to_all(sent, ring, split_axis=0, concat_axis=0, tiled=True).reshape(-1, width)
    span = own.shape[0]
    near, far = span + rows, PARTNERS * span
    pairs = []
    for h in (0, REPEAT):
        pair = jnp.concatenate([own[:, of_keys(h)], own[:, of_vals(h)]], 1)
        pairs.append([lax.ppermute(pair, "x", partner(by)) for by in SHIFTS])

    flat, resp_kind = (q_resp.shape, bf16), (resp_kv.shape, bf16)
    product = 2 * rows * HEAD
    in_hbm = [pltpu.with_memory_space_constraint(t, pltpu.HBM) for t in (resp_lengths, q_resp, resp_kv)]
    low, near_out, near_stat = call(
        near_forward_kernel,
        "near_forward",
        16,
        [((HEADS, near, rows), bf16), ((HEADS, HEAD, rows), bf16), ((HEADS, 16, rows), f32)],
        [
            pltpu.SMEM(resp_lengths.shape, jnp.int32),
            pltpu.VMEM(q_resp.shape, bf16),
            pltpu.VMEM(resp_kv.shape, bf16),
            pltpu.VMEM((rows, rows), f32),
            pltpu.VMEM((2, near, rows), f32),
            pltpu.SemaphoreType.DMA((3,)),
        ],
        2 * HEADS * near * product,
        HEADS * near * rows,
        [*in_hbm, own],
        [pl.BlockSpec(memory_space=pltpu.HBM)] * 3 + [whole(own.shape)],
    )
    attn = None
    d_queries, stats, returned = [], [], []
    for g in range(KV_HEADS):
        of_group = pl.BlockSpec((1, rows, REPEAT * HEAD), lambda i, g=g: (0, 0, g))
        of_heads = lambda n, g=g: pl.BlockSpec((REPEAT, n, rows), lambda i: (g, 0, 0))
        pair_spec = whole((span, 2 * HEAD))
        specs = [of_group, of_group, of_heads(HEAD), of_heads(16)] + [pair_spec] * PARTNERS
        args = [q_resp, d_out, near_out, near_stat, *pairs[g]]
        if g:
            specs, args = specs + [pl.BlockSpec(memory_space=pl.ANY)], args + [attn]
        dq_kind, stat_kind = ((REPEAT, HEAD, rows), bf16), ((REPEAT, 16, rows), f32)
        attn, d_query, stat, *d_pairs = call(
            functools.partial(far_kernel, int(g > 0)),
            f"far_{g}",
            20,
            [flat, dq_kind, stat_kind] + [((span, 2 * HEAD), bf16)] * PARTNERS,
            [
                ((2 * HEAD, far), bf16),
                ((2, HEAD, far), f32),
                ((2, far, rows), f32),
                ((2, far, rows), bf16),
                ((2, far, rows), f32),
            ],
            6 * REPEAT * far * product,
            REPEAT * far * rows,
            args,
            specs,
            [of_group, whole(dq_kind[0]), whole(stat_kind[0])] + [pair_spec] * PARTNERS,
            input_output_aliases={len(args) - 1: 0} if g else {},
        )
        d_queries.append(d_query)
        stats.append(stat)
        if g:
            returned, d_pairs = lax.optimization_barrier((returned, d_pairs))
        returned.append([lax.ppermute(t, "x", partner(by)) for t, by in zip(d_pairs, SHIFTS)])
    d_own, d_resp, dq = call(
        near_backward_kernel,
        "near_backward",
        20,
        [(own.shape, f32), resp_kind, flat],
        [((2, HEAD, near), f32), ((2, near, rows), f32)],
        4 * HEADS * near * product,
        0,
        [q_resp, d_out, own, resp_kv, low, *d_queries, *stats],
    )
    total = [d_own[:, of_keys(0)], d_own[:, of_keys(REPEAT)], d_own[:, of_vals(0)], d_own[:, of_vals(REPEAT)]]
    for g in range(KV_HEADS):
        for t in returned[g]:
            total[g] = total[g] + t[:, :HEAD].astype(f32)
            total[KV_HEADS + g] = total[KV_HEADS + g] + t[:, HEAD:].astype(f32)
    total = jnp.concatenate(total, 1).astype(bf16).reshape(-1, own_rows, width)
    total = lax.all_to_all(total, ring, split_axis=0, concat_axis=0, tiled=True)
    total = total.reshape(groups, copies, own_rows, width)
    d_prompt = jnp.sum(total.astype(f32), axis=1).astype(bf16)
    return attn, dq, d_resp, d_prompt


def solution(mesh):
    fine = Mesh(mesh.devices.reshape(4, 2, 2, 4, 4), ("zl", "c", "zh", "y", "x"))
    grp, seq = ("zl", "c"), ("zh", "y", "x")
    rows = P(grp, seq, None)
    prompt = P(None, grp + seq, None)
    return jax.shard_map(
        on_device,
        mesh=fine,
        in_specs=(rows, rows, prompt, rows, rows),
        out_specs=(rows, rows, rows, prompt),
        check_vma=False,
    )
```

time: 87.9 us -> 83.4 us (0.949)
  waiting for transfers between devices: 6.16 us -> 1.59 us
  Pallas kernels: 15.2 us -> 17 us
  blocking collectives: 48.7 us -> 47.4 us
    ppermute x6, waiting for transfers between devices: 3.09 us -> 0.02 us  [on_device(): pairs.append([lax.ppermute(pair, 'x', partner(by)) for by in SHIFTS])]
    pallas_call x2 -> x4, Pallas kernels: 15.2 us -> 17 us  [call(): pl.pallas_call(kernel, grid=(1,), in_specs=specs, out_specs=list(out_spec...]
    ppermute x6, waiting for transfers between devices: 3.07 us -> 1.58 us  [on_device(): lax.ppermute(t, 'x', partner(by))]
    all_to_all x2, blocking collectives: 48.7 us -> 47.4 us  [the longest x1 25.4 us: on_device(): lax.all_to_all(sent, ring, split_axis=0, concat_axis=0, tiled=True)]
  transfers between devices with their start and end apart: 12 -> 12, of which waited for: 3 -> 2; matrix products, arithmetic and copies ran while one was open for 0% -> 0% of each run, Pallas kernels for 17% -> 20%
where the time goes in v3:
time: 83.4 us; the launch traced here: 83.2 us
  blocking collectives  47.4 us (57%)
  Pallas kernels  17 us (20%)
  starting transfers between devices  14.5 us (17%)
  waiting for transfers between devices  1.59 us (2%)
  local copies, waits for them, and re-layouts  1.06 us (1%)
  other arithmetic  1.03 us (1%)
    all_to_all x1, blocking collectives, on_device(): lax.all_to_all(sent, ring, split_axis=0, concat_axis=0, tiled=True)  25.4 us
    all_to_all x1, blocking collectives, on_device(): total = lax.all_to_all(total, ring, split_axis=0, concat_axis=0, tiled=True)  22 us
    pallas_call x4, Pallas kernels, call(): pl.pallas_call(kernel, grid=(1,), in_specs=specs, out_specs=list(out_spec...  17 us
    ppermute x6, starting transfers between devices, on_device(): pairs.append([lax.ppermute(pair, 'x', partner(by)) for by in SHIFTS])  7.97 us
    ppermute x6, starting transfers between devices, on_device(): lax.ppermute(t, 'x', partner(by))  6.51 us
  transfers between devices with their start and end apart: 12, of which 2 were waited for; matrix products, arithmetic and copies ran while one was open for 0% of the time, Pallas kernels for 20%

profile of v3, /device:TPU:1, one launch (start us, length us, event | category | flops | bytes accessed | tf_op | source)
XLA Modules:
  0.0 83.2 jit_solution(10537847794966654031)
XLA Ops:
  0.6 0.0 copy-start
  0.6 0.0 copy-start.1
  0.7 0.9 %broadcast_in_dim.2 = bf16[8,8,4,512]{3,2,1,0:T(4,128)(2,1)S(1)} broadcast(bf16[8,4,512]{2,1,0:T(4,128)(2,1)} %param.7), dimensions={0,2,3} | broadcast | bytes 294912 | tf_op jit(solution)/shard_map/broadcast_in_dim | solution.py:263
  1.6 25.4 %all_to_all.10 = bf16[64,4,512]{2,1,0:T(4,128)(2,1)S(1)} all-to-all(bf16[64,4,512]{2,1,0:T(4,128)(2,1)S(1)} %bitcast.7), channel_id=1, replica_groups=mesh['zl'=4,'c'=2,'zh'=2,'y'=4,'x'=4] {'zl','c','zh','y'}, dimensions={0} | all-to-all | bytes 524288 | tf_op jit(solution)/shard_map/all_to_all | solution.py:265
  27.0 0.1 reshape.28.own_ref
  27.1 2.6 %collective-permute-start.5 = (bf16[256,256]{1,0:T(8,128)(2,1)S(1)}, bf16[256,256]{1,0:T(8,128)(2,1)S(1)}, u32[]{:S(2)}, u32[]{:S(2)}) collective-permute-start(bf16[256,256]{1,0:T(8,128)(2,1)S(1)} %pad_maximum_fusion.2), channel_id=1, source_target_pairs={{0,3},{1,2},{2,1},{3,0},{4,7},{5,6},{6,5},{7,4},{8,11},{9,10},{10,... | collective-permute-start | bytes 393224 | tf_op jit(solution)/shard_map/ppermute | solution.py:271
  29.7 0.0 collective-permute-start.4
  29.7 1.4 %collective-permute-start.3 = (bf16[256,256]{1,0:T(8,128)(2,1)S(1)}, bf16[256,256]{1,0:T(8,128)(2,1)S(1)}, u32[]{:S(2)}, u32[]{:S(2)}) collective-permute-start(bf16[256,256]{1,0:T(8,128)(2,1)S(1)} %pad_maximum_fusion.2), channel_id=1, source_target_pairs={{0,2},{1,3},{2,0},{3,1},{4,6},{5,7},{6,4},{7,5},{8,10},{9,11},{10,... | collective-permute-start | bytes 393224 | tf_op jit(solution)/shard_map/ppermute | solution.py:271
  31.1 2.6 %collective-permute-start.2 = (bf16[256,256]{1,0:T(8,128)(2,1)S(1)}, bf16[256,256]{1,0:T(8,128)(2,1)S(1)}, u32[]{:S(2)}, u32[]{:S(2)}) collective-permute-start(bf16[256,256]{1,0:T(8,128)(2,1)S(1)} %pad_maximum_fusion.1), channel_id=1, source_target_pairs={{0,3},{1,2},{2,1},{3,0},{4,7},{5,6},{6,5},{7,4},{8,11},{9,10},{10,... | collective-permute-start | bytes 393224 | tf_op jit(solution)/shard_map/ppermute | solution.py:271
  33.6 0.0 collective-permute-start.1
  33.6 3.8 %near_forward.1 = (bf16[10,512,256]{2,1,0:T(8,128)(2,1)S(1)}, bf16[10,128,256]{2,1,0:T(8,128)(2,1)S(1)}, f32[10,16,256]{2,1,0:T(8,128)S(1)}) custom-call(s32[1,1,4]{2,1,0:T(1,128)} %lens_hbm.1, bf16[1,256,1280]{2,1,0:T(8,128)(2,1)} %q_ref.5, bf16[1,256,512]{2,1,0:T(8,128)(2,1)} %resp_ref.1, bf16[256,512]{1,0:T(8,128)(2,1)S(1)} %reshape.28.own_ref), custom_call_target="tpu_custom_call" | custom-call | flops 671088640 | bytes 1048576 | tf_op jit(solution)/shard_map/near_forward/pallas_call | solution.py:240
  37.5 0.0 collective-permute-done.5.refs_2_
  37.5 1.5 %collective-permute-start = (bf16[256,256]{1,0:T(8,128)(2,1)S(1)}, bf16[256,256]{1,0:T(8,128)(2,1)S(1)}, u32[]{:S(2)}, u32[]{:S(2)}) collective-permute-start(bf16[256,256]{1,0:T(8,128)(2,1)S(1)} %pad_maximum_fusion.1), channel_id=1, source_target_pairs={{0,2},{1,3},{2,0},{3,1},{4,6},{5,7},{6,4},{7,5},{8,10},{9,11},{10,... | collective-permute-start | bytes 393224 | tf_op jit(solution)/shard_map/ppermute | solution.py:271
  39.0 0.0 collective-permute-done.4.refs_1_
  39.0 0.0 collective-permute-done.3.refs_0_
  39.0 0.0 copy-done
  39.0 0.0 copy-done.1
  39.0 4.9 %far_0.1 = (bf16[1,256,1280]{2,1,0:T(8,128)(2,1)}, bf16[5,128,256]{2,1,0:T(8,128)(2,1)S(1)}, f32[5,16,256]{2,1,0:T(8,128)S(1)}, bf16[256,256]{1,0:T(8,128)(2,1)S...) custom-call(bf16[1,256,1280]{2,1,0:T(8,128)(2,1)S(1)} %copy-done, bf16[1,256,1280]{2,1,0:T(8,128)(2,1)S(1)} %copy-done.1, ...), custom_call_target="tpu_custom_call" | custom-call | flops 1509949440 | bytes 1048576 | tf_op jit(solution)/shard_map/far_0/pallas_call | solution.py:240
  43.9 1.6 %collective-permute-start.6 = (bf16[256,256]{1,0:T(8,128)(2,1)S(1)}, bf16[256,256]{1,0:T(8,128)(2,1)S(1)}, u32[]{:S(2)}, u32[]{:S(2)}) collective-permute-start(bf16[256,256]{1,0:T(8,128)(2,1)S(1)} %get-tuple-element.40), channel_id=1, source_target_pairs={{0,2},{1,3},{2,0},{3,1},{4,6},{5,7},{6,4},{7,5},{8,10},{9,11},{10,... | collective-permute-start | bytes 393224 | tf_op jit(solution)/shard_map/ppermute | solution.py:328
  45.5 1.5 %collective-permute-start.7 = (bf16[256,256]{1,0:T(8,128)(2,1)S(1)}, bf16[256,256]{1,0:T(8,128)(2,1)S(1)}, u32[]{:S(2)}, u32[]{:S(2)}) collective-permute-start(bf16[256,256]{1,0:T(8,128)(2,1)S(1)} %get-tuple-element.41), channel_id=1, source_target_pairs={{0,1},{1,0},{2,3},{3,2},{4,5},{5,4},{6,7},{7,6},{8,9},{9,8},{10,11... | collective-permute-start | bytes 393224 | tf_op jit(solution)/shard_map/ppermute | solution.py:328
  47.0 0.0 collective-permute-done.2.refs_2_
  47.0 0.2 collective-permute-start.8
  47.2 0.0 collective-permute-done.1.refs_1_
  47.2 0.0 collective-permute-done.refs_0_
  47.2 0.0 copy-start.2
  47.2 4.8 %far_1.1 = (bf16[1,256,1280]{2,1,0:T(8,128)(2,1)}, bf16[5,128,256]{2,1,0:T(8,128)(2,1)S(1)}, f32[5,16,256]{2,1,0:T(8,128)S(1)}, bf16[256,256]{1,0:T(8,128)(2,1)S...) custom-call(bf16[1,256,1280]{2,1,0:T(8,128)(2,1)S(1)} %copy-done, ...), custom_call_target="tpu_custom_call", output_to_operand_aliasing={{0}: (7, {})} | custom-call | flops 1509949440 | bytes 1048576 | tf_op jit(solution)/shard_map/far_1/pallas_call | solution.py:240
  52.0 0.0 collective-permute-done.6
  52.0 0.0 collective-permute-done.7
  52.0 1.5 %collective-permute-done.8 = bf16[256,256]{1,0:T(8,128)(2,1)S(1)} collective-permute-done((bf16[256,256]{1,0:T(8,128)(2,1)S(1)}, bf16[256,256]{1,0:T(8,128)(2,1)S(1)}, u32[]{:S(2)}, u32[]{:S(2)}) %collective-permute-start.8) | collective-permute-done | bytes 131104 | tf_op jit(solution)/shard_map/ppermute | solution.py:328
  53.5 0.2 collective-permute-start.9
  53.7 1.5 %collective-permute-start.10 = (bf16[256,256]{1,0:T(8,128)(2,1)S(1)}, bf16[256,256]{1,0:T(8,128)(2,1)S(1)}, u32[]{:S(2)}, u32[]{:S(2)}) collective-permute-start(bf16[256,256]{1,0:T(8,128)(2,1)S(1)} %get-tuple-element.50), channel_id=1, source_target_pairs={{0,1},{1,0},{2,3},{3,2},{4,5},{5,4},{6,7},{7,6},{8,9},{9,8},{10,11... | collective-permute-start | bytes 393224 | tf_op jit(solution)/shard_map/ppermute | solution.py:328
  55.2 1.6 %collective-permute-start.11 = (bf16[256,256]{1,0:T(8,128)(2,1)S(1)}, bf16[256,256]{1,0:T(8,128)(2,1)S(1)}, u32[]{:S(2)}, u32[]{:S(2)}) collective-permute-start(bf16[256,256]{1,0:T(8,128)(2,1)S(1)} %get-tuple-element.51), channel_id=1, source_target_pairs={{0,3},{1,2},{2,1},{3,0},{4,7},{5,6},{6,5},{7,4},{8,11},{9,10},{10,... | collective-permute-start | bytes 393224 | tf_op jit(solution)/shard_map/ppermute | solution.py:328
  56.8 0.0 copy-done.2
  56.8 3.4 %near_backward.1 = (f32[256,512]{1,0:T(8,128)S(1)}, bf16[1,256,512]{2,1,0:T(8,128)(2,1)}, bf16[1,256,1280]{2,1,0:T(8,128)(2,1)}) custom-call(bf16[1,256,1280]{2,1,0:T(8,128)(2,1)S(1)} %copy-done, bf16[1,256,1280]{2,1,0:T(8,128)(2,1)S(1)} %copy-done.1, bf16[256,512]{1,0:T(8,128)(2,1)S(1)} %reshape.28.own_ref, bf16[1,256,512]{2,1,0:T(8,128)(2,1)S(1)} %copy-done.2, ...), custom_call_target="tpu_custom_call" | custom-call | flops 1342177280 | bytes 1048576 | tf_op jit(solution)/shard_map/near_backward/pallas_call | solution.py:240
  60.1 0.0 collective-permute-done.9
  60.1 0.0 collective-permute-done.10
  60.1 0.1 collective-permute-done.11
  60.2 0.1 add_convert_fusion.3
  60.4 0.2 pad_maximum_fusion
  60.5 22.0 %all_to_all.11 = bf16[64,4,512]{2,1,0:T(4,128)(2,1)S(1)} all-to-all(bf16[64,4,512]{2,1,0:T(4,128)(2,1)S(1)} %pad_maximum_fusion), channel_id=1, replica_groups=mesh['zl'=4,'c'=2,'zh'=2,'y'=4,'x'=4] {'zl','c','zh','y'}, dimensions={0} | all-to-all | bytes 524288 | tf_op jit(solution)/shard_map/all_to_all | solution.py:345
  82.5 0.7 bitcast_reduce_fusion
  (3 shorter events, 0.1 us)
Async XLA Ops:
  0.6 38.3 %copy-start = (bf16[1,256,1280]{2,1,0:T(8,128)(2,1)S(1)}, bf16[1,256,1280]{2,1,0:T(8,128)(2,1)}, u32[]{:S(2)}) copy-start(bf16[1,256,1280]{2,1,0:T(8,128)(2,1)} %q_ref.5) | copy-start | bytes 1966084
  0.6 38.3 %copy-start.1 = (bf16[1,256,1280]{2,1,0:T(8,128)(2,1)S(1)}, bf16[1,256,1280]{2,1,0:T(8,128)(2,1)}, u32[]{:S(2)}) copy-start(bf16[1,256,1280]{2,1,0:T(8,128)(2,1)} %do_ref.5) | copy-start | bytes 1966084
  27.1 10.4 %collective-permute-start.5 = (bf16[256,256]{1,0:T(8,128)(2,1)S(1)}, bf16[256,256]{1,0:T(8,128)(2,1)S(1)}, u32[]{:S(2)}, u32[]{:S(2)}) collective-permute-start(bf16[256,256]{1,0:T(8,128)(2,1)S(1)} %pad_maximum_fusion.2), channel_id=1, source_target_pairs={{0,3},{1,2},{2,1},{3,0},{4,7},{5,6},{6,5},{7,4},{8,11},{9,10},{10,... | collective-permute-start | bytes 393224 | tf_op jit(solution)/shard_map/ppermute | solution.py:271
  29.7 9.3 %collective-permute-start.4 = (bf16[256,256]{1,0:T(8,128)(2,1)S(1)}, bf16[256,256]{1,0:T(8,128)(2,1)S(1)}, u32[]{:S(2)}, u32[]{:S(2)}) collective-permute-start(bf16[256,256]{1,0:T(8,128)(2,1)S(1)} %pad_maximum_fusion.2), channel_id=1, source_target_pairs={{0,1},{1,0},{2,3},{3,2},{4,5},{5,4},{6,7},{7,6},{8,9},{9,8},{10,11... | collective-permute-start | bytes 393224 | tf_op jit(solution)/shard_map/ppermute | solution.py:271
  29.7 9.3 %collective-permute-start.3 = (bf16[256,256]{1,0:T(8,128)(2,1)S(1)}, bf16[256,256]{1,0:T(8,128)(2,1)S(1)}, u32[]{:S(2)}, u32[]{:S(2)}) collective-permute-start(bf16[256,256]{1,0:T(8,128)(2,1)S(1)} %pad_maximum_fusion.2), channel_id=1, source_target_pairs={{0,2},{1,3},{2,0},{3,1},{4,6},{5,7},{6,4},{7,5},{8,10},{9,11},{10,... | collective-permute-start | bytes 393224 | tf_op jit(solution)/shard_map/ppermute | solution.py:271
  31.1 15.9 %collective-permute-start.2 = (bf16[256,256]{1,0:T(8,128)(2,1)S(1)}, bf16[256,256]{1,0:T(8,128)(2,1)S(1)}, u32[]{:S(2)}, u32[]{:S(2)}) collective-permute-start(bf16[256,256]{1,0:T(8,128)(2,1)S(1)} %pad_maximum_fusion.1), channel_id=1, source_target_pairs={{0,3},{1,2},{2,1},{3,0},{4,7},{5,6},{6,5},{7,4},{8,11},{9,10},{10,... | collective-permute-start | bytes 393224 | tf_op jit(solution)/shard_map/ppermute | solution.py:271
  33.6 13.5 %collective-permute-start.1 = (bf16[256,256]{1,0:T(8,128)(2,1)S(1)}, bf16[256,256]{1,0:T(8,128)(2,1)S(1)}, u32[]{:S(2)}, u32[]{:S(2)}) collective-permute-start(bf16[256,256]{1,0:T(8,128)(2,1)S(1)} %pad_maximum_fusion.1), channel_id=1, source_target_pairs={{0,1},{1,0},{2,3},{3,2},{4,5},{5,4},{6,7},{7,6},{8,9},{9,8},{10,11... | collective-permute-start | bytes 393224 | tf_op jit(solution)/shard_map/ppermute | solution.py:271
  37.5 9.7 %collective-permute-start = (bf16[256,256]{1,0:T(8,128)(2,1)S(1)}, bf16[256,256]{1,0:T(8,128)(2,1)S(1)}, u32[]{:S(2)}, u32[]{:S(2)}) collective-permute-start(bf16[256,256]{1,0:T(8,128)(2,1)S(1)} %pad_maximum_fusion.1), channel_id=1, source_target_pairs={{0,2},{1,3},{2,0},{3,1},{4,6},{5,7},{6,4},{7,5},{8,10},{9,11},{10,... | collective-permute-start | bytes 393224 | tf_op jit(solution)/shard_map/ppermute | solution.py:271
  43.9 8.1 %collective-permute-start.6 = (bf16[256,256]{1,0:T(8,128)(2,1)S(1)}, bf16[256,256]{1,0:T(8,128)(2,1)S(1)}, u32[]{:S(2)}, u32[]{:S(2)}) collective-permute-start(bf16[256,256]{1,0:T(8,128)(2,1)S(1)} %get-tuple-element.40), channel_id=1, source_target_pairs={{0,2},{1,3},{2,0},{3,1},{4,6},{5,7},{6,4},{7,5},{8,10},{9,11},{10,... | collective-permute-start | bytes 393224 | tf_op jit(solution)/shard_map/ppermute | solution.py:328
  45.5 6.5 %collective-permute-start.7 = (bf16[256,256]{1,0:T(8,128)(2,1)S(1)}, bf16[256,256]{1,0:T(8,128)(2,1)S(1)}, u32[]{:S(2)}, u32[]{:S(2)}) collective-permute-start(bf16[256,256]{1,0:T(8,128)(2,1)S(1)} %get-tuple-element.41), channel_id=1, source_target_pairs={{0,1},{1,0},{2,3},{3,2},{4,5},{5,4},{6,7},{7,6},{8,9},{9,8},{10,11... | collective-permute-start | bytes 393224 | tf_op jit(solution)/shard_map/ppermute | solution.py:328
  47.0 6.5 %collective-permute-start.8 = (bf16[256,256]{1,0:T(8,128)(2,1)S(1)}, bf16[256,256]{1,0:T(8,128)(2,1)S(1)}, u32[]{:S(2)}, u32[]{:S(2)}) collective-permute-start(bf16[256,256]{1,0:T(8,128)(2,1)S(1)} %get-tuple-element.42), channel_id=1, source_target_pairs={{0,3},{1,2},{2,1},{3,0},{4,7},{5,6},{6,5},{7,4},{8,11},{9,10},{10,... | collective-permute-start | bytes 393224 | tf_op jit(solution)/shard_map/ppermute | solution.py:328
  47.2 9.6 %copy-start.2 = (bf16[1,256,512]{2,1,0:T(8,128)(2,1)S(1)}, bf16[1,256,512]{2,1,0:T(8,128)(2,1)}, u32[]{:S(2)}) copy-start(bf16[1,256,512]{2,1,0:T(8,128)(2,1)} %resp_ref.1) | copy-start | bytes 786436
  53.5 6.6 %collective-permute-start.9 = (bf16[256,256]{1,0:T(8,128)(2,1)S(1)}, bf16[256,256]{1,0:T(8,128)(2,1)S(1)}, u32[]{:S(2)}, u32[]{:S(2)}) collective-permute-start(bf16[256,256]{1,0:T(8,128)(2,1)S(1)} %get-tuple-element.49), channel_id=1, source_target_pairs={{0,2},{1,3},{2,0},{3,1},{4,6},{5,7},{6,4},{7,5},{8,10},{9,11},{10,... | collective-permute-start | bytes 393224 | tf_op jit(solution)/shard_map/ppermute | solution.py:328
  53.7 6.4 %collective-permute-start.10 = (bf16[256,256]{1,0:T(8,128)(2,1)S(1)}, bf16[256,256]{1,0:T(8,128)(2,1)S(1)}, u32[]{:S(2)}, u32[]{:S(2)}) collective-permute-start(bf16[256,256]{1,0:T(8,128)(2,1)S(1)} %get-tuple-element.50), channel_id=1, source_target_pairs={{0,1},{1,0},{2,3},{3,2},{4,5},{5,4},{6,7},{7,6},{8,9},{9,8},{10,11... | collective-permute-start | bytes 393224 | tf_op jit(solution)/shard_map/ppermute | solution.py:328
  55.2 5.0 %collective-permute-start.11 = (bf16[256,256]{1,0:T(8,128)(2,1)S(1)}, bf16[256,256]{1,0:T(8,128)(2,1)S(1)}, u32[]{:S(2)}, u32[]{:S(2)}) collective-permute-start(bf16[256,256]{1,0:T(8,128)(2,1)S(1)} %get-tuple-element.51), channel_id=1, source_target_pairs={{0,3},{1,2},{2,1},{3,0},{4,7},{5,6},{6,5},{7,4},{8,11},{9,10},{10,... | collective-permute-start | bytes 393224 | tf_op jit(solution)/shard_map/ppermute | solution.py:328

commit v4 on v0

v4 whole, which is shorter than its diff:
```python
import functools

import jax
import jax.numpy as jnp
from jax import lax
from jax.experimental import pallas as pl
from jax.experimental.pallas import tpu as pltpu
from jax.sharding import Mesh
from jax.sharding import PartitionSpec as P

HEADS = 10
KV_HEADS = 2
HEAD = 128
REPEAT = HEADS // KV_HEADS
SCALE = HEAD ** (-0.5)
LOG2E = 1.4426950408889634
MASKED = -1e30
WIDTH = KV_HEADS * HEAD
ROWS = 256
bf16 = jnp.bfloat16
f32 = jnp.float32


def dot_nn(a, b):
    return lax.dot_general(a, b, (((1,), (0,)), ((), ())), preferred_element_type=f32)


def dot_nt(a, b):
    return lax.dot_general(a, b, (((1,), (1,)), ((), ())), preferred_element_type=f32)


def by_eights(op, t):
    return op(t.reshape(t.shape[0] // 8, 8, t.shape[1]), axis=0)


def of_keys(head):
    at = head // REPEAT * HEAD
    return slice(at, at + HEAD)


def of_vals(head):
    at = WIDTH + head // REPEAT * HEAD
    return slice(at, at + HEAD)


def of_head(head):
    return slice(head * HEAD, (head + 1) * HEAD)


def self_bias(lens_ref, rows):
    key = lax.broadcasted_iota(jnp.int32, (rows, rows), 0)
    row = lax.broadcasted_iota(jnp.int32, (rows, rows), 1)
    key_seg = jnp.zeros((rows, rows), jnp.int32)
    row_seg = jnp.zeros((rows, rows), jnp.int32)
    end = jnp.int32(0)
    for i in range(lens_ref.shape[-1]):
        end = end + lens_ref[0, 0, i]
        key_seg += (key >= end).astype(jnp.int32)
        row_seg += (row >= end).astype(jnp.int32)
    return jnp.where((key_seg == row_seg) & (key <= row), 0.0, MASKED).astype(f32)


def scaled(t, factor):
    return (t.astype(f32) * factor).astype(bf16)


def of_group(head):
    at = head // REPEAT * HEAD
    return slice(at, at + HEAD)


def start_all(copies, semaphores):
    started = []
    for i, (source, target) in enumerate(copies):
        started.append(pltpu.make_async_copy(source, target, semaphores.at[i]))
        started[-1].start()
    return started


def wait_all(copies):
    for copy in copies:
        copy.wait()


def halves(ref):
    return ref.at[:, :WIDTH], ref.at[:, WIDTH:]


def eight(row):
    return jnp.broadcast_to(row, (8, row.shape[1]))


def places_of(chunks):
    return [slice(i * ROWS, (i + 1) * ROWS) for i in range(len(chunks))]


def forward(q_ref, chunks, bias_ref, low_ref, out_ref, stat_ref, scores_ref):
    places = places_of(chunks)
    vals_t = [[v[:, of_group(g * REPEAT)].T for _, v in chunks] for g in range(KV_HEADS)]
    tops = {}

    def score_pass(h):
        q_t = q_ref[0, :, of_head(h)].T
        top = None
        for at, (k, _) in zip(places, chunks):
            s = dot_nn(k[:, of_group(h)], q_t)
            if bias_ref is not None and at is places[-1]:
                s = s + bias_ref[...]
            scores_ref[h % 2, at] = s
            s = by_eights(jnp.max, s)
            top = s if top is None else jnp.maximum(top, s)
        tops[h] = jnp.max(top, axis=0, keepdims=True) * (SCALE * LOG2E)

    def weight_pass(h):
        sums, out_t = 0.0, 0.0
        for at, v_t in zip(places, vals_t[h // REPEAT]):
            weights = jnp.exp2(scores_ref[h % 2, at] * (SCALE * LOG2E) - tops[h])
            low = weights.astype(bf16)
            low_ref[h, at] = low
            sums = sums + by_eights(jnp.sum, weights)
            out_t = out_t + dot_nn(v_t, low)
        stat_ref[h, 0:8] = eight(tops[h])
        stat_ref[h, 8:16] = sums
        out_ref[h] = out_t.astype(bf16)

    score_pass(0)
    for h in range(HEADS):
        if h + 1 < HEADS:
            score_pass(h + 1)
        weight_pass(h)


def backward(q_ref, do_ref, chunks, lows, shares, stat_ref, acc, d_probs_ref, put_dq, put_sums):
    places = places_of(chunks)
    keys_t = [[k[:, of_group(g * REPEAT)].T for k, _ in chunks] for g in range(KV_HEADS)]
    d_outs = {}

    def d_probs_pass(h):
        d_outs[h] = do_ref[0, :, of_head(h)].T
        for at, (_, v) in zip(places, chunks):
            d_probs_ref[h % 2, at] = dot_nn(v[:, of_group(h)], d_outs[h])

    def add(h, j, at, new):
        acc[j, :, at] = new if h % REPEAT == 0 else acc[j, :, at] + new

    def gradient_pass(h):
        delta = stat_ref[h, 0:1]
        share = {at: stat_ref[h, at : at + 1] for at in set(shares)}
        do_scaled = {at: scaled(d_outs[h], t) for at, t in share.items()}
        q_t = q_ref[0, :, of_head(h)].T
        q_scaled = {at: scaled(q_t, t * SCALE) for at, t in share.items()}
        for at, low, which in zip(places, lows, shares):
            add(h, 1, at, dot_nt(do_scaled[which], low(h)))
        dq_t = {at: 0.0 for at in share}
        for at, low, which, k_t in zip(places, lows, shares, keys_t[h // REPEAT]):
            d_probs = d_probs_ref[h % 2, at] - delta
            d_scores = (low(h).astype(f32) * d_probs).astype(bf16)
            dq_t[which] = dq_t[which] + dot_nn(k_t, d_scores)
            add(h, 0, at, dot_nt(q_scaled[which], d_scores))
        put_dq(h, sum(dq_t[at] * (share[at] * SCALE) for at in sorted(share)))
        if h % REPEAT == REPEAT - 1:
            for j in range(2):
                put_sums(j, of_group(h), [acc[j, :, at].T for at in places])

    d_probs_pass(0)
    for h in range(HEADS):
        if h + 1 < HEADS:
            d_probs_pass(h + 1)
        gradient_pass(h)


def self_forward_kernel(
    lens_hbm, q_hbm, resp_hbm, low_hbm, out_hbm, stat_hbm,
    lens_ref, q_ref, resp_ref, bias_ref, scores_ref, low_ref, out_ref, stat_ref, arrived, left,
):
    arriving = start_all(((lens_hbm, lens_ref), (resp_hbm, resp_ref), (q_hbm, q_ref)), arrived)
    wait_all(arriving[:1])
    bias_ref[...] = self_bias(lens_ref, ROWS)
    wait_all(arriving[1:])
    chunks = [halves(resp_ref.at[0])]
    forward(q_ref, chunks, bias_ref, low_ref, out_ref, stat_ref, scores_ref)
    wait_all(start_all(((low_ref, low_hbm), (out_ref, out_hbm), (stat_ref, stat_hbm)), left))


def next_forward_kernel(
    q_ref, one_k, one_v, three_k, three_v, own_ref, low_ref, out_ref, stat_ref, scores_ref
):
    chunks = [(one_k, one_v), (three_k, three_v), halves(own_ref)]
    forward(q_ref, chunks, None, low_ref, out_ref, stat_ref, scores_ref)


def opposite_kernel(
    q_ref, do_ref, k_ref, v_ref, self_out_ref, self_stat_ref, next_out_ref, next_stat_ref,
    attn_ref, dq_ref, stat_ref, dk_ref, dv_ref, acc, scores_ref, low_ref, d_probs_ref,
):
    heads = range(0, HEADS, REPEAT)
    keys_t = [k_ref[:, of_group(h)].T for h in heads]
    vals_t = [v_ref[:, of_group(h)].T for h in heads]
    state = [{} for _ in range(HEADS)]

    def score_pass(h):
        q_t = q_ref[0, :, of_head(h)].T
        s = dot_nn(k_ref[:, of_group(h)], q_t)
        scores_ref[h % 2] = s
        top = by_eights(jnp.max, s) * (SCALE * LOG2E)
        top = jnp.maximum(jnp.maximum(self_stat_ref[h, 0:8], next_stat_ref[h, 0:8]), top)
        state[h].update(q_t=q_t, top=jnp.max(top, axis=0, keepdims=True))

    def weight_pass(h):
        top = state[h]["top"]
        weights = jnp.exp2(scores_ref[h % 2] * (SCALE * LOG2E) - top)
        low = weights.astype(bf16)
        low_ref[h % 4] = low
        own = jnp.exp2(self_stat_ref[h, 0:1] - top)
        next_ = jnp.exp2(next_stat_ref[h, 0:1] - top)
        sums = by_eights(jnp.sum, weights)
        sums = sums + self_stat_ref[h, 8:16] * own + next_stat_ref[h, 8:16] * next_
        inverse = 1.0 / jnp.sum(sums, axis=0, keepdims=True)
        out_t = self_out_ref[h].astype(f32) * own + next_out_ref[h].astype(f32) * next_
        out_t = (out_t + dot_nn(vals_t[h // REPEAT], low)) * inverse
        do_t = do_ref[0, :, of_head(h)].T
        d_probs_ref[h % 4] = dot_nn(v_ref[:, of_group(h)], do_t)
        stat_ref[h, 8:16] = eight(inverse * own)
        stat_ref[h, 16:24] = eight(inverse * next_)
        state[h].update(inverse=inverse, do_t=do_t, out_t=out_t)

    def delta_pass(h):
        do_t, out_t = state[h]["do_t"], state[h]["out_t"]
        delta = jnp.sum(
            do_t.astype(f32) * out_t.astype(bf16).astype(f32), axis=0, keepdims=True
        )
        stat_ref[h, 0:8] = eight(delta)
        attn_ref[0, :, of_head(h)] = out_t.T.astype(bf16)
        state[h]["delta"] = delta
        add(h, 1, dot_nt(scaled(do_t, state[h]["inverse"]), low_ref[h % 4]))

    def add(h, j, new):
        acc[j] = new if h % REPEAT == 0 else acc[j] + new

    def gradient_pass(h):
        inverse = state[h]["inverse"]
        d_probs = d_probs_ref[h % 4] - state[h]["delta"]
        d_scores = (low_ref[h % 4].astype(f32) * d_probs).astype(bf16)
        dq_ref[h] = dot_nn(keys_t[h // REPEAT], d_scores) * (inverse * SCALE)
        add(h, 0, dot_nt(scaled(state[h]["q_t"], inverse * SCALE), d_scores))
        if h % REPEAT == REPEAT - 1:
            dk_ref[:, of_group(h)] = acc[0].T.astype(bf16)
            dv_ref[:, of_group(h)] = acc[1].T.astype(bf16)

    passes = (gradient_pass, delta_pass, weight_pass, score_pass)
    for step in range(1 - len(passes), HEADS):
        for lag, one_pass in enumerate(passes):
            if 0 <= step + lag < HEADS:
                one_pass(step + lag)


def next_backward_kernel(
    q_ref, do_ref, one_k, one_v, three_k, three_v, low_ref, stat_ref, dq_part_ref,
    dq_ref, d_one_k, d_one_v, d_three_k, d_three_v, acc, d_probs_ref,
):
    def put_dq(h, dq_t):
        dq_ref[h] = dq_part_ref[h] + dq_t

    def put_sums(j, cols, sums):
        for t, ref in zip(sums, ((d_one_k, d_three_k), (d_one_v, d_three_v))[j]):
            ref[:, cols] = t.astype(ref.dtype)

    chunks = [(one_k, one_v), (three_k, three_v)]
    lows = [lambda h, at=at: low_ref[h, at] for at in places_of(chunks)]
    backward(q_ref, do_ref, chunks, lows, [16, 16], stat_ref, acc, d_probs_ref, put_dq, put_sums)


def near_backward_kernel(
    q_ref, do_ref, own_ref, resp_ref, low_ref, self_low_ref, stat_ref, dq_part_ref,
    dq_ref, d_own_ref, d_resp_ref, acc, d_probs_ref,
):
    def put_dq(h, dq_t):
        dq_ref[0, :, of_head(h)] = (dq_part_ref[h] + dq_t).T.astype(bf16)

    def put_sums(j, cols, sums):
        cols = slice(j * WIDTH + cols.start, j * WIDTH + cols.stop)
        d_own_ref[:, cols] = sums[0]
        d_resp_ref[0, :, cols] = sums[1].astype(bf16)

    chunks = [halves(own_ref), halves(resp_ref.at[0])]
    lows = [lambda h: low_ref[h], lambda h: self_low_ref[h]]
    backward(q_ref, do_ref, chunks, lows, [16, 8], stat_ref, acc, d_probs_ref, put_dq, put_sums)


def whole(shape):
    return pl.BlockSpec(shape, lambda i: (0,) * len(shape))


def call(kernel, name, outs, scratch, args, flops=ROWS, in_hbm=False, specs={}):
    hbm = pl.BlockSpec(memory_space=pltpu.HBM)
    if in_hbm:
        args = [pltpu.with_memory_space_constraint(t, pltpu.HBM) for t in args]
    return pl.pallas_call(
        kernel,
        grid=(1,),
        in_specs=[hbm if in_hbm else specs.get(i, whole(t.shape)) for i, t in enumerate(args)],
        out_specs=[hbm if in_hbm else whole(shape) for shape, _ in outs],
        out_shape=[
            pltpu.HBM(shape, dtype) if in_hbm else jax.ShapeDtypeStruct(shape, dtype)
            for shape, dtype in outs
        ],
        scratch_shapes=[pltpu.VMEM(*t) if isinstance(t, tuple) else t for t in scratch],
        compiler_params=pltpu.CompilerParams(vmem_limit_bytes=30 << 20),
        cost_estimate=pl.CostEstimate(flops=flops, bytes_accessed=ROWS, transcendentals=0),
        name=name,
    )(*args)


def added(*terms):
    return sum(t.astype(f32) for t in terms).astype(bf16)


def exchange(t, axes):
    return lax.all_to_all(t, axes, split_axis=0, concat_axis=0, tiled=True)


def to_neighbour(t, by):
    return lax.ppermute(t, "x", [(i, i ^ by) for i in range(lax.axis_size("x"))])


def on_device(q_resp, resp_kv, prompt_kv, d_out, resp_lengths):
    groups, own_rows, width = prompt_kv.shape
    ring = ("zl", "c", "zh", "y")
    copies = lax.axis_size(("zh", "y"))
    sent = jnp.broadcast_to(prompt_kv[:, None], (groups, copies, own_rows, width))
    own = exchange(sent.reshape(-1, own_rows, width), ring).reshape(-1, width)

    flat, resp_kind, prompt = (q_resp.shape, bf16), (resp_kv.shape, bf16), own.shape
    tall, stat_kind = (HEADS, HEAD, ROWS), ((HEADS, 16, ROWS), f32)
    parts = lambda n: [((HEADS, n * ROWS, ROWS), bf16), (tall, bf16), stat_kind]
    scores = lambda n: ((2, n * ROWS, ROWS), f32)
    sums = ((2, HEAD, 2 * ROWS), f32)
    self_low, self_out, self_stat = call(
        self_forward_kernel,
        "self_forward",
        parts(1),
        [
            pltpu.SMEM(resp_lengths.shape, jnp.int32),
            flat,
            resp_kind,
            ((ROWS, ROWS), f32),
            scores(1),
            *parts(1),
            pltpu.SemaphoreType.DMA((3,)),
            pltpu.SemaphoreType.DMA((3,)),
        ],
        [resp_lengths, q_resp, resp_kv],
        flops=1 << 33,
        in_hbm=True,
    )

    own, self_stat = lax.optimization_barrier((own, self_stat))
    own_k, own_v = own[:, :WIDTH], own[:, WIDTH:]
    one_k, three_v = to_neighbour(own_k, 1), to_neighbour(own_v, 3)
    one_v, three_k = to_neighbour(own_v, 1), to_neighbour(own_k, 3)
    far_k, far_v = to_neighbour(one_k, 3), to_neighbour(three_v, 1)
    next_ = [one_k, one_v, three_k, three_v]
    next_low, next_out, next_stat = call(
        next_forward_kernel, "next_forward", parts(3), [scores(3)], [q_resp, *next_, own]
    )
    half = lambda dtype: ((ROWS, WIDTH), dtype)
    attn, dq, stat, dk, dv = call(
        opposite_kernel,
        "opposite",
        [flat, (tall, f32), ((HEADS, 24, ROWS), f32), half(bf16), half(bf16)],
        [
            ((2, HEAD, ROWS), f32),
            ((2, ROWS, ROWS), f32),
            ((4, ROWS, ROWS), bf16),
            ((4, ROWS, ROWS), f32),
        ],
        [q_resp, d_out, far_k, far_v, self_out, self_stat, next_out, next_stat],
    )
    dk, dv = to_neighbour(dk, 3), to_neighbour(dv, 1)
    dq, d_one_k, d_one_v, d_three_k, d_three_v = call(
        next_backward_kernel,
        "next_backward",
        [(tall, f32), half(f32), half(bf16), half(bf16), half(f32)],
        [sums, scores(2)],
        [q_resp, d_out, *next_, next_low, stat, dq],
        specs={6: pl.BlockSpec((HEADS, 2 * ROWS, ROWS), lambda i: (0, 0, 0))},
    )
    d_one_v, d_three_k = to_neighbour(d_one_v, 1), to_neighbour(d_three_k, 3)
    dk, dv, d_one_k, d_three_v = lax.optimization_barrier((dk, dv, d_one_k, d_three_v))
    d_one_k, d_three_v = added(d_one_k, dk), added(d_three_v, dv)
    d_one_k, d_three_v = lax.optimization_barrier((d_one_k, d_three_v))
    d_one_k, d_three_v = to_neighbour(d_one_k, 1), to_neighbour(d_three_v, 3)
    dq, d_own, d_resp = call(
        near_backward_kernel,
        "near_backward",
        [flat, (prompt, f32), resp_kind],
        [sums, scores(2)],
        [q_resp, d_out, own, resp_kv, next_low, self_low, stat, dq],
        specs={4: pl.BlockSpec((HEADS, ROWS, ROWS), lambda i: (0, 2, 0))},
    )
    came = (d_one_k, d_three_k, d_one_v, d_three_v)
    d_own, *came = lax.optimization_barrier((d_own, *came))
    keys = added(d_own[:, :WIDTH], came[0], came[1])
    vals = added(d_own[:, WIDTH:], came[2], came[3])
    total = jnp.concatenate([keys, vals], 1)
    total = exchange(total.reshape(-1, own_rows, width), ring)
    total = total.reshape(groups, copies, own_rows, width)
    d_prompt = jnp.sum(total.astype(f32), axis=1).astype(bf16)
    return attn, dq, d_resp, d_prompt


def solution(mesh):
    fine = Mesh(mesh.devices.reshape(4, 2, 2, 4, 4), ("zl", "c", "zh", "y", "x"))
    grp, seq = ("zl", "c"), ("zh", "y", "x")
    rows = P(grp, seq, None)
    prompt = P(None, grp + seq, None)
    return jax.shard_map(
        on_device,
        mesh=fine,
        in_specs=(rows, rows, prompt, rows, rows),
        out_specs=(rows, rows, rows, prompt),
        check_vma=False,
    )
```

time: 1020 us -> 80.5 us (0.08)
  waiting for transfers between devices: 916 us -> 14.2 us
  matrix products: 28.2 us -> 0 us
  local copies, waits for them, and re-layouts: 25.1 us -> 1.72 us
  blocking collectives: 0 us -> 21.9 us
  Pallas kernels: 0 us -> 17.5 us
  between operations: 14.2 us -> 0.75 us
    all_gather x1 -> x0, waiting for transfers between devices: 718 us -> none  [on_device(): everything = lax.all_gather(prompt_kv, ('grp', 'seq'), axis=1, tiled=True)]
    reduce_scatter x1 -> x0, waiting for transfers between devices: 196 us -> none  [on_device(): lax.psum_scatter(jnp.concatenate([part_keys.reshape(count, width), part_v...]
    all_to_all x0 -> x1, blocking collectives: none -> 21.9 us  [exchange(): return lax.all_to_all(t, axes, split_axis=0, concat_axis=0, tiled=True)]
    dot_general x7 -> x0, matrix products: 21 us -> none  [the longest x1 5.84 us: on_device(): jnp.einsum('rgnd,jgd->gnrj', grads_out, vals_all, preferred_element_type=...]
    pallas_call x0 -> x5, Pallas kernels: none -> 17.5 us  [call(): pl.pallas_call(kernel, grid=(1,), in_specs=[hbm if in_hbm else specs.get(...]
    all_to_all x1, starting transfers between devices: 29.3 us -> 13.2 us  [exchange(): return lax.all_to_all(t, axes, split_axis=0, concat_axis=0, tiled=True)]
    unnamed x19 -> x12, local copies, waits for them, and re-layouts: 10.7 us -> 0.03 us
    ppermute x0 -> x12, starting transfers between devices: none -> 10.2 us  [to_neighbour(): lax.ppermute(t, 'x', [(i, i ^ by) for i in range(lax.axis_size('x'))])]
  transfers between devices with their start and end apart: 3 -> 13, of which waited for: 3 -> 8; matrix products, arithmetic and copies ran while one was open for 2% -> 0% of each run, Pallas kernels for 0% -> 17%
where the time goes in v4:
time: 80.5 us; the launch traced here: 80.3 us
  starting transfers between devices  23.4 us (29%)
  blocking collectives  21.9 us (27%)
  Pallas kernels  17.5 us (22%)
  waiting for transfers between devices  14.2 us (18%)
  local copies, waits for them, and re-layouts  1.72 us (2%)
  other arithmetic  0.88 us (1%)
    all_to_all x1, blocking collectives, exchange(): return lax.all_to_all(t, axes, split_axis=0, concat_axis=0, tiled=True)  21.9 us
    pallas_call x5, Pallas kernels, call(): pl.pallas_call(kernel, grid=(1,), in_specs=[hbm if in_hbm else specs.get(...  17.5 us
    all_to_all x1, starting transfers between devices, exchange(): return lax.all_to_all(t, axes, split_axis=0, concat_axis=0, tiled=True)  13.2 us
    ppermute x12, starting transfers between devices, to_neighbour(): lax.ppermute(t, 'x', [(i, i ^ by) for i in range(lax.axis_size('x'))])  10.2 us
    all_to_all x1, waiting for transfers between devices, exchange(): return lax.all_to_all(t, axes, split_axis=0, concat_axis=0, tiled=True)  8.17 us
    ppermute x12, waiting for transfers between devices, to_neighbour(): lax.ppermute(t, 'x', [(i, i ^ by) for i in range(lax.axis_size('x'))])  6 us
  transfers between devices with their start and end apart: 13, of which 8 were waited for; matrix products, arithmetic and copies ran while one was open for 0% of the time, Pallas kernels for 17%

profile of v4, /device:TPU:1, one launch (start us, length us, event | category | flops | bytes accessed | tf_op | source)
XLA Modules:
  0.0 80.3 jit_solution(2344653733859684360)
XLA Ops:
  0.6 1.5 %broadcast_in_dim.2 = bf16[8,8,4,512]{3,2,1,0:T(4,128)(2,1)} broadcast(bf16[8,4,512]{2,1,0:T(4,128)(2,1)} %param.7), dimensions={0,2,3} | broadcast | bytes 294912 | tf_op jit(solution)/shard_map/broadcast_in_dim | solution.py:330
  2.2 13.2 %all-to-all-start = ((bf16[64,4,512]{2,1,0:T(4,128)(2,1)}), bf16[64,4,512]{2,1,0:T(4,128)(2,1)S(1)}, u32[]{:S(2)}, u32[]{:S(2)}) async-start(bf16[64,4,512]{2,1,0:T(4,128)(2,1)} %bitcast), calls=%async_computation | async-start | bytes 524288 | tf_op jit(solution)/shard_map/all_to_all | solution.py:319
  15.3 4.2 %self_forward.1 = (bf16[10,256,256]{2,1,0:T(8,128)(2,1)}, bf16[10,128,256]{2,1,0:T(8,128)(2,1)}, f32[10,16,256]{2,1,0:T(8,128)}) custom-call(s32[1,1,4]{2,1,0:T(1,128)} %lens_hbm.1, bf16[1,256,1280]{2,1,0:T(8,128)(2,1)} %q_ref.7, bf16[1,256,512]{2,1,0:T(8,128)(2,1)} %resp_ref.1), custom_call_target="tpu_custom_call" | custom-call | flops 8589934592 | bytes 256 | tf_op jit(solution)/shard_map/self_forward/pallas_call | solution.py:298
  19.5 0.0 copy-start
  19.5 0.0 copy-start.1
  19.6 0.0 copy-start.3
  19.6 0.0 copy-start.5
  19.6 8.2 %all-to-all-done = bf16[64,4,512]{2,1,0:T(4,128)(2,1)S(1)} async-done(((bf16[64,4,512]{2,1,0:T(4,128)(2,1)}), bf16[64,4,512]{2,1,0:T(4,128)(2,1)S(1)}, u32[]{:S(2)}, u32[]{:S(2)}) %all-to-all-start) | async-done | bytes 262176 | tf_op jit(solution)/shard_map/all_to_all | solution.py:319
  27.7 0.1 reshape.22.own_ref
  27.8 2.6 %collective-permute-start.2 = (bf16[256,256]{1,0:T(8,128)(2,1)S(1)}, bf16[256,256]{1,0:T(8,128)(2,1)S(1)}, u32[]{:S(2)}, u32[]{:S(2)}) collective-permute-start(bf16[256,256]{1,0:T(8,128)(2,1)S(1)} %get-tuple-element.70), channel_id=1, source_target_pairs={{0,3},{1,2},{2,1},{3,0},{4,7},{5,6},{6,5},{7,4},{8,11},{9,10},{10,... | collective-permute-start | bytes 393224 | tf_op jit(solution)/shard_map/ppermute | solution.py:323
  30.4 0.0 collective-permute-start
  30.4 1.5 %collective-permute-start.4 = (bf16[256,256]{1,0:T(8,128)(2,1)S(1)}, bf16[256,256]{1,0:T(8,128)(2,1)S(1)}, u32[]{:S(2)}, u32[]{:S(2)}) collective-permute-start(bf16[256,256]{1,0:T(8,128)(2,1)S(1)} %get-tuple-element.70), channel_id=1, source_target_pairs={{0,1},{1,0},{2,3},{3,2},{4,5},{5,4},{6,7},{7,6},{8,9},{9,8},{10,11... | collective-permute-start | bytes 393224 | tf_op jit(solution)/shard_map/ppermute | solution.py:323
  31.9 0.2 collective-permute-start.5
  32.1 0.9 %collective-permute-done.2.three_v = bf16[256,256]{1,0:T(8,128)(2,1)S(1)} collective-permute-done((bf16[256,256]{1,0:T(8,128)(2,1)S(1)}, bf16[256,256]{1,0:T(8,128)(2,1)S(1)}, u32[]{:S(2)}, u32[]{:S(2)}) %collective-permute-start.2) | collective-permute-done | bytes 131104 | tf_op jit(solution)/shard_map/ppermute | solution.py:323
  33.0 0.0 collective-permute-start.3
  33.0 1.6 %collective-permute-done.one_k = bf16[256,256]{1,0:T(8,128)(2,1)S(1)} collective-permute-done((bf16[256,256]{1,0:T(8,128)(2,1)S(1)}, bf16[256,256]{1,0:T(8,128)(2,1)S(1)}, u32[]{:S(2)}, u32[]{:S(2)}) %collective-permute-start) | collective-permute-done | bytes 131104 | tf_op jit(solution)/shard_map/ppermute | solution.py:323
  34.5 0.9 %collective-permute-start.1 = (bf16[256,256]{1,0:T(8,128)(2,1)S(1)}, bf16[256,256]{1,0:T(8,128)(2,1)S(1)}, u32[]{:S(2)}, u32[]{:S(2)}) collective-permute-start(bf16[256,256]{1,0:T(8,128)(2,1)S(1)} %collective-permute-done.one_k), channel_id=1, source_target_pairs={{0,3},{1,2},{2,1},{3,0},{4,7},{5,6},{6,5},{7,4},{8,11},{9,10},{10,... | collective-permute-start | bytes 393224 | tf_op jit(solution)/shard_map/ppermute | solution.py:323
  35.4 0.7 collective-permute-done.4.one_v
  36.2 0.7 collective-permute-done.5.three_k
  36.9 0.0 copy-done
  36.9 3.3 %next_forward.1 = (bf16[10,768,256]{2,1,0:T(8,128)(2,1)S(1)}, bf16[10,128,256]{2,1,0:T(8,128)(2,1)S(1)}, f32[10,16,256]{2,1,0:T(8,128)S(1)}) custom-call(bf16[1,256,1280]{2,1,0:T(8,128)(2,1)S(1)} %copy-done, bf16[256,256]{1,0:T(8,128)(2,1)S(1)} %collective-permute-done.one_k, bf16[256,256]{1,0:T(8,128)(2,1)S(1)} %collective-permute-done.4.one_v, ...), custom_call_target="tpu_custom_call" | custom-call | flops 256 | bytes 256 | tf_op jit(solution)/shard_map/next_forward/pallas_call | solution.py:298
  40.2 0.0 collective-permute-done.3.v_ref
  40.2 0.7 collective-permute-done.1.k_ref
  40.9 0.0 copy-done.1
  40.9 0.0 copy-done.3
  40.9 0.0 copy-done.5
  40.9 4.0 %opposite.1 = (bf16[1,256,1280]{2,1,0:T(8,128)(2,1)}, f32[10,128,256]{2,1,0:T(8,128)S(1)}, f32[10,24,256]{2,1,0:T(8,128)S(1)}, bf16[256,256]{1,0:T(8,128)(2,1)S(1)}, bf16[256,256]{1,0:T(8,128)(2,1)S(1)}) custom-call(bf16[1,256,1280]{2,1,0:T(8,128)(2,1)S(1)} %copy-done, bf16[1,256,1280]{2,1,0:T(8,128)(2,1)S(1)} %copy-done.1, ...), custom_call_target="tpu_custom_call" | custom-call | flops 256 | bytes 256 | tf_op jit(solution)/shard_map/opposite/pallas_call | solution.py:298
  44.9 0.7 collective-permute-start.6
  45.7 0.0 collective-permute-start.7
  45.7 0.0 copy-start.2
  45.7 0.0 copy-start.4
  45.7 2.6 %next_backward.1 = (f32[10,128,256]{2,1,0:T(8,128)S(1)}, f32[256,256]{1,0:T(8,128)S(1)}, bf16[256,256]{1,0:T(8,128)(2,1)S(1)}, bf16[256,256]{1,0:T(8,128)(2,1)S(1)}, f32[256,256]{1,0:T(8,128)S(1)}) custom-call(bf16[1,256,1280]{2,1,0:T(8,128)(2,1)S(1)} %copy-done, bf16[1,256,1280]{2,1,0:T(8,128)(2,1)S(1)} %copy-done.1, ...), custom_call_target="tpu_custom_call" | custom-call | flops 256 | bytes 256 | tf_op jit(solution)/shard_map/next_backward/pallas_call | solution.py:298
  48.3 2.0 %collective-permute-start.9 = (bf16[256,256]{1,0:T(8,128)(2,1)S(1)}, bf16[256,256]{1,0:T(8,128)(2,1)S(1)}, u32[]{:S(2)}, u32[]{:S(2)}) collective-permute-start(bf16[256,256]{1,0:T(8,128)(2,1)S(1)} %get-tuple-element.60), channel_id=1, source_target_pairs={{0,3},{1,2},{2,1},{3,0},{4,7},{5,6},{6,5},{7,4},{8,11},{9,10},{10,... | collective-permute-start | bytes 393224 | tf_op jit(solution)/shard_map/ppermute | solution.py:323
  50.3 0.9 %collective-permute-start.10 = (bf16[256,256]{1,0:T(8,128)(2,1)S(1)}, bf16[256,256]{1,0:T(8,128)(2,1)S(1)}, u32[]{:S(2)}, u32[]{:S(2)}) collective-permute-start(bf16[256,256]{1,0:T(8,128)(2,1)S(1)} %get-tuple-element.61), channel_id=1, source_target_pairs={{0,1},{1,0},{2,3},{3,2},{4,5},{5,4},{6,7},{7,6},{8,9},{9,8},{10,11... | collective-permute-start | bytes 393224 | tf_op jit(solution)/shard_map/ppermute | solution.py:323
  51.1 0.0 collective-permute-done.6
  51.2 0.0 collective-permute-done.7
  51.2 0.1 add_convert_fusion.2
  51.2 0.7 collective-permute-start.8
  51.9 0.7 collective-permute-start.11
  52.6 0.0 copy-done.2
  52.6 0.0 copy-done.4
  52.7 3.5 %near_backward.1 = (bf16[1,256,1280]{2,1,0:T(8,128)(2,1)}, f32[256,512]{1,0:T(8,128)S(1)}, bf16[1,256,512]{2,1,0:T(8,128)(2,1)}) custom-call(bf16[1,256,1280]{2,1,0:T(8,128)(2,1)S(1)} %copy-done, bf16[1,256,1280]{2,1,0:T(8,128)(2,1)S(1)} %copy-done.1, bf16[256,512]{1,0:T(8,128)(2,1)S(1)} %reshape.22.own_ref, bf16[1,256,512]{2,1,0:T(8,128)(2,1)S(1)} %copy-done.4, ...), custom_call_target="tpu_custom_call" | custom-call | flops 256 | bytes 256 | tf_op jit(solution)/shard_map/near_backward/pallas_call | solution.py:298
  56.1 0.0 collective-permute-done.9
  56.1 0.0 collective-permute-done.10
  56.1 0.9 %collective-permute-done.8 = bf16[256,256]{1,0:T(8,128)(2,1)S(1)} collective-permute-done((bf16[256,256]{1,0:T(8,128)(2,1)S(1)}, bf16[256,256]{1,0:T(8,128)(2,1)S(1)}, u32[]{:S(2)}, u32[]{:S(2)}) %collective-permute-start.8) | collective-permute-done | bytes 131104 | tf_op jit(solution)/shard_map/ppermute | solution.py:323
  57.1 0.4 collective-permute-done.11
  57.5 0.1 add_convert_fusion.1
  57.6 0.1 reshape.23
  57.7 21.9 %all_to_all.10 = bf16[64,4,512]{2,1,0:T(4,128)(2,1)S(1)} all-to-all(bf16[64,4,512]{2,1,0:T(4,128)(2,1)S(1)} %reshape.23), channel_id=1, replica_groups=mesh['zl'=4,'c'=2,'zh'=2,'y'=4,'x'=4] {'zl','c','zh','y'}, dimensions={0} | all-to-all | bytes 524288 | tf_op jit(solution)/shard_map/all_to_all | solution.py:319
  79.5 0.7 bitcast_reduce_fusion
  (2 shorter events, 0.0 us)
Async XLA Ops:
  2.2 25.6 %all-to-all-start = ((bf16[64,4,512]{2,1,0:T(4,128)(2,1)}), bf16[64,4,512]{2,1,0:T(4,128)(2,1)S(1)}, u32[]{:S(2)}, u32[]{:S(2)}) async-start(bf16[64,4,512]{2,1,0:T(4,128)(2,1)} %bitcast), calls=%async_computation | async-start | bytes 524288 | tf_op jit(solution)/shard_map/all_to_all | solution.py:319
  19.5 17.4 %copy-start = (bf16[1,256,1280]{2,1,0:T(8,128)(2,1)S(1)}, bf16[1,256,1280]{2,1,0:T(8,128)(2,1)}, u32[]{:S(2)}) copy-start(bf16[1,256,1280]{2,1,0:T(8,128)(2,1)} %q_ref.7) | copy-start | bytes 1966084
  19.5 21.4 %copy-start.1 = (bf16[1,256,1280]{2,1,0:T(8,128)(2,1)S(1)}, bf16[1,256,1280]{2,1,0:T(8,128)(2,1)}, u32[]{:S(2)}) copy-start(bf16[1,256,1280]{2,1,0:T(8,128)(2,1)} %do_ref.5) | copy-start | bytes 1966084
  19.6 21.4 %copy-start.3 = (bf16[10,128,256]{2,1,0:T(8,128)(2,1)S(1)}, bf16[10,128,256]{2,1,0:T(8,128)(2,1)}, u32[]{:S(2)}) copy-start(bf16[10,128,256]{2,1,0:T(8,128)(2,1)} %get-tuple-element.38.self_out_ref) | copy-start | bytes 1966084
  19.6 21.4 %copy-start.5 = (f32[10,16,256]{2,1,0:T(8,128)S(1)}, f32[10,16,256]{2,1,0:T(8,128)}, u32[]{:S(2)}) copy-start(f32[10,16,256]{2,1,0:T(8,128)} %get-tuple-element.39.self_stat_ref) | copy-start | bytes 491524
  27.8 5.1 %collective-permute-start.2 = (bf16[256,256]{1,0:T(8,128)(2,1)S(1)}, bf16[256,256]{1,0:T(8,128)(2,1)S(1)}, u32[]{:S(2)}, u32[]{:S(2)}) collective-permute-start(bf16[256,256]{1,0:T(8,128)(2,1)S(1)} %get-tuple-element.70), channel_id=1, source_target_pairs={{0,3},{1,2},{2,1},{3,0},{4,7},{5,6},{6,5},{7,4},{8,11},{9,10},{10,... | collective-permute-start | bytes 393224 | tf_op jit(solution)/shard_map/ppermute | solution.py:323
  30.4 4.1 %collective-permute-start = (bf16[256,256]{1,0:T(8,128)(2,1)S(1)}, bf16[256,256]{1,0:T(8,128)(2,1)S(1)}, u32[]{:S(2)}, u32[]{:S(2)}) collective-permute-start(bf16[256,256]{1,0:T(8,128)(2,1)S(1)} %get-tuple-element.71), channel_id=1, source_target_pairs={{0,1},{1,0},{2,3},{3,2},{4,5},{5,4},{6,7},{7,6},{8,9},{9,8},{10,11... | collective-permute-start | bytes 393224 | tf_op jit(solution)/shard_map/ppermute | solution.py:323
  30.4 5.8 %collective-permute-start.4 = (bf16[256,256]{1,0:T(8,128)(2,1)S(1)}, bf16[256,256]{1,0:T(8,128)(2,1)S(1)}, u32[]{:S(2)}, u32[]{:S(2)}) collective-permute-start(bf16[256,256]{1,0:T(8,128)(2,1)S(1)} %get-tuple-element.70), channel_id=1, source_target_pairs={{0,1},{1,0},{2,3},{3,2},{4,5},{5,4},{6,7},{7,6},{8,9},{9,8},{10,11... | collective-permute-start | bytes 393224 | tf_op jit(solution)/shard_map/ppermute | solution.py:323
  31.9 5.0 %collective-permute-start.5 = (bf16[256,256]{1,0:T(8,128)(2,1)S(1)}, bf16[256,256]{1,0:T(8,128)(2,1)S(1)}, u32[]{:S(2)}, u32[]{:S(2)}) collective-permute-start(bf16[256,256]{1,0:T(8,128)(2,1)S(1)} %get-tuple-element.71), channel_id=1, source_target_pairs={{0,3},{1,2},{2,1},{3,0},{4,7},{5,6},{6,5},{7,4},{8,11},{9,10},{10,... | collective-permute-start | bytes 393224 | tf_op jit(solution)/shard_map/ppermute | solution.py:323
  33.0 7.2 %collective-permute-start.3 = (bf16[256,256]{1,0:T(8,128)(2,1)S(1)}, bf16[256,256]{1,0:T(8,128)(2,1)S(1)}, u32[]{:S(2)}, u32[]{:S(2)}) collective-permute-start(bf16[256,256]{1,0:T(8,128)(2,1)S(1)} %collective-permute-done.2.three_v), channel_id=1, source_target_pairs={{0,1},{1,0},{2,3},{3,2},{4,5},{5,4},{6,7},{7,6},{8,9},{9,8},{10,11... | collective-permute-start | bytes 393224 | tf_op jit(solution)/shard_map/ppermute | solution.py:323
  34.5 6.4 %collective-permute-start.1 = (bf16[256,256]{1,0:T(8,128)(2,1)S(1)}, bf16[256,256]{1,0:T(8,128)(2,1)S(1)}, u32[]{:S(2)}, u32[]{:S(2)}) collective-permute-start(bf16[256,256]{1,0:T(8,128)(2,1)S(1)} %collective-permute-done.one_k), channel_id=1, source_target_pairs={{0,3},{1,2},{2,1},{3,0},{4,7},{5,6},{6,5},{7,4},{8,11},{9,10},{10,... | collective-permute-start | bytes 393224 | tf_op jit(solution)/shard_map/ppermute | solution.py:323
  44.9 6.2 %collective-permute-start.6 = (bf16[256,256]{1,0:T(8,128)(2,1)S(1)}, bf16[256,256]{1,0:T(8,128)(2,1)S(1)}, u32[]{:S(2)}, u32[]{:S(2)}) collective-permute-start(bf16[256,256]{1,0:T(8,128)(2,1)S(1)} %get-tuple-element.51), channel_id=1, source_target_pairs={{0,3},{1,2},{2,1},{3,0},{4,7},{5,6},{6,5},{7,4},{8,11},{9,10},{10,... | collective-permute-start | bytes 393224 | tf_op jit(solution)/shard_map/ppermute | solution.py:323
  45.7 5.5 %collective-permute-start.7 = (bf16[256,256]{1,0:T(8,128)(2,1)S(1)}, bf16[256,256]{1,0:T(8,128)(2,1)S(1)}, u32[]{:S(2)}, u32[]{:S(2)}) collective-permute-start(bf16[256,256]{1,0:T(8,128)(2,1)S(1)} %get-tuple-element.52), channel_id=1, source_target_pairs={{0,1},{1,0},{2,3},{3,2},{4,5},{5,4},{6,7},{7,6},{8,9},{9,8},{10,11... | collective-permute-start | bytes 393224 | tf_op jit(solution)/shard_map/ppermute | solution.py:323
  45.7 7.0 %copy-start.2 = (bf16[10,256,256]{2,1,0:T(8,128)(2,1)S(1)}, bf16[10,256,256]{2,1,0:T(8,128)(2,1)}, u32[]{:S(2)}) copy-start(bf16[10,256,256]{2,1,0:T(8,128)(2,1)} %get-tuple-element.44.self_low_ref) | copy-start | bytes 3932164
  45.7 7.0 %copy-start.4 = (bf16[1,256,512]{2,1,0:T(8,128)(2,1)S(1)}, bf16[1,256,512]{2,1,0:T(8,128)(2,1)}, u32[]{:S(2)}) copy-start(bf16[1,256,512]{2,1,0:T(8,128)(2,1)} %resp_ref.1) | copy-start | bytes 786436
  48.3 7.9 %collective-permute-start.9 = (bf16[256,256]{1,0:T(8,128)(2,1)S(1)}, bf16[256,256]{1,0:T(8,128)(2,1)S(1)}, u32[]{:S(2)}, u32[]{:S(2)}) collective-permute-start(bf16[256,256]{1,0:T(8,128)(2,1)S(1)} %get-tuple-element.60), channel_id=1, source_target_pairs={{0,3},{1,2},{2,1},{3,0},{4,7},{5,6},{6,5},{7,4},{8,11},{9,10},{10,... | collective-permute-start | bytes 393224 | tf_op jit(solution)/shard_map/ppermute | solution.py:323
  50.3 5.8 %collective-permute-start.10 = (bf16[256,256]{1,0:T(8,128)(2,1)S(1)}, bf16[256,256]{1,0:T(8,128)(2,1)S(1)}, u32[]{:S(2)}, u32[]{:S(2)}) collective-permute-start(bf16[256,256]{1,0:T(8,128)(2,1)S(1)} %get-tuple-element.61), channel_id=1, source_target_pairs={{0,1},{1,0},{2,3},{3,2},{4,5},{5,4},{6,7},{7,6},{8,9},{9,8},{10,11... | collective-permute-start | bytes 393224 | tf_op jit(solution)/shard_map/ppermute | solution.py:323
  51.2 5.8 %collective-permute-start.8 = (bf16[256,256]{1,0:T(8,128)(2,1)S(1)}, bf16[256,256]{1,0:T(8,128)(2,1)S(1)}, u32[]{:S(2)}, u32[]{:S(2)}) collective-permute-start(bf16[256,256]{1,0:T(8,128)(2,1)S(1)} %get-tuple-element.59), channel_id=1, source_target_pairs={{0,1},{1,0},{2,3},{3,2},{4,5},{5,4},{6,7},{7,6},{8,9},{9,8},{10,11... | collective-permute-start | bytes 393224 | tf_op jit(solution)/shard_map/ppermute | solution.py:323
  51.9 5.6 %collective-permute-start.11 = (bf16[256,256]{1,0:T(8,128)(2,1)S(1)}, bf16[256,256]{1,0:T(8,128)(2,1)S(1)}, u32[]{:S(2)}, u32[]{:S(2)}) collective-permute-start(bf16[256,256]{1,0:T(8,128)(2,1)S(1)} %get-tuple-element.62), channel_id=1, source_target_pairs={{0,3},{1,2},{2,1},{3,0},{4,7},{5,6},{6,5},{7,4},{8,11},{9,10},{10,... | collective-permute-start | bytes 393224 | tf_op jit(solution)/shard_map/ppermute | solution.py:323

commit v5 on v4

--- a/solution.py
+++ b/solution.py
@@ -191,7 +191,7 @@
 
 def opposite_kernel(
     q_ref, do_ref, k_ref, v_ref, self_out_ref, self_stat_ref, next_out_ref, next_stat_ref,
-    attn_ref, dq_ref, stat_ref, dk_ref, dv_ref, acc, scores_ref, low_ref, d_probs_ref,
+    out_ref, dq_ref, stat_ref, dk_ref, dv_ref, acc, scores_ref, low_ref, d_probs_ref,
 ):
     heads = range(0, HEADS, REPEAT)
     keys_t = [k_ref[:, of_group(h)].T for h in heads]
@@ -230,12 +230,13 @@
             do_t.astype(f32) * out_t.astype(bf16).astype(f32), axis=0, keepdims=True
         )
         stat_ref[h, 0:8] = eight(delta)
-        attn_ref[0, :, of_head(h)] = out_t.T.astype(bf16)
+        out_ref[h] = out_t.astype(bf16)
         state[h]["delta"] = delta
         add(h, 1, dot_nt(scaled(do_t, state[h]["inverse"]), low_ref[h % 4]))
 
     def add(h, j, new):
-        acc[j] = new if h % REPEAT == 0 else acc[j] + new
+        at = (h // REPEAT, j)
+        acc[at] = new if h % REPEAT == 0 else acc[at] + new
 
     def gradient_pass(h):
         inverse = state[h]["inverse"]
@@ -244,14 +245,14 @@
         dq_ref[h] = dot_nn(keys_t[h // REPEAT], d_scores) * (inverse * SCALE)
         add(h, 0, dot_nt(scaled(state[h]["q_t"], inverse * SCALE), d_scores))
         if h % REPEAT == REPEAT - 1:
-            dk_ref[:, of_group(h)] = acc[0].T.astype(bf16)
-            dv_ref[:, of_group(h)] = acc[1].T.astype(bf16)
+            dk_ref[:, of_group(h)] = acc[h // REPEAT, 0].T.astype(bf16)
+            dv_ref[:, of_group(h)] = acc[h // REPEAT, 1].T.astype(bf16)
 
     passes = (gradient_pass, delta_pass, weight_pass, score_pass)
     for step in range(1 - len(passes), HEADS):
-        for lag, one_pass in enumerate(passes):
+        for lag in (1, 3, 0, 2):
             if 0 <= step + lag < HEADS:
-                one_pass(step + lag)
+                passes[lag](step + lag)
 
 
 def next_backward_kernel(
@@ -271,11 +272,12 @@
 
 
 def near_backward_kernel(
-    q_ref, do_ref, own_ref, resp_ref, low_ref, self_low_ref, stat_ref, dq_part_ref,
-    dq_ref, d_own_ref, d_resp_ref, acc, d_probs_ref,
+    q_ref, do_ref, own_ref, resp_ref, low_ref, self_low_ref, stat_ref, dq_part_ref, out_ref,
+    attn_ref, dq_ref, d_own_ref, d_resp_ref, acc, d_probs_ref,
 ):
     def put_dq(h, dq_t):
         dq_ref[0, :, of_head(h)] = (dq_part_ref[h] + dq_t).T.astype(bf16)
+        attn_ref[0, :, of_head(h)] = out_ref[h].T
 
     def put_sums(j, cols, sums):
         cols = slice(j * WIDTH + cols.start, j * WIDTH + cols.stop)
@@ -319,8 +321,15 @@
     return lax.all_to_all(t, axes, split_axis=0, concat_axis=0, tiled=True)
 
 
-def to_neighbour(t, by):
-    return lax.ppermute(t, "x", [(i, i ^ by) for i in range(lax.axis_size("x"))])
+def to_neighbour(t, side):
+    size = lax.axis_size("x")
+    by = ((1, 3), (3, 1))
+    pairs = [
+        (core * size + i, core * size + (i ^ by[core][side]))
+        for core in range(lax.axis_size("c"))
+        for i in range(size)
+    ]
+    return lax.ppermute(t, ("c", "x"), pairs)
 
 
 def on_device(q_resp, resp_kv, prompt_kv, d_out, resp_lengths):
@@ -356,27 +365,27 @@
 
     own, self_stat = lax.optimization_barrier((own, self_stat))
     own_k, own_v = own[:, :WIDTH], own[:, WIDTH:]
-    one_k, three_v = to_neighbour(own_k, 1), to_neighbour(own_v, 3)
-    one_v, three_k = to_neighbour(own_v, 1), to_neighbour(own_k, 3)
-    far_k, far_v = to_neighbour(one_k, 3), to_neighbour(three_v, 1)
+    one_k, three_v = to_neighbour(own_k, 0), to_neighbour(own_v, 1)
+    one_v, three_k = to_neighbour(own_v, 0), to_neighbour(own_k, 1)
+    far_k, far_v = to_neighbour(one_k, 1), to_neighbour(three_v, 0)
     next_ = [one_k, one_v, three_k, three_v]
     next_low, next_out, next_stat = call(
         next_forward_kernel, "next_forward", parts(3), [scores(3)], [q_resp, *next_, own]
     )
     half = lambda dtype: ((ROWS, WIDTH), dtype)
-    attn, dq, stat, dk, dv = call(
+    out, dq, stat, dk, dv = call(
         opposite_kernel,
         "opposite",
-        [flat, (tall, f32), ((HEADS, 24, ROWS), f32), half(bf16), half(bf16)],
+        [(tall, bf16), (tall, f32), ((HEADS, 24, ROWS), f32), half(bf16), half(bf16)],
         [
-            ((2, HEAD, ROWS), f32),
+            ((KV_HEADS, 2, HEAD, ROWS), f32),
             ((2, ROWS, ROWS), f32),
             ((4, ROWS, ROWS), bf16),
             ((4, ROWS, ROWS), f32),
         ],
         [q_resp, d_out, far_k, far_v, self_out, self_stat, next_out, next_stat],
     )
-    dk, dv = to_neighbour(dk, 3), to_neighbour(dv, 1)
+    dk, dv = to_neighbour(dk, 1), to_neighbour(dv, 0)
     dq, d_one_k, d_one_v, d_three_k, d_three_v = call(
         next_backward_kernel,
         "next_backward",
@@ -385,17 +394,17 @@
         [q_resp, d_out, *next_, next_low, stat, dq],
         specs={6: pl.BlockSpec((HEADS, 2 * ROWS, ROWS), lambda i: (0, 0, 0))},
     )
-    d_one_v, d_three_k = to_neighbour(d_one_v, 1), to_neighbour(d_three_k, 3)
+    d_one_v, d_three_k = to_neighbour(d_one_v, 0), to_neighbour(d_three_k, 1)
     dk, dv, d_one_k, d_three_v = lax.optimization_barrier((dk, dv, d_one_k, d_three_v))
     d_one_k, d_three_v = added(d_one_k, dk), added(d_three_v, dv)
     d_one_k, d_three_v = lax.optimization_barrier((d_one_k, d_three_v))
-    d_one_k, d_three_v = to_neighbour(d_one_k, 1), to_neighbour(d_three_v, 3)
-    dq, d_own, d_resp = call(
+    d_one_k, d_three_v = to_neighbour(d_one_k, 0), to_neighbour(d_three_v, 1)
+    attn, dq, d_own, d_resp = call(
         near_backward_kernel,
         "near_backward",
-        [flat, (prompt, f32), resp_kind],
+        [flat, flat, (prompt, f32), resp_kind],
         [sums, scores(2)],
-        [q_resp, d_out, own, resp_kv, next_low, self_low, stat, dq],
+        [q_resp, d_out, own, resp_kv, next_low, self_low, stat, dq, out],
         specs={4: pl.BlockSpec((HEADS, ROWS, ROWS), lambda i: (0, 2, 0))},
     )
     came = (d_one_k, d_three_k, d_one_v, d_three_v)

time: 80.5 us -> 78.7 us (0.978)
  waiting for transfers between devices: 14.2 us -> 16.7 us
  blocking collectives: 21.9 us -> 19.5 us
  Pallas kernels: 17.5 us -> 16.3 us
  starting transfers between devices: 23.4 us -> 22.5 us
    ppermute x12, waiting for transfers between devices: 6 us -> 8.55 us  [to_neighbour(): return lax.ppermute(t, ('c', 'x'), pairs)]
    all_to_all x1, blocking collectives: 21.9 us -> 19.5 us  [exchange(): return lax.all_to_all(t, axes, split_axis=0, concat_axis=0, tiled=True)]
    pallas_call x5, Pallas kernels: 17.5 us -> 16.3 us  [call(): pl.pallas_call(kernel, grid=(1,), in_specs=[hbm if in_hbm else specs.get(...]
    ppermute x12, starting transfers between devices: 10.2 us -> 9.38 us  [to_neighbour(): return lax.ppermute(t, ('c', 'x'), pairs)]
where the time goes in v5:
time: 78.7 us; the launch traced here: 78.4 us
  starting transfers between devices  22.5 us (29%)
  blocking collectives  19.5 us (25%)
  waiting for transfers between devices  16.7 us (21%)
  Pallas kernels  16.3 us (21%)
  local copies, waits for them, and re-layouts  1.72 us (2%)
  other arithmetic  0.88 us (1%)
    all_to_all x1, blocking collectives, exchange(): return lax.all_to_all(t, axes, split_axis=0, concat_axis=0, tiled=True)  19.5 us
    pallas_call x5, Pallas kernels, call(): pl.pallas_call(kernel, grid=(1,), in_specs=[hbm if in_hbm else specs.get(...  16.3 us
    all_to_all x1, starting transfers between devices, exchange(): return lax.all_to_all(t, axes, split_axis=0, concat_axis=0, tiled=True)  13.2 us
    ppermute x12, starting transfers between devices, to_neighbour(): return lax.ppermute(t, ('c', 'x'), pairs)  9.38 us
    ppermute x12, waiting for transfers between devices, to_neighbour(): return lax.ppermute(t, ('c', 'x'), pairs)  8.55 us
    all_to_all x1, waiting for transfers between devices, exchange(): return lax.all_to_all(t, axes, split_axis=0, concat_axis=0, tiled=True)  8.17 us
  transfers between devices with their start and end apart: 13, of which 8 were waited for; matrix products, arithmetic and copies ran while one was open for 0% of the time, Pallas kernels for 17%

profile of v5, /device:TPU:1, one launch (start us, length us, event | category | flops | bytes accessed | tf_op | source)
XLA Modules:
  0.0 78.4 jit_solution(9403189980949475627)
XLA Ops:
  0.6 1.5 %broadcast_in_dim.2 = bf16[8,8,4,512]{3,2,1,0:T(4,128)(2,1)} broadcast(bf16[8,4,512]{2,1,0:T(4,128)(2,1)} %param.7), dimensions={0,2,3} | broadcast | bytes 294912 | tf_op jit(solution)/shard_map/broadcast_in_dim | solution.py:339
  2.2 13.2 %all-to-all-start = ((bf16[64,4,512]{2,1,0:T(4,128)(2,1)}), bf16[64,4,512]{2,1,0:T(4,128)(2,1)S(1)}, u32[]{:S(2)}, u32[]{:S(2)}) async-start(bf16[64,4,512]{2,1,0:T(4,128)(2,1)} %bitcast), calls=%async_computation | async-start | bytes 524288 | tf_op jit(solution)/shard_map/all_to_all | solution.py:321
  15.3 4.2 %self_forward.1 = (bf16[10,256,256]{2,1,0:T(8,128)(2,1)}, bf16[10,128,256]{2,1,0:T(8,128)(2,1)}, f32[10,16,256]{2,1,0:T(8,128)}) custom-call(s32[1,1,4]{2,1,0:T(1,128)} %lens_hbm.1, bf16[1,256,1280]{2,1,0:T(8,128)(2,1)} %q_ref.7, bf16[1,256,512]{2,1,0:T(8,128)(2,1)} %resp_ref.1), custom_call_target="tpu_custom_call" | custom-call | flops 8589934592 | bytes 256 | tf_op jit(solution)/shard_map/self_forward/pallas_call | solution.py:300
  19.5 0.0 copy-start
  19.5 0.0 copy-start.1
  19.6 0.0 copy-start.3
  19.6 0.0 copy-start.5
  19.6 8.2 %all-to-all-done = bf16[64,4,512]{2,1,0:T(4,128)(2,1)S(1)} async-done(((bf16[64,4,512]{2,1,0:T(4,128)(2,1)}), bf16[64,4,512]{2,1,0:T(4,128)(2,1)S(1)}, u32[]{:S(2)}, u32[]{:S(2)}) %all-to-all-start) | async-done | bytes 262176 | tf_op jit(solution)/shard_map/all_to_all | solution.py:321
  27.7 0.1 reshape.22.own_ref
  27.8 2.6 %collective-permute-start = (bf16[256,256]{1,0:T(8,128)(2,1)S(1)}, bf16[256,256]{1,0:T(8,128)(2,1)S(1)}, u32[]{:S(2)}, u32[]{:S(2)}) collective-permute-start(bf16[256,256]{1,0:T(8,128)(2,1)S(1)} %get-tuple-element.73), channel_id=1, source_target_pairs={{0,1},{1,0},{2,3},{3,2},{32,35},{33,34},{34,33},{35,32},{4,5},{5,4... | collective-permute-start | bytes 393224 | tf_op jit(solution)/shard_map/ppermute | solution.py:332
  30.4 0.0 collective-permute-start.3
  30.4 0.8 %collective-permute-start.1 = (bf16[256,256]{1,0:T(8,128)(2,1)S(1)}, bf16[256,256]{1,0:T(8,128)(2,1)S(1)}, u32[]{:S(2)}, u32[]{:S(2)}) collective-permute-start(bf16[256,256]{1,0:T(8,128)(2,1)S(1)} %get-tuple-element.72), channel_id=1, source_target_pairs={{0,1},{1,0},{2,3},{3,2},{32,35},{33,34},{34,33},{35,32},{4,5},{5,4... | collective-permute-start | bytes 393224 | tf_op jit(solution)/shard_map/ppermute | solution.py:332
  31.2 0.7 collective-permute-start.2
  31.9 1.1 %collective-permute-done.one_k = bf16[256,256]{1,0:T(8,128)(2,1)S(1)} collective-permute-done((bf16[256,256]{1,0:T(8,128)(2,1)S(1)}, bf16[256,256]{1,0:T(8,128)(2,1)S(1)}, u32[]{:S(2)}, u32[]{:S(2)}) %collective-permute-start) | collective-permute-done | bytes 131104 | tf_op jit(solution)/shard_map/ppermute | solution.py:332
  33.0 0.0 collective-permute-start.4
  33.0 2.7 %collective-permute-done.3.three_v = bf16[256,256]{1,0:T(8,128)(2,1)S(1)} collective-permute-done((bf16[256,256]{1,0:T(8,128)(2,1)S(1)}, bf16[256,256]{1,0:T(8,128)(2,1)S(1)}, u32[]{:S(2)}, u32[]{:S(2)}) %collective-permute-start.3) | collective-permute-done | bytes 131104 | tf_op jit(solution)/shard_map/ppermute | solution.py:332
  35.7 0.0 collective-permute-start.5
  35.7 0.2 collective-permute-done.1.one_v
  35.9 1.7 %collective-permute-done.2.three_k = bf16[256,256]{1,0:T(8,128)(2,1)S(1)} collective-permute-done((bf16[256,256]{1,0:T(8,128)(2,1)S(1)}, bf16[256,256]{1,0:T(8,128)(2,1)S(1)}, u32[]{:S(2)}, u32[]{:S(2)}) %collective-permute-start.2) | collective-permute-done | bytes 131104 | tf_op jit(solution)/shard_map/ppermute | solution.py:332
  37.6 0.0 copy-done
  37.6 3.3 %next_forward.1 = (bf16[10,768,256]{2,1,0:T(8,128)(2,1)S(1)}, bf16[10,128,256]{2,1,0:T(8,128)(2,1)S(1)}, f32[10,16,256]{2,1,0:T(8,128)S(1)}) custom-call(bf16[1,256,1280]{2,1,0:T(8,128)(2,1)S(1)} %copy-done, bf16[256,256]{1,0:T(8,128)(2,1)S(1)} %collective-permute-done.one_k, bf16[256,256]{1,0:T(8,128)(2,1)S(1)} %collective-permute-done.1.one_v, ...), custom_call_target="tpu_custom_call" | custom-call | flops 256 | bytes 256 | tf_op jit(solution)/shard_map/next_forward/pallas_call | solution.py:300
  40.9 0.0 collective-permute-done.4.k_ref
  40.9 1.1 %collective-permute-done.5.v_ref = bf16[256,256]{1,0:T(8,128)(2,1)S(1)} collective-permute-done((bf16[256,256]{1,0:T(8,128)(2,1)S(1)}, bf16[256,256]{1,0:T(8,128)(2,1)S(1)}, u32[]{:S(2)}, u32[]{:S(2)}) %collective-permute-start.5) | collective-permute-done | bytes 131104 | tf_op jit(solution)/shard_map/ppermute | solution.py:332
  42.0 0.0 copy-done.1
  42.0 0.0 copy-done.3
  42.0 0.0 copy-done.5
  42.0 2.7 %opposite.1 = (bf16[10,128,256]{2,1,0:T(8,128)(2,1)S(1)}, f32[10,128,256]{2,1,0:T(8,128)S(1)}, f32[10,24,256]{2,1,0:T(8,128)S(1)}, bf16[256,256]{1,0:T(8,128)(2,1)S(1)}, bf16[256,256]{1,0:T(8,128)(2,1)S(1)}) custom-call(bf16[1,256,1280]{2,1,0:T(8,128)(2,1)S(1)} %copy-done, bf16[1,256,1280]{2,1,0:T(8,128)(2,1)S(1)} %copy-done.1, ...), custom_call_target="tpu_custom_call" | custom-call | flops 256 | bytes 256 | tf_op jit(solution)/shard_map/opposite/pallas_call | solution.py:300
  44.7 0.3 collective-permute-start.6
  45.0 0.8 collective-permute-start.7
  45.8 0.0 copy-start.2
  45.8 0.0 copy-start.4
  45.8 2.6 %next_backward.1 = (f32[10,128,256]{2,1,0:T(8,128)S(1)}, f32[256,256]{1,0:T(8,128)S(1)}, bf16[256,256]{1,0:T(8,128)(2,1)S(1)}, bf16[256,256]{1,0:T(8,128)(2,1)S(1)}, f32[256,256]{1,0:T(8,128)S(1)}) custom-call(bf16[1,256,1280]{2,1,0:T(8,128)(2,1)S(1)} %copy-done, bf16[1,256,1280]{2,1,0:T(8,128)(2,1)S(1)} %copy-done.1, ...), custom_call_target="tpu_custom_call" | custom-call | flops 256 | bytes 256 | tf_op jit(solution)/shard_map/next_backward/pallas_call | solution.py:300
  48.4 2.1 %collective-permute-start.10 = (bf16[256,256]{1,0:T(8,128)(2,1)S(1)}, bf16[256,256]{1,0:T(8,128)(2,1)S(1)}, u32[]{:S(2)}, u32[]{:S(2)}) collective-permute-start(bf16[256,256]{1,0:T(8,128)(2,1)S(1)} %get-tuple-element.63), channel_id=1, source_target_pairs={{0,1},{1,0},{2,3},{3,2},{32,35},{33,34},{34,33},{35,32},{4,5},{5,4... | collective-permute-start | bytes 393224 | tf_op jit(solution)/shard_map/ppermute | solution.py:332
  50.5 0.2 collective-permute-start.9
  50.6 0.0 collective-permute-done.6
  50.6 0.0 collective-permute-done.7
  50.6 0.1 add_convert_fusion.2
  50.7 1.4 %collective-permute-start.11 = (bf16[256,256]{1,0:T(8,128)(2,1)S(1)}, bf16[256,256]{1,0:T(8,128)(2,1)S(1)}, u32[]{:S(2)}, u32[]{:S(2)}) collective-permute-start(bf16[256,256]{1,0:T(8,128)(2,1)S(1)} %get-tuple-element.64), channel_id=1, source_target_pairs={{0,3},{1,2},{2,1},{3,0},{32,33},{33,32},{34,35},{35,34},{4,7},{5,6... | collective-permute-start | bytes 393224 | tf_op jit(solution)/shard_map/ppermute | solution.py:332
  52.1 0.7 collective-permute-start.8
  52.8 0.0 copy-done.2
  52.8 0.0 copy-done.4
  52.8 3.5 %near_backward.1 = (bf16[1,256,1280]{2,1,0:T(8,128)(2,1)}, bf16[1,256,1280]{2,1,0:T(8,128)(2,1)}, f32[256,512]{1,0:T(8,128)S(1)}, bf16[1,256,512]{2,1,0:T(8,128)(2,1)}) custom-call(bf16[1,256,1280]{2,1,0:T(8,128)(2,1)S(1)} %copy-done, bf16[1,256,1280]{2,1,0:T(8,128)(2,1)S(1)} %copy-done.1, bf16[256,512]{1,0:T(8,128)(2,1)S(1)} %reshape.22.own_ref, ...), custom_call_target="tpu_custom_call" | custom-call | flops 256 | bytes 256 | tf_op jit(solution)/shard_map/near_backward/pallas_call | solution.py:300
  56.3 0.0 collective-permute-done.10
  56.3 0.0 collective-permute-done.9
  56.3 1.1 %collective-permute-done.11 = bf16[256,256]{1,0:T(8,128)(2,1)S(1)} collective-permute-done((bf16[256,256]{1,0:T(8,128)(2,1)S(1)}, bf16[256,256]{1,0:T(8,128)(2,1)S(1)}, u32[]{:S(2)}, u32[]{:S(2)}) %collective-permute-start.11) | collective-permute-done | bytes 131104 | tf_op jit(solution)/shard_map/ppermute | solution.py:332
  57.4 0.6 collective-permute-done.8
  58.0 0.1 add_convert_fusion.1
  58.1 0.1 reshape.23
  58.2 19.5 %all_to_all.10 = bf16[64,4,512]{2,1,0:T(4,128)(2,1)S(1)} all-to-all(bf16[64,4,512]{2,1,0:T(4,128)(2,1)S(1)} %reshape.23), channel_id=1, replica_groups=mesh['zl'=4,'c'=2,'zh'=2,'y'=4,'x'=4] {'zl','c','zh','y'}, dimensions={0} | all-to-all | bytes 524288 | tf_op jit(solution)/shard_map/all_to_all | solution.py:321
  77.7 0.7 bitcast_reduce_fusion
  (2 shorter events, 0.0 us)
Async XLA Ops:
  2.2 25.6 %all-to-all-start = ((bf16[64,4,512]{2,1,0:T(4,128)(2,1)}), bf16[64,4,512]{2,1,0:T(4,128)(2,1)S(1)}, u32[]{:S(2)}, u32[]{:S(2)}) async-start(bf16[64,4,512]{2,1,0:T(4,128)(2,1)} %bitcast), calls=%async_computation | async-start | bytes 524288 | tf_op jit(solution)/shard_map/all_to_all | solution.py:321
  19.5 18.1 %copy-start = (bf16[1,256,1280]{2,1,0:T(8,128)(2,1)S(1)}, bf16[1,256,1280]{2,1,0:T(8,128)(2,1)}, u32[]{:S(2)}) copy-start(bf16[1,256,1280]{2,1,0:T(8,128)(2,1)} %q_ref.7) | copy-start | bytes 1966084
  19.5 22.4 %copy-start.1 = (bf16[1,256,1280]{2,1,0:T(8,128)(2,1)S(1)}, bf16[1,256,1280]{2,1,0:T(8,128)(2,1)}, u32[]{:S(2)}) copy-start(bf16[1,256,1280]{2,1,0:T(8,128)(2,1)} %do_ref.5) | copy-start | bytes 1966084
  19.6 22.4 %copy-start.3 = (bf16[10,128,256]{2,1,0:T(8,128)(2,1)S(1)}, bf16[10,128,256]{2,1,0:T(8,128)(2,1)}, u32[]{:S(2)}) copy-start(bf16[10,128,256]{2,1,0:T(8,128)(2,1)} %get-tuple-element.41.self_out_ref) | copy-start | bytes 1966084
  19.6 22.4 %copy-start.5 = (f32[10,16,256]{2,1,0:T(8,128)S(1)}, f32[10,16,256]{2,1,0:T(8,128)}, u32[]{:S(2)}) copy-start(f32[10,16,256]{2,1,0:T(8,128)} %get-tuple-element.42.self_stat_ref) | copy-start | bytes 491524
  27.8 5.1 %collective-permute-start = (bf16[256,256]{1,0:T(8,128)(2,1)S(1)}, bf16[256,256]{1,0:T(8,128)(2,1)S(1)}, u32[]{:S(2)}, u32[]{:S(2)}) collective-permute-start(bf16[256,256]{1,0:T(8,128)(2,1)S(1)} %get-tuple-element.73), channel_id=1, source_target_pairs={{0,1},{1,0},{2,3},{3,2},{32,35},{33,34},{34,33},{35,32},{4,5},{5,4... | collective-permute-start | bytes 393224 | tf_op jit(solution)/shard_map/ppermute | solution.py:332
  30.4 5.3 %collective-permute-start.3 = (bf16[256,256]{1,0:T(8,128)(2,1)S(1)}, bf16[256,256]{1,0:T(8,128)(2,1)S(1)}, u32[]{:S(2)}, u32[]{:S(2)}) collective-permute-start(bf16[256,256]{1,0:T(8,128)(2,1)S(1)} %get-tuple-element.72), channel_id=1, source_target_pairs={{0,3},{1,2},{2,1},{3,0},{32,33},{33,32},{34,35},{35,34},{4,7},{5,6... | collective-permute-start | bytes 393224 | tf_op jit(solution)/shard_map/ppermute | solution.py:332
  30.4 5.5 %collective-permute-start.1 = (bf16[256,256]{1,0:T(8,128)(2,1)S(1)}, bf16[256,256]{1,0:T(8,128)(2,1)S(1)}, u32[]{:S(2)}, u32[]{:S(2)}) collective-permute-start(bf16[256,256]{1,0:T(8,128)(2,1)S(1)} %get-tuple-element.72), channel_id=1, source_target_pairs={{0,1},{1,0},{2,3},{3,2},{32,35},{33,34},{34,33},{35,32},{4,5},{5,4... | collective-permute-start | bytes 393224 | tf_op jit(solution)/shard_map/ppermute | solution.py:332
  31.2 6.4 %collective-permute-start.2 = (bf16[256,256]{1,0:T(8,128)(2,1)S(1)}, bf16[256,256]{1,0:T(8,128)(2,1)S(1)}, u32[]{:S(2)}, u32[]{:S(2)}) collective-permute-start(bf16[256,256]{1,0:T(8,128)(2,1)S(1)} %get-tuple-element.73), channel_id=1, source_target_pairs={{0,3},{1,2},{2,1},{3,0},{32,33},{33,32},{34,35},{35,34},{4,7},{5,6... | collective-permute-start | bytes 393224 | tf_op jit(solution)/shard_map/ppermute | solution.py:332
  33.0 7.9 %collective-permute-start.4 = (bf16[256,256]{1,0:T(8,128)(2,1)S(1)}, bf16[256,256]{1,0:T(8,128)(2,1)S(1)}, u32[]{:S(2)}, u32[]{:S(2)}) collective-permute-start(bf16[256,256]{1,0:T(8,128)(2,1)S(1)} %collective-permute-done.one_k), channel_id=1, source_target_pairs={{0,3},{1,2},{2,1},{3,0},{32,33},{33,32},{34,35},{35,34},{4,7},{5,6... | collective-permute-start | bytes 393224 | tf_op jit(solution)/shard_map/ppermute | solution.py:332
  35.7 6.3 %collective-permute-start.5 = (bf16[256,256]{1,0:T(8,128)(2,1)S(1)}, bf16[256,256]{1,0:T(8,128)(2,1)S(1)}, u32[]{:S(2)}, u32[]{:S(2)}) collective-permute-start(bf16[256,256]{1,0:T(8,128)(2,1)S(1)} %collective-permute-done.3.three_v), channel_id=1, source_target_pairs={{0,1},{1,0},{2,3},{3,2},{32,35},{33,34},{34,33},{35,32},{4,5},{5,4... | collective-permute-start | bytes 393224 | tf_op jit(solution)/shard_map/ppermute | solution.py:332
  44.7 5.9 %collective-permute-start.6 = (bf16[256,256]{1,0:T(8,128)(2,1)S(1)}, bf16[256,256]{1,0:T(8,128)(2,1)S(1)}, u32[]{:S(2)}, u32[]{:S(2)}) collective-permute-start(bf16[256,256]{1,0:T(8,128)(2,1)S(1)} %get-tuple-element.53), channel_id=1, source_target_pairs={{0,3},{1,2},{2,1},{3,0},{32,33},{33,32},{34,35},{35,34},{4,7},{5,6... | collective-permute-start | bytes 393224 | tf_op jit(solution)/shard_map/ppermute | solution.py:332
  45.0 5.6 %collective-permute-start.7 = (bf16[256,256]{1,0:T(8,128)(2,1)S(1)}, bf16[256,256]{1,0:T(8,128)(2,1)S(1)}, u32[]{:S(2)}, u32[]{:S(2)}) collective-permute-start(bf16[256,256]{1,0:T(8,128)(2,1)S(1)} %get-tuple-element.54), channel_id=1, source_target_pairs={{0,1},{1,0},{2,3},{3,2},{32,35},{33,34},{34,33},{35,32},{4,5},{5,4... | collective-permute-start | bytes 393224 | tf_op jit(solution)/shard_map/ppermute | solution.py:332
  45.8 7.0 %copy-start.2 = (bf16[10,256,256]{2,1,0:T(8,128)(2,1)S(1)}, bf16[10,256,256]{2,1,0:T(8,128)(2,1)}, u32[]{:S(2)}) copy-start(bf16[10,256,256]{2,1,0:T(8,128)(2,1)} %get-tuple-element.40.self_low_ref) | copy-start | bytes 3932164
  45.8 7.0 %copy-start.4 = (bf16[1,256,512]{2,1,0:T(8,128)(2,1)S(1)}, bf16[1,256,512]{2,1,0:T(8,128)(2,1)}, u32[]{:S(2)}) copy-start(bf16[1,256,512]{2,1,0:T(8,128)(2,1)} %resp_ref.1) | copy-start | bytes 786436
  48.4 7.9 %collective-permute-start.10 = (bf16[256,256]{1,0:T(8,128)(2,1)S(1)}, bf16[256,256]{1,0:T(8,128)(2,1)S(1)}, u32[]{:S(2)}, u32[]{:S(2)}) collective-permute-start(bf16[256,256]{1,0:T(8,128)(2,1)S(1)} %get-tuple-element.63), channel_id=1, source_target_pairs={{0,1},{1,0},{2,3},{3,2},{32,35},{33,34},{34,33},{35,32},{4,5},{5,4... | collective-permute-start | bytes 393224 | tf_op jit(solution)/shard_map/ppermute | solution.py:332
  50.5 5.8 %collective-permute-start.9 = (bf16[256,256]{1,0:T(8,128)(2,1)S(1)}, bf16[256,256]{1,0:T(8,128)(2,1)S(1)}, u32[]{:S(2)}, u32[]{:S(2)}) collective-permute-start(bf16[256,256]{1,0:T(8,128)(2,1)S(1)} %get-tuple-element.62), channel_id=1, source_target_pairs={{0,3},{1,2},{2,1},{3,0},{32,33},{33,32},{34,35},{35,34},{4,7},{5,6... | collective-permute-start | bytes 393224 | tf_op jit(solution)/shard_map/ppermute | solution.py:332
  50.7 6.7 %collective-permute-start.11 = (bf16[256,256]{1,0:T(8,128)(2,1)S(1)}, bf16[256,256]{1,0:T(8,128)(2,1)S(1)}, u32[]{:S(2)}, u32[]{:S(2)}) collective-permute-start(bf16[256,256]{1,0:T(8,128)(2,1)S(1)} %get-tuple-element.64), channel_id=1, source_target_pairs={{0,3},{1,2},{2,1},{3,0},{32,33},{33,32},{34,35},{35,34},{4,7},{5,6... | collective-permute-start | bytes 393224 | tf_op jit(solution)/shard_map/ppermute | solution.py:332
  52.1 5.9 %collective-permute-start.8 = (bf16[256,256]{1,0:T(8,128)(2,1)S(1)}, bf16[256,256]{1,0:T(8,128)(2,1)S(1)}, u32[]{:S(2)}, u32[]{:S(2)}) collective-permute-start(bf16[256,256]{1,0:T(8,128)(2,1)S(1)} %get-tuple-element.61), channel_id=1, source_target_pairs={{0,1},{1,0},{2,3},{3,2},{32,35},{33,34},{34,33},{35,32},{4,5},{5,4... | collective-permute-start | bytes 393224 | tf_op jit(solution)/shard_map/ppermute | solution.py:332

commit v6 on v5

--- a/solution.py
+++ b/solution.py
@@ -106,7 +106,7 @@
             s = dot_nn(k[:, of_group(h)], q_t)
             if bias_ref is not None and at is places[-1]:
                 s = s + bias_ref[...]
-            scores_ref[h % 2, at] = s
+            scores_ref[h % 3, at] = s
             s = by_eights(jnp.max, s)
             top = s if top is None else jnp.maximum(top, s)
         tops[h] = jnp.max(top, axis=0, keepdims=True) * (SCALE * LOG2E)
@@ -114,7 +114,7 @@
     def weight_pass(h):
         sums, out_t = 0.0, 0.0
         for at, v_t in zip(places, vals_t[h // REPEAT]):
-            weights = jnp.exp2(scores_ref[h % 2, at] * (SCALE * LOG2E) - tops[h])
+            weights = jnp.exp2(scores_ref[h % 3, at] * (SCALE * LOG2E) - tops[h])
             low = weights.astype(bf16)
             low_ref[h, at] = low
             sums = sums + by_eights(jnp.sum, weights)
@@ -124,10 +124,11 @@
         out_ref[h] = out_t.astype(bf16)
 
     score_pass(0)
+    score_pass(1)
     for h in range(HEADS):
-        if h + 1 < HEADS:
-            score_pass(h + 1)
         weight_pass(h)
+        if h + 2 < HEADS:
+            score_pass(h + 2)
 
 
 def backward(q_ref, do_ref, chunks, lows, shares, stat_ref, acc, d_probs_ref, put_dq, put_sums):
@@ -138,7 +139,7 @@
     def d_probs_pass(h):
         d_outs[h] = do_ref[0, :, of_head(h)].T
         for at, (_, v) in zip(places, chunks):
-            d_probs_ref[h % 2, at] = dot_nn(v[:, of_group(h)], d_outs[h])
+            d_probs_ref[h % 3, at] = dot_nn(v[:, of_group(h)], d_outs[h])
 
     def add(h, j, at, new):
         acc[j, :, at] = new if h % REPEAT == 0 else acc[j, :, at] + new
@@ -153,7 +154,7 @@
             add(h, 1, at, dot_nt(do_scaled[which], low(h)))
         dq_t = {at: 0.0 for at in share}
         for at, low, which, k_t in zip(places, lows, shares, keys_t[h // REPEAT]):
-            d_probs = d_probs_ref[h % 2, at] - delta
+            d_probs = d_probs_ref[h % 3, at] - delta
             d_scores = (low(h).astype(f32) * d_probs).astype(bf16)
             dq_t[which] = dq_t[which] + dot_nn(k_t, d_scores)
             add(h, 0, at, dot_nt(q_scaled[which], d_scores))
@@ -163,10 +164,11 @@
                 put_sums(j, of_group(h), [acc[j, :, at].T for at in places])
 
     d_probs_pass(0)
+    d_probs_pass(1)
     for h in range(HEADS):
-        if h + 1 < HEADS:
-            d_probs_pass(h + 1)
         gradient_pass(h)
+        if h + 2 < HEADS:
+            d_probs_pass(h + 2)
 
 
 def self_forward_kernel(
@@ -342,7 +344,7 @@
     flat, resp_kind, prompt = (q_resp.shape, bf16), (resp_kv.shape, bf16), own.shape
     tall, stat_kind = (HEADS, HEAD, ROWS), ((HEADS, 16, ROWS), f32)
     parts = lambda n: [((HEADS, n * ROWS, ROWS), bf16), (tall, bf16), stat_kind]
-    scores = lambda n: ((2, n * ROWS, ROWS), f32)
+    scores = lambda n: ((3, n * ROWS, ROWS), f32)
     sums = ((2, HEAD, 2 * ROWS), f32)
     self_low, self_out, self_stat = call(
         self_forward_kernel,

time: 78.7 us -> 78.7 us (level)
  no operation moved by 1% of the time
where the time goes in v6:
time: 78.7 us; the launch traced here: 78.4 us
  starting transfers between devices  22.5 us (29%)
  blocking collectives  19.5 us (25%)
  waiting for transfers between devices  16.7 us (21%)
  Pallas kernels  16.3 us (21%)
  local copies, waits for them, and re-layouts  1.72 us (2%)
  other arithmetic  0.88 us (1%)
    all_to_all x1, blocking collectives, exchange(): return lax.all_to_all(t, axes, split_axis=0, concat_axis=0, tiled=True)  19.5 us
    pallas_call x5, Pallas kernels, call(): pl.pallas_call(kernel, grid=(1,), in_specs=[hbm if in_hbm else specs.get(...  16.3 us
    all_to_all x1, starting transfers between devices, exchange(): return lax.all_to_all(t, axes, split_axis=0, concat_axis=0, tiled=True)  13.2 us
    ppermute x12, starting transfers between devices, to_neighbour(): return lax.ppermute(t, ('c', 'x'), pairs)  9.38 us
    ppermute x12, waiting for transfers between devices, to_neighbour(): return lax.ppermute(t, ('c', 'x'), pairs)  8.55 us
    all_to_all x1, waiting for transfers between devices, exchange(): return lax.all_to_all(t, axes, split_axis=0, concat_axis=0, tiled=True)  8.17 us
  transfers between devices with their start and end apart: 13, of which 8 were waited for; matrix products, arithmetic and copies ran while one was open for 0% of the time, Pallas kernels for 17%

profile of v6, /device:TPU:1, one launch (start us, length us, event | category | flops | bytes accessed | tf_op | source)
XLA Modules:
  0.0 78.4 jit_solution(9403189980949475627)
XLA Ops:
  0.6 1.5 %broadcast_in_dim.2 = bf16[8,8,4,512]{3,2,1,0:T(4,128)(2,1)} broadcast(bf16[8,4,512]{2,1,0:T(4,128)(2,1)} %param.7), dimensions={0,2,3} | broadcast | bytes 294912 | tf_op jit(solution)/shard_map/broadcast_in_dim | solution.py:341
  2.2 13.2 %all-to-all-start = ((bf16[64,4,512]{2,1,0:T(4,128)(2,1)}), bf16[64,4,512]{2,1,0:T(4,128)(2,1)S(1)}, u32[]{:S(2)}, u32[]{:S(2)}) async-start(bf16[64,4,512]{2,1,0:T(4,128)(2,1)} %bitcast), calls=%async_computation | async-start | bytes 524288 | tf_op jit(solution)/shard_map/all_to_all | solution.py:323
  15.3 4.2 %self_forward.1 = (bf16[10,256,256]{2,1,0:T(8,128)(2,1)}, bf16[10,128,256]{2,1,0:T(8,128)(2,1)}, f32[10,16,256]{2,1,0:T(8,128)}) custom-call(s32[1,1,4]{2,1,0:T(1,128)} %lens_hbm.1, bf16[1,256,1280]{2,1,0:T(8,128)(2,1)} %q_ref.7, bf16[1,256,512]{2,1,0:T(8,128)(2,1)} %resp_ref.1), custom_call_target="tpu_custom_call" | custom-call | flops 8589934592 | bytes 256 | tf_op jit(solution)/shard_map/self_forward/pallas_call | solution.py:302
  19.5 0.0 copy-start
  19.5 0.0 copy-start.1
  19.6 0.0 copy-start.3
  19.6 0.0 copy-start.5
  19.6 8.2 %all-to-all-done = bf16[64,4,512]{2,1,0:T(4,128)(2,1)S(1)} async-done(((bf16[64,4,512]{2,1,0:T(4,128)(2,1)}), bf16[64,4,512]{2,1,0:T(4,128)(2,1)S(1)}, u32[]{:S(2)}, u32[]{:S(2)}) %all-to-all-start) | async-done | bytes 262176 | tf_op jit(solution)/shard_map/all_to_all | solution.py:323
  27.7 0.1 reshape.22.own_ref
  27.8 2.6 %collective-permute-start = (bf16[256,256]{1,0:T(8,128)(2,1)S(1)}, bf16[256,256]{1,0:T(8,128)(2,1)S(1)}, u32[]{:S(2)}, u32[]{:S(2)}) collective-permute-start(bf16[256,256]{1,0:T(8,128)(2,1)S(1)} %get-tuple-element.73), channel_id=1, source_target_pairs={{0,1},{1,0},{2,3},{3,2},{32,35},{33,34},{34,33},{35,32},{4,5},{5,4... | collective-permute-start | bytes 393224 | tf_op jit(solution)/shard_map/ppermute | solution.py:334
  30.4 0.0 collective-permute-start.3
  30.4 0.8 %collective-permute-start.1 = (bf16[256,256]{1,0:T(8,128)(2,1)S(1)}, bf16[256,256]{1,0:T(8,128)(2,1)S(1)}, u32[]{:S(2)}, u32[]{:S(2)}) collective-permute-start(bf16[256,256]{1,0:T(8,128)(2,1)S(1)} %get-tuple-element.72), channel_id=1, source_target_pairs={{0,1},{1,0},{2,3},{3,2},{32,35},{33,34},{34,33},{35,32},{4,5},{5,4... | collective-permute-start | bytes 393224 | tf_op jit(solution)/shard_map/ppermute | solution.py:334
  31.2 0.7 collective-permute-start.2
  31.9 1.1 %collective-permute-done.one_k = bf16[256,256]{1,0:T(8,128)(2,1)S(1)} collective-permute-done((bf16[256,256]{1,0:T(8,128)(2,1)S(1)}, bf16[256,256]{1,0:T(8,128)(2,1)S(1)}, u32[]{:S(2)}, u32[]{:S(2)}) %collective-permute-start) | collective-permute-done | bytes 131104 | tf_op jit(solution)/shard_map/ppermute | solution.py:334
  33.0 0.0 collective-permute-start.4
  33.0 2.7 %collective-permute-done.3.three_v = bf16[256,256]{1,0:T(8,128)(2,1)S(1)} collective-permute-done((bf16[256,256]{1,0:T(8,128)(2,1)S(1)}, bf16[256,256]{1,0:T(8,128)(2,1)S(1)}, u32[]{:S(2)}, u32[]{:S(2)}) %collective-permute-start.3) | collective-permute-done | bytes 131104 | tf_op jit(solution)/shard_map/ppermute | solution.py:334
  35.7 0.0 collective-permute-start.5
  35.7 0.2 collective-permute-done.1.one_v
  35.9 1.7 %collective-permute-done.2.three_k = bf16[256,256]{1,0:T(8,128)(2,1)S(1)} collective-permute-done((bf16[256,256]{1,0:T(8,128)(2,1)S(1)}, bf16[256,256]{1,0:T(8,128)(2,1)S(1)}, u32[]{:S(2)}, u32[]{:S(2)}) %collective-permute-start.2) | collective-permute-done | bytes 131104 | tf_op jit(solution)/shard_map/ppermute | solution.py:334
  37.6 0.0 copy-done
  37.6 3.3 %next_forward.1 = (bf16[10,768,256]{2,1,0:T(8,128)(2,1)S(1)}, bf16[10,128,256]{2,1,0:T(8,128)(2,1)S(1)}, f32[10,16,256]{2,1,0:T(8,128)S(1)}) custom-call(bf16[1,256,1280]{2,1,0:T(8,128)(2,1)S(1)} %copy-done, bf16[256,256]{1,0:T(8,128)(2,1)S(1)} %collective-permute-done.one_k, bf16[256,256]{1,0:T(8,128)(2,1)S(1)} %collective-permute-done.1.one_v, ...), custom_call_target="tpu_custom_call" | custom-call | flops 256 | bytes 256 | tf_op jit(solution)/shard_map/next_forward/pallas_call | solution.py:302
  40.9 0.0 collective-permute-done.4.k_ref
  40.9 1.1 %collective-permute-done.5.v_ref = bf16[256,256]{1,0:T(8,128)(2,1)S(1)} collective-permute-done((bf16[256,256]{1,0:T(8,128)(2,1)S(1)}, bf16[256,256]{1,0:T(8,128)(2,1)S(1)}, u32[]{:S(2)}, u32[]{:S(2)}) %collective-permute-start.5) | collective-permute-done | bytes 131104 | tf_op jit(solution)/shard_map/ppermute | solution.py:334
  42.0 0.0 copy-done.1
  42.0 0.0 copy-done.3
  42.0 0.0 copy-done.5
  42.0 2.7 %opposite.1 = (bf16[10,128,256]{2,1,0:T(8,128)(2,1)S(1)}, f32[10,128,256]{2,1,0:T(8,128)S(1)}, f32[10,24,256]{2,1,0:T(8,128)S(1)}, bf16[256,256]{1,0:T(8,128)(2,1)S(1)}, bf16[256,256]{1,0:T(8,128)(2,1)S(1)}) custom-call(bf16[1,256,1280]{2,1,0:T(8,128)(2,1)S(1)} %copy-done, bf16[1,256,1280]{2,1,0:T(8,128)(2,1)S(1)} %copy-done.1, ...), custom_call_target="tpu_custom_call" | custom-call | flops 256 | bytes 256 | tf_op jit(solution)/shard_map/opposite/pallas_call | solution.py:302
  44.7 0.3 collective-permute-start.6
  45.0 0.8 collective-permute-start.7
  45.8 0.0 copy-start.2
  45.8 0.0 copy-start.4
  45.8 2.6 %next_backward.1 = (f32[10,128,256]{2,1,0:T(8,128)S(1)}, f32[256,256]{1,0:T(8,128)S(1)}, bf16[256,256]{1,0:T(8,128)(2,1)S(1)}, bf16[256,256]{1,0:T(8,128)(2,1)S(1)}, f32[256,256]{1,0:T(8,128)S(1)}) custom-call(bf16[1,256,1280]{2,1,0:T(8,128)(2,1)S(1)} %copy-done, bf16[1,256,1280]{2,1,0:T(8,128)(2,1)S(1)} %copy-done.1, ...), custom_call_target="tpu_custom_call" | custom-call | flops 256 | bytes 256 | tf_op jit(solution)/shard_map/next_backward/pallas_call | solution.py:302
  48.4 2.1 %collective-permute-start.10 = (bf16[256,256]{1,0:T(8,128)(2,1)S(1)}, bf16[256,256]{1,0:T(8,128)(2,1)S(1)}, u32[]{:S(2)}, u32[]{:S(2)}) collective-permute-start(bf16[256,256]{1,0:T(8,128)(2,1)S(1)} %get-tuple-element.63), channel_id=1, source_target_pairs={{0,1},{1,0},{2,3},{3,2},{32,35},{33,34},{34,33},{35,32},{4,5},{5,4... | collective-permute-start | bytes 393224 | tf_op jit(solution)/shard_map/ppermute | solution.py:334
  50.5 0.2 collective-permute-start.9
  50.6 0.0 collective-permute-done.6
  50.6 0.0 collective-permute-done.7
  50.6 0.1 add_convert_fusion.2
  50.7 1.4 %collective-permute-start.11 = (bf16[256,256]{1,0:T(8,128)(2,1)S(1)}, bf16[256,256]{1,0:T(8,128)(2,1)S(1)}, u32[]{:S(2)}, u32[]{:S(2)}) collective-permute-start(bf16[256,256]{1,0:T(8,128)(2,1)S(1)} %get-tuple-element.64), channel_id=1, source_target_pairs={{0,3},{1,2},{2,1},{3,0},{32,33},{33,32},{34,35},{35,34},{4,7},{5,6... | collective-permute-start | bytes 393224 | tf_op jit(solution)/shard_map/ppermute | solution.py:334
  52.1 0.7 collective-permute-start.8
  52.8 0.0 copy-done.2
  52.8 0.0 copy-done.4
  52.8 3.5 %near_backward.1 = (bf16[1,256,1280]{2,1,0:T(8,128)(2,1)}, bf16[1,256,1280]{2,1,0:T(8,128)(2,1)}, f32[256,512]{1,0:T(8,128)S(1)}, bf16[1,256,512]{2,1,0:T(8,128)(2,1)}) custom-call(bf16[1,256,1280]{2,1,0:T(8,128)(2,1)S(1)} %copy-done, bf16[1,256,1280]{2,1,0:T(8,128)(2,1)S(1)} %copy-done.1, bf16[256,512]{1,0:T(8,128)(2,1)S(1)} %reshape.22.own_ref, ...), custom_call_target="tpu_custom_call" | custom-call | flops 256 | bytes 256 | tf_op jit(solution)/shard_map/near_backward/pallas_call | solution.py:302
  56.3 0.0 collective-permute-done.10
  56.3 0.0 collective-permute-done.9
  56.3 1.1 %collective-permute-done.11 = bf16[256,256]{1,0:T(8,128)(2,1)S(1)} collective-permute-done((bf16[256,256]{1,0:T(8,128)(2,1)S(1)}, bf16[256,256]{1,0:T(8,128)(2,1)S(1)}, u32[]{:S(2)}, u32[]{:S(2)}) %collective-permute-start.11) | collective-permute-done | bytes 131104 | tf_op jit(solution)/shard_map/ppermute | solution.py:334
  57.4 0.6 collective-permute-done.8
  58.0 0.1 add_convert_fusion.1
  58.1 0.1 reshape.23
  58.2 19.5 %all_to_all.10 = bf16[64,4,512]{2,1,0:T(4,128)(2,1)S(1)} all-to-all(bf16[64,4,512]{2,1,0:T(4,128)(2,1)S(1)} %reshape.23), channel_id=1, replica_groups=mesh['zl'=4,'c'=2,'zh'=2,'y'=4,'x'=4] {'zl','c','zh','y'}, dimensions={0} | all-to-all | bytes 524288 | tf_op jit(solution)/shard_map/all_to_all | solution.py:323
  77.7 0.7 bitcast_reduce_fusion
  (2 shorter events, 0.0 us)
Async XLA Ops:
  2.2 25.6 %all-to-all-start = ((bf16[64,4,512]{2,1,0:T(4,128)(2,1)}), bf16[64,4,512]{2,1,0:T(4,128)(2,1)S(1)}, u32[]{:S(2)}, u32[]{:S(2)}) async-start(bf16[64,4,512]{2,1,0:T(4,128)(2,1)} %bitcast), calls=%async_computation | async-start | bytes 524288 | tf_op jit(solution)/shard_map/all_to_all | solution.py:323
  19.5 18.1 %copy-start = (bf16[1,256,1280]{2,1,0:T(8,128)(2,1)S(1)}, bf16[1,256,1280]{2,1,0:T(8,128)(2,1)}, u32[]{:S(2)}) copy-start(bf16[1,256,1280]{2,1,0:T(8,128)(2,1)} %q_ref.7) | copy-start | bytes 1966084
  19.5 22.4 %copy-start.1 = (bf16[1,256,1280]{2,1,0:T(8,128)(2,1)S(1)}, bf16[1,256,1280]{2,1,0:T(8,128)(2,1)}, u32[]{:S(2)}) copy-start(bf16[1,256,1280]{2,1,0:T(8,128)(2,1)} %do_ref.5) | copy-start | bytes 1966084
  19.6 22.4 %copy-start.3 = (bf16[10,128,256]{2,1,0:T(8,128)(2,1)S(1)}, bf16[10,128,256]{2,1,0:T(8,128)(2,1)}, u32[]{:S(2)}) copy-start(bf16[10,128,256]{2,1,0:T(8,128)(2,1)} %get-tuple-element.41.self_out_ref) | copy-start | bytes 1966084
  19.6 22.4 %copy-start.5 = (f32[10,16,256]{2,1,0:T(8,128)S(1)}, f32[10,16,256]{2,1,0:T(8,128)}, u32[]{:S(2)}) copy-start(f32[10,16,256]{2,1,0:T(8,128)} %get-tuple-element.42.self_stat_ref) | copy-start | bytes 491524
  27.8 5.1 %collective-permute-start = (bf16[256,256]{1,0:T(8,128)(2,1)S(1)}, bf16[256,256]{1,0:T(8,128)(2,1)S(1)}, u32[]{:S(2)}, u32[]{:S(2)}) collective-permute-start(bf16[256,256]{1,0:T(8,128)(2,1)S(1)} %get-tuple-element.73), channel_id=1, source_target_pairs={{0,1},{1,0},{2,3},{3,2},{32,35},{33,34},{34,33},{35,32},{4,5},{5,4... | collective-permute-start | bytes 393224 | tf_op jit(solution)/shard_map/ppermute | solution.py:334
  30.4 5.3 %collective-permute-start.3 = (bf16[256,256]{1,0:T(8,128)(2,1)S(1)}, bf16[256,256]{1,0:T(8,128)(2,1)S(1)}, u32[]{:S(2)}, u32[]{:S(2)}) collective-permute-start(bf16[256,256]{1,0:T(8,128)(2,1)S(1)} %get-tuple-element.72), channel_id=1, source_target_pairs={{0,3},{1,2},{2,1},{3,0},{32,33},{33,32},{34,35},{35,34},{4,7},{5,6... | collective-permute-start | bytes 393224 | tf_op jit(solution)/shard_map/ppermute | solution.py:334
  30.4 5.5 %collective-permute-start.1 = (bf16[256,256]{1,0:T(8,128)(2,1)S(1)}, bf16[256,256]{1,0:T(8,128)(2,1)S(1)}, u32[]{:S(2)}, u32[]{:S(2)}) collective-permute-start(bf16[256,256]{1,0:T(8,128)(2,1)S(1)} %get-tuple-element.72), channel_id=1, source_target_pairs={{0,1},{1,0},{2,3},{3,2},{32,35},{33,34},{34,33},{35,32},{4,5},{5,4... | collective-permute-start | bytes 393224 | tf_op jit(solution)/shard_map/ppermute | solution.py:334
  31.2 6.4 %collective-permute-start.2 = (bf16[256,256]{1,0:T(8,128)(2,1)S(1)}, bf16[256,256]{1,0:T(8,128)(2,1)S(1)}, u32[]{:S(2)}, u32[]{:S(2)}) collective-permute-start(bf16[256,256]{1,0:T(8,128)(2,1)S(1)} %get-tuple-element.73), channel_id=1, source_target_pairs={{0,3},{1,2},{2,1},{3,0},{32,33},{33,32},{34,35},{35,34},{4,7},{5,6... | collective-permute-start | bytes 393224 | tf_op jit(solution)/shard_map/ppermute | solution.py:334
  33.0 7.9 %collective-permute-start.4 = (bf16[256,256]{1,0:T(8,128)(2,1)S(1)}, bf16[256,256]{1,0:T(8,128)(2,1)S(1)}, u32[]{:S(2)}, u32[]{:S(2)}) collective-permute-start(bf16[256,256]{1,0:T(8,128)(2,1)S(1)} %collective-permute-done.one_k), channel_id=1, source_target_pairs={{0,3},{1,2},{2,1},{3,0},{32,33},{33,32},{34,35},{35,34},{4,7},{5,6... | collective-permute-start | bytes 393224 | tf_op jit(solution)/shard_map/ppermute | solution.py:334
  35.7 6.3 %collective-permute-start.5 = (bf16[256,256]{1,0:T(8,128)(2,1)S(1)}, bf16[256,256]{1,0:T(8,128)(2,1)S(1)}, u32[]{:S(2)}, u32[]{:S(2)}) collective-permute-start(bf16[256,256]{1,0:T(8,128)(2,1)S(1)} %collective-permute-done.3.three_v), channel_id=1, source_target_pairs={{0,1},{1,0},{2,3},{3,2},{32,35},{33,34},{34,33},{35,32},{4,5},{5,4... | collective-permute-start | bytes 393224 | tf_op jit(solution)/shard_map/ppermute | solution.py:334
  44.7 5.9 %collective-permute-start.6 = (bf16[256,256]{1,0:T(8,128)(2,1)S(1)}, bf16[256,256]{1,0:T(8,128)(2,1)S(1)}, u32[]{:S(2)}, u32[]{:S(2)}) collective-permute-start(bf16[256,256]{1,0:T(8,128)(2,1)S(1)} %get-tuple-element.53), channel_id=1, source_target_pairs={{0,3},{1,2},{2,1},{3,0},{32,33},{33,32},{34,35},{35,34},{4,7},{5,6... | collective-permute-start | bytes 393224 | tf_op jit(solution)/shard_map/ppermute | solution.py:334
  45.0 5.6 %collective-permute-start.7 = (bf16[256,256]{1,0:T(8,128)(2,1)S(1)}, bf16[256,256]{1,0:T(8,128)(2,1)S(1)}, u32[]{:S(2)}, u32[]{:S(2)}) collective-permute-start(bf16[256,256]{1,0:T(8,128)(2,1)S(1)} %get-tuple-element.54), channel_id=1, source_target_pairs={{0,1},{1,0},{2,3},{3,2},{32,35},{33,34},{34,33},{35,32},{4,5},{5,4... | collective-permute-start | bytes 393224 | tf_op jit(solution)/shard_map/ppermute | solution.py:334
  45.8 7.0 %copy-start.2 = (bf16[10,256,256]{2,1,0:T(8,128)(2,1)S(1)}, bf16[10,256,256]{2,1,0:T(8,128)(2,1)}, u32[]{:S(2)}) copy-start(bf16[10,256,256]{2,1,0:T(8,128)(2,1)} %get-tuple-element.40.self_low_ref) | copy-start | bytes 3932164
  45.8 7.0 %copy-start.4 = (bf16[1,256,512]{2,1,0:T(8,128)(2,1)S(1)}, bf16[1,256,512]{2,1,0:T(8,128)(2,1)}, u32[]{:S(2)}) copy-start(bf16[1,256,512]{2,1,0:T(8,128)(2,1)} %resp_ref.1) | copy-start | bytes 786436
  48.4 7.9 %collective-permute-start.10 = (bf16[256,256]{1,0:T(8,128)(2,1)S(1)}, bf16[256,256]{1,0:T(8,128)(2,1)S(1)}, u32[]{:S(2)}, u32[]{:S(2)}) collective-permute-start(bf16[256,256]{1,0:T(8,128)(2,1)S(1)} %get-tuple-element.63), channel_id=1, source_target_pairs={{0,1},{1,0},{2,3},{3,2},{32,35},{33,34},{34,33},{35,32},{4,5},{5,4... | collective-permute-start | bytes 393224 | tf_op jit(solution)/shard_map/ppermute | solution.py:334
  50.5 5.8 %collective-permute-start.9 = (bf16[256,256]{1,0:T(8,128)(2,1)S(1)}, bf16[256,256]{1,0:T(8,128)(2,1)S(1)}, u32[]{:S(2)}, u32[]{:S(2)}) collective-permute-start(bf16[256,256]{1,0:T(8,128)(2,1)S(1)} %get-tuple-element.62), channel_id=1, source_target_pairs={{0,3},{1,2},{2,1},{3,0},{32,33},{33,32},{34,35},{35,34},{4,7},{5,6... | collective-permute-start | bytes 393224 | tf_op jit(solution)/shard_map/ppermute | solution.py:334
  50.7 6.7 %collective-permute-start.11 = (bf16[256,256]{1,0:T(8,128)(2,1)S(1)}, bf16[256,256]{1,0:T(8,128)(2,1)S(1)}, u32[]{:S(2)}, u32[]{:S(2)}) collective-permute-start(bf16[256,256]{1,0:T(8,128)(2,1)S(1)} %get-tuple-element.64), channel_id=1, source_target_pairs={{0,3},{1,2},{2,1},{3,0},{32,33},{33,32},{34,35},{35,34},{4,7},{5,6... | collective-permute-start | bytes 393224 | tf_op jit(solution)/shard_map/ppermute | solution.py:334
  52.1 5.9 %collective-permute-start.8 = (bf16[256,256]{1,0:T(8,128)(2,1)S(1)}, bf16[256,256]{1,0:T(8,128)(2,1)S(1)}, u32[]{:S(2)}, u32[]{:S(2)}) collective-permute-start(bf16[256,256]{1,0:T(8,128)(2,1)S(1)} %get-tuple-element.61), channel_id=1, source_target_pairs={{0,1},{1,0},{2,3},{3,2},{32,35},{33,34},{34,33},{35,32},{4,5},{5,4... | collective-permute-start | bytes 393224 | tf_op jit(solution)/shard_map/ppermute | solution.py:334

commit v7 on v5

--- a/solution.py
+++ b/solution.py
@@ -96,7 +96,13 @@
 
 def forward(q_ref, chunks, bias_ref, low_ref, out_ref, stat_ref, scores_ref):
     places = places_of(chunks)
-    vals_t = [[v[:, of_group(g * REPEAT)].T for _, v in chunks] for g in range(KV_HEADS)]
+    vals_t = [
+        jnp.concatenate([v[:, of_group(g * REPEAT)].T for _, v in chunks], 1)
+        for g in range(KV_HEADS)
+    ]
+    first = lax.broadcasted_iota(jnp.int32, (16, len(chunks) * ROWS), 0) == 0
+    one_row = first.astype(f32).astype(bf16)
+    vals_t = [jnp.concatenate([t, one_row], 0) for t in vals_t]
     tops = {}
 
     def score_pass(h):
@@ -112,16 +118,13 @@
         tops[h] = jnp.max(top, axis=0, keepdims=True) * (SCALE * LOG2E)
 
     def weight_pass(h):
-        sums, out_t = 0.0, 0.0
-        for at, v_t in zip(places, vals_t[h // REPEAT]):
+        for at in places:
             weights = jnp.exp2(scores_ref[h % 2, at] * (SCALE * LOG2E) - tops[h])
-            low = weights.astype(bf16)
-            low_ref[h, at] = low
-            sums = sums + by_eights(jnp.sum, weights)
-            out_t = out_t + dot_nn(v_t, low)
+            low_ref[h, at] = weights.astype(bf16)
+        out_t = dot_nn(vals_t[h // REPEAT], low_ref[h])
         stat_ref[h, 0:8] = eight(tops[h])
-        stat_ref[h, 8:16] = sums
-        out_ref[h] = out_t.astype(bf16)
+        stat_ref[h, 8:16] = out_t[HEAD : HEAD + 8]
+        out_ref[h] = out_t[:HEAD].astype(bf16)
 
     score_pass(0)
     for h in range(HEADS):

time: 78.7 us -> 78.7 us (level)
  no operation moved by 1% of the time
where the time goes in v7:
time: 78.7 us; the launch traced here: 78.4 us
  starting transfers between devices  22.5 us (29%)
  blocking collectives  19.5 us (25%)
  waiting for transfers between devices  16.9 us (21%)
  Pallas kernels  16.1 us (20%)
  local copies, waits for them, and re-layouts  1.72 us (2%)
  other arithmetic  0.88 us (1%)
    all_to_all x1, blocking collectives, exchange(): return lax.all_to_all(t, axes, split_axis=0, concat_axis=0, tiled=True)  19.5 us
    pallas_call x5, Pallas kernels, call(): pl.pallas_call(kernel, grid=(1,), in_specs=[hbm if in_hbm else specs.get(...  16.1 us
    all_to_all x1, starting transfers between devices, exchange(): return lax.all_to_all(t, axes, split_axis=0, concat_axis=0, tiled=True)  13.2 us
    ppermute x12, starting transfers between devices, to_neighbour(): return lax.ppermute(t, ('c', 'x'), pairs)  9.39 us
    ppermute x12, waiting for transfers between devices, to_neighbour(): return lax.ppermute(t, ('c', 'x'), pairs)  8.57 us
    all_to_all x1, waiting for transfers between devices, exchange(): return lax.all_to_all(t, axes, split_axis=0, concat_axis=0, tiled=True)  8.36 us
  transfers between devices with their start and end apart: 13, of which 8 were waited for; matrix products, arithmetic and copies ran while one was open for 0% of the time, Pallas kernels for 17%

profile of v7, /device:TPU:1, one launch (start us, length us, event | category | flops | bytes accessed | tf_op | source)
XLA Modules:
  0.0 78.4 jit_solution(2079483263426425182)
XLA Ops:
  0.6 1.5 %broadcast_in_dim.2 = bf16[8,8,4,512]{3,2,1,0:T(4,128)(2,1)} broadcast(bf16[8,4,512]{2,1,0:T(4,128)(2,1)} %param.7), dimensions={0,2,3} | broadcast | bytes 294912 | tf_op jit(solution)/shard_map/broadcast_in_dim | solution.py:342
  2.2 13.2 %all-to-all-start = ((bf16[64,4,512]{2,1,0:T(4,128)(2,1)}), bf16[64,4,512]{2,1,0:T(4,128)(2,1)S(1)}, u32[]{:S(2)}, u32[]{:S(2)}) async-start(bf16[64,4,512]{2,1,0:T(4,128)(2,1)} %bitcast), calls=%async_computation | async-start | bytes 524288 | tf_op jit(solution)/shard_map/all_to_all | solution.py:324
  15.3 4.0 %self_forward.1 = (bf16[10,256,256]{2,1,0:T(8,128)(2,1)}, bf16[10,128,256]{2,1,0:T(8,128)(2,1)}, f32[10,16,256]{2,1,0:T(8,128)}) custom-call(s32[1,1,4]{2,1,0:T(1,128)} %lens_hbm.1, bf16[1,256,1280]{2,1,0:T(8,128)(2,1)} %q_ref.7, bf16[1,256,512]{2,1,0:T(8,128)(2,1)} %resp_ref.1), custom_call_target="tpu_custom_call" | custom-call | flops 8589934592 | bytes 256 | tf_op jit(solution)/shard_map/self_forward/pallas_call | solution.py:303
  19.3 0.0 copy-start
  19.3 0.0 copy-start.1
  19.4 0.0 copy-start.3
  19.4 0.0 copy-start.5
  19.4 8.4 %all-to-all-done = bf16[64,4,512]{2,1,0:T(4,128)(2,1)S(1)} async-done(((bf16[64,4,512]{2,1,0:T(4,128)(2,1)}), bf16[64,4,512]{2,1,0:T(4,128)(2,1)S(1)}, u32[]{:S(2)}, u32[]{:S(2)}) %all-to-all-start) | async-done | bytes 262176 | tf_op jit(solution)/shard_map/all_to_all | solution.py:324
  27.7 0.1 reshape.22.own_ref
  27.8 2.6 %collective-permute-start = (bf16[256,256]{1,0:T(8,128)(2,1)S(1)}, bf16[256,256]{1,0:T(8,128)(2,1)S(1)}, u32[]{:S(2)}, u32[]{:S(2)}) collective-permute-start(bf16[256,256]{1,0:T(8,128)(2,1)S(1)} %get-tuple-element.73), channel_id=1, source_target_pairs={{0,1},{1,0},{2,3},{3,2},{32,35},{33,34},{34,33},{35,32},{4,5},{5,4... | collective-permute-start | bytes 393224 | tf_op jit(solution)/shard_map/ppermute | solution.py:335
  30.4 0.0 collective-permute-start.3
  30.4 0.8 %collective-permute-start.1 = (bf16[256,256]{1,0:T(8,128)(2,1)S(1)}, bf16[256,256]{1,0:T(8,128)(2,1)S(1)}, u32[]{:S(2)}, u32[]{:S(2)}) collective-permute-start(bf16[256,256]{1,0:T(8,128)(2,1)S(1)} %get-tuple-element.72), channel_id=1, source_target_pairs={{0,1},{1,0},{2,3},{3,2},{32,35},{33,34},{34,33},{35,32},{4,5},{5,4... | collective-permute-start | bytes 393224 | tf_op jit(solution)/shard_map/ppermute | solution.py:335
  31.2 0.7 collective-permute-start.2
  31.9 1.1 %collective-permute-done.one_k = bf16[256,256]{1,0:T(8,128)(2,1)S(1)} collective-permute-done((bf16[256,256]{1,0:T(8,128)(2,1)S(1)}, bf16[256,256]{1,0:T(8,128)(2,1)S(1)}, u32[]{:S(2)}, u32[]{:S(2)}) %collective-permute-start) | collective-permute-done | bytes 131104 | tf_op jit(solution)/shard_map/ppermute | solution.py:335
  33.0 0.0 collective-permute-start.4
  33.0 2.7 %collective-permute-done.3.three_v = bf16[256,256]{1,0:T(8,128)(2,1)S(1)} collective-permute-done((bf16[256,256]{1,0:T(8,128)(2,1)S(1)}, bf16[256,256]{1,0:T(8,128)(2,1)S(1)}, u32[]{:S(2)}, u32[]{:S(2)}) %collective-permute-start.3) | collective-permute-done | bytes 131104 | tf_op jit(solution)/shard_map/ppermute | solution.py:335
  35.7 0.0 collective-permute-start.5
  35.7 0.2 collective-permute-done.1.one_v
  35.9 1.7 %collective-permute-done.2.three_k = bf16[256,256]{1,0:T(8,128)(2,1)S(1)} collective-permute-done((bf16[256,256]{1,0:T(8,128)(2,1)S(1)}, bf16[256,256]{1,0:T(8,128)(2,1)S(1)}, u32[]{:S(2)}, u32[]{:S(2)}) %collective-permute-start.2) | collective-permute-done | bytes 131104 | tf_op jit(solution)/shard_map/ppermute | solution.py:335
  37.6 0.0 copy-done
  37.6 3.3 %next_forward.1 = (bf16[10,768,256]{2,1,0:T(8,128)(2,1)S(1)}, bf16[10,128,256]{2,1,0:T(8,128)(2,1)S(1)}, f32[10,16,256]{2,1,0:T(8,128)S(1)}) custom-call(bf16[1,256,1280]{2,1,0:T(8,128)(2,1)S(1)} %copy-done, bf16[256,256]{1,0:T(8,128)(2,1)S(1)} %collective-permute-done.one_k, bf16[256,256]{1,0:T(8,128)(2,1)S(1)} %collective-permute-done.1.one_v, ...), custom_call_target="tpu_custom_call" | custom-call | flops 256 | bytes 256 | tf_op jit(solution)/shard_map/next_forward/pallas_call | solution.py:303
  40.9 0.0 collective-permute-done.4.k_ref
  40.9 1.1 %collective-permute-done.5.v_ref = bf16[256,256]{1,0:T(8,128)(2,1)S(1)} collective-permute-done((bf16[256,256]{1,0:T(8,128)(2,1)S(1)}, bf16[256,256]{1,0:T(8,128)(2,1)S(1)}, u32[]{:S(2)}, u32[]{:S(2)}) %collective-permute-start.5) | collective-permute-done | bytes 131104 | tf_op jit(solution)/shard_map/ppermute | solution.py:335
  42.0 0.0 copy-done.1
  42.0 0.0 copy-done.3
  42.0 0.0 copy-done.5
  42.0 2.7 %opposite.1 = (bf16[10,128,256]{2,1,0:T(8,128)(2,1)S(1)}, f32[10,128,256]{2,1,0:T(8,128)S(1)}, f32[10,24,256]{2,1,0:T(8,128)S(1)}, bf16[256,256]{1,0:T(8,128)(2,1)S(1)}, bf16[256,256]{1,0:T(8,128)(2,1)S(1)}) custom-call(bf16[1,256,1280]{2,1,0:T(8,128)(2,1)S(1)} %copy-done, bf16[1,256,1280]{2,1,0:T(8,128)(2,1)S(1)} %copy-done.1, ...), custom_call_target="tpu_custom_call" | custom-call | flops 256 | bytes 256 | tf_op jit(solution)/shard_map/opposite/pallas_call | solution.py:303
  44.7 0.3 collective-permute-start.6
  45.0 0.8 collective-permute-start.7
  45.8 0.0 copy-start.2
  45.8 0.0 copy-start.4
  45.8 2.6 %next_backward.1 = (f32[10,128,256]{2,1,0:T(8,128)S(1)}, f32[256,256]{1,0:T(8,128)S(1)}, bf16[256,256]{1,0:T(8,128)(2,1)S(1)}, bf16[256,256]{1,0:T(8,128)(2,1)S(1)}, f32[256,256]{1,0:T(8,128)S(1)}) custom-call(bf16[1,256,1280]{2,1,0:T(8,128)(2,1)S(1)} %copy-done, bf16[1,256,1280]{2,1,0:T(8,128)(2,1)S(1)} %copy-done.1, ...), custom_call_target="tpu_custom_call" | custom-call | flops 256 | bytes 256 | tf_op jit(solution)/shard_map/next_backward/pallas_call | solution.py:303
  48.4 2.1 %collective-permute-start.10 = (bf16[256,256]{1,0:T(8,128)(2,1)S(1)}, bf16[256,256]{1,0:T(8,128)(2,1)S(1)}, u32[]{:S(2)}, u32[]{:S(2)}) collective-permute-start(bf16[256,256]{1,0:T(8,128)(2,1)S(1)} %get-tuple-element.63), channel_id=1, source_target_pairs={{0,1},{1,0},{2,3},{3,2},{32,35},{33,34},{34,33},{35,32},{4,5},{5,4... | collective-permute-start | bytes 393224 | tf_op jit(solution)/shard_map/ppermute | solution.py:335
  50.5 0.2 collective-permute-start.9
  50.6 0.0 collective-permute-done.6
  50.6 0.0 collective-permute-done.7
  50.6 0.1 add_convert_fusion.2
  50.7 1.4 %collective-permute-start.11 = (bf16[256,256]{1,0:T(8,128)(2,1)S(1)}, bf16[256,256]{1,0:T(8,128)(2,1)S(1)}, u32[]{:S(2)}, u32[]{:S(2)}) collective-permute-start(bf16[256,256]{1,0:T(8,128)(2,1)S(1)} %get-tuple-element.64), channel_id=1, source_target_pairs={{0,3},{1,2},{2,1},{3,0},{32,33},{33,32},{34,35},{35,34},{4,7},{5,6... | collective-permute-start | bytes 393224 | tf_op jit(solution)/shard_map/ppermute | solution.py:335
  52.1 0.7 collective-permute-start.8
  52.8 0.0 copy-done.2
  52.8 0.0 copy-done.4
  52.8 3.5 %near_backward.1 = (bf16[1,256,1280]{2,1,0:T(8,128)(2,1)}, bf16[1,256,1280]{2,1,0:T(8,128)(2,1)}, f32[256,512]{1,0:T(8,128)S(1)}, bf16[1,256,512]{2,1,0:T(8,128)(2,1)}) custom-call(bf16[1,256,1280]{2,1,0:T(8,128)(2,1)S(1)} %copy-done, bf16[1,256,1280]{2,1,0:T(8,128)(2,1)S(1)} %copy-done.1, bf16[256,512]{1,0:T(8,128)(2,1)S(1)} %reshape.22.own_ref, ...), custom_call_target="tpu_custom_call" | custom-call | flops 256 | bytes 256 | tf_op jit(solution)/shard_map/near_backward/pallas_call | solution.py:303
  56.3 0.0 collective-permute-done.10
  56.3 0.0 collective-permute-done.9
  56.3 1.1 %collective-permute-done.11 = bf16[256,256]{1,0:T(8,128)(2,1)S(1)} collective-permute-done((bf16[256,256]{1,0:T(8,128)(2,1)S(1)}, bf16[256,256]{1,0:T(8,128)(2,1)S(1)}, u32[]{:S(2)}, u32[]{:S(2)}) %collective-permute-start.11) | collective-permute-done | bytes 131104 | tf_op jit(solution)/shard_map/ppermute | solution.py:335
  57.4 0.7 collective-permute-done.8
  58.0 0.1 add_convert_fusion.1
  58.2 0.1 reshape.23
  58.2 19.5 %all_to_all.10 = bf16[64,4,512]{2,1,0:T(4,128)(2,1)S(1)} all-to-all(bf16[64,4,512]{2,1,0:T(4,128)(2,1)S(1)} %reshape.23), channel_id=1, replica_groups=mesh['zl'=4,'c'=2,'zh'=2,'y'=4,'x'=4] {'zl','c','zh','y'}, dimensions={0} | all-to-all | bytes 524288 | tf_op jit(solution)/shard_map/all_to_all | solution.py:324
  77.7 0.7 bitcast_reduce_fusion
  (2 shorter events, 0.0 us)
Async XLA Ops:
  2.2 25.6 %all-to-all-start = ((bf16[64,4,512]{2,1,0:T(4,128)(2,1)}), bf16[64,4,512]{2,1,0:T(4,128)(2,1)S(1)}, u32[]{:S(2)}, u32[]{:S(2)}) async-start(bf16[64,4,512]{2,1,0:T(4,128)(2,1)} %bitcast), calls=%async_computation | async-start | bytes 524288 | tf_op jit(solution)/shard_map/all_to_all | solution.py:324
  19.3 18.3 %copy-start = (bf16[1,256,1280]{2,1,0:T(8,128)(2,1)S(1)}, bf16[1,256,1280]{2,1,0:T(8,128)(2,1)}, u32[]{:S(2)}) copy-start(bf16[1,256,1280]{2,1,0:T(8,128)(2,1)} %q_ref.7) | copy-start | bytes 1966084
  19.3 22.6 %copy-start.1 = (bf16[1,256,1280]{2,1,0:T(8,128)(2,1)S(1)}, bf16[1,256,1280]{2,1,0:T(8,128)(2,1)}, u32[]{:S(2)}) copy-start(bf16[1,256,1280]{2,1,0:T(8,128)(2,1)} %do_ref.5) | copy-start | bytes 1966084
  19.4 22.6 %copy-start.3 = (bf16[10,128,256]{2,1,0:T(8,128)(2,1)S(1)}, bf16[10,128,256]{2,1,0:T(8,128)(2,1)}, u32[]{:S(2)}) copy-start(bf16[10,128,256]{2,1,0:T(8,128)(2,1)} %get-tuple-element.41.self_out_ref) | copy-start | bytes 1966084
  19.4 22.6 %copy-start.5 = (f32[10,16,256]{2,1,0:T(8,128)S(1)}, f32[10,16,256]{2,1,0:T(8,128)}, u32[]{:S(2)}) copy-start(f32[10,16,256]{2,1,0:T(8,128)} %get-tuple-element.42.self_stat_ref) | copy-start | bytes 491524
  27.8 5.1 %collective-permute-start = (bf16[256,256]{1,0:T(8,128)(2,1)S(1)}, bf16[256,256]{1,0:T(8,128)(2,1)S(1)}, u32[]{:S(2)}, u32[]{:S(2)}) collective-permute-start(bf16[256,256]{1,0:T(8,128)(2,1)S(1)} %get-tuple-element.73), channel_id=1, source_target_pairs={{0,1},{1,0},{2,3},{3,2},{32,35},{33,34},{34,33},{35,32},{4,5},{5,4... | collective-permute-start | bytes 393224 | tf_op jit(solution)/shard_map/ppermute | solution.py:335
  30.4 5.3 %collective-permute-start.3 = (bf16[256,256]{1,0:T(8,128)(2,1)S(1)}, bf16[256,256]{1,0:T(8,128)(2,1)S(1)}, u32[]{:S(2)}, u32[]{:S(2)}) collective-permute-start(bf16[256,256]{1,0:T(8,128)(2,1)S(1)} %get-tuple-element.72), channel_id=1, source_target_pairs={{0,3},{1,2},{2,1},{3,0},{32,33},{33,32},{34,35},{35,34},{4,7},{5,6... | collective-permute-start | bytes 393224 | tf_op jit(solution)/shard_map/ppermute | solution.py:335
  30.4 5.5 %collective-permute-start.1 = (bf16[256,256]{1,0:T(8,128)(2,1)S(1)}, bf16[256,256]{1,0:T(8,128)(2,1)S(1)}, u32[]{:S(2)}, u32[]{:S(2)}) collective-permute-start(bf16[256,256]{1,0:T(8,128)(2,1)S(1)} %get-tuple-element.72), channel_id=1, source_target_pairs={{0,1},{1,0},{2,3},{3,2},{32,35},{33,34},{34,33},{35,32},{4,5},{5,4... | collective-permute-start | bytes 393224 | tf_op jit(solution)/shard_map/ppermute | solution.py:335
  31.2 6.4 %collective-permute-start.2 = (bf16[256,256]{1,0:T(8,128)(2,1)S(1)}, bf16[256,256]{1,0:T(8,128)(2,1)S(1)}, u32[]{:S(2)}, u32[]{:S(2)}) collective-permute-start(bf16[256,256]{1,0:T(8,128)(2,1)S(1)} %get-tuple-element.73), channel_id=1, source_target_pairs={{0,3},{1,2},{2,1},{3,0},{32,33},{33,32},{34,35},{35,34},{4,7},{5,6... | collective-permute-start | bytes 393224 | tf_op jit(solution)/shard_map/ppermute | solution.py:335
  33.0 7.9 %collective-permute-start.4 = (bf16[256,256]{1,0:T(8,128)(2,1)S(1)}, bf16[256,256]{1,0:T(8,128)(2,1)S(1)}, u32[]{:S(2)}, u32[]{:S(2)}) collective-permute-start(bf16[256,256]{1,0:T(8,128)(2,1)S(1)} %collective-permute-done.one_k), channel_id=1, source_target_pairs={{0,3},{1,2},{2,1},{3,0},{32,33},{33,32},{34,35},{35,34},{4,7},{5,6... | collective-permute-start | bytes 393224 | tf_op jit(solution)/shard_map/ppermute | solution.py:335
  35.7 6.3 %collective-permute-start.5 = (bf16[256,256]{1,0:T(8,128)(2,1)S(1)}, bf16[256,256]{1,0:T(8,128)(2,1)S(1)}, u32[]{:S(2)}, u32[]{:S(2)}) collective-permute-start(bf16[256,256]{1,0:T(8,128)(2,1)S(1)} %collective-permute-done.3.three_v), channel_id=1, source_target_pairs={{0,1},{1,0},{2,3},{3,2},{32,35},{33,34},{34,33},{35,32},{4,5},{5,4... | collective-permute-start | bytes 393224 | tf_op jit(solution)/shard_map/ppermute | solution.py:335
  44.7 5.9 %collective-permute-start.6 = (bf16[256,256]{1,0:T(8,128)(2,1)S(1)}, bf16[256,256]{1,0:T(8,128)(2,1)S(1)}, u32[]{:S(2)}, u32[]{:S(2)}) collective-permute-start(bf16[256,256]{1,0:T(8,128)(2,1)S(1)} %get-tuple-element.53), channel_id=1, source_target_pairs={{0,3},{1,2},{2,1},{3,0},{32,33},{33,32},{34,35},{35,34},{4,7},{5,6... | collective-permute-start | bytes 393224 | tf_op jit(solution)/shard_map/ppermute | solution.py:335
  45.0 5.6 %collective-permute-start.7 = (bf16[256,256]{1,0:T(8,128)(2,1)S(1)}, bf16[256,256]{1,0:T(8,128)(2,1)S(1)}, u32[]{:S(2)}, u32[]{:S(2)}) collective-permute-start(bf16[256,256]{1,0:T(8,128)(2,1)S(1)} %get-tuple-element.54), channel_id=1, source_target_pairs={{0,1},{1,0},{2,3},{3,2},{32,35},{33,34},{34,33},{35,32},{4,5},{5,4... | collective-permute-start | bytes 393224 | tf_op jit(solution)/shard_map/ppermute | solution.py:335
  45.8 7.0 %copy-start.2 = (bf16[10,256,256]{2,1,0:T(8,128)(2,1)S(1)}, bf16[10,256,256]{2,1,0:T(8,128)(2,1)}, u32[]{:S(2)}) copy-start(bf16[10,256,256]{2,1,0:T(8,128)(2,1)} %get-tuple-element.40.self_low_ref) | copy-start | bytes 3932164
  45.8 7.0 %copy-start.4 = (bf16[1,256,512]{2,1,0:T(8,128)(2,1)S(1)}, bf16[1,256,512]{2,1,0:T(8,128)(2,1)}, u32[]{:S(2)}) copy-start(bf16[1,256,512]{2,1,0:T(8,128)(2,1)} %resp_ref.1) | copy-start | bytes 786436
  48.4 7.9 %collective-permute-start.10 = (bf16[256,256]{1,0:T(8,128)(2,1)S(1)}, bf16[256,256]{1,0:T(8,128)(2,1)S(1)}, u32[]{:S(2)}, u32[]{:S(2)}) collective-permute-start(bf16[256,256]{1,0:T(8,128)(2,1)S(1)} %get-tuple-element.63), channel_id=1, source_target_pairs={{0,1},{1,0},{2,3},{3,2},{32,35},{33,34},{34,33},{35,32},{4,5},{5,4... | collective-permute-start | bytes 393224 | tf_op jit(solution)/shard_map/ppermute | solution.py:335
  50.5 5.8 %collective-permute-start.9 = (bf16[256,256]{1,0:T(8,128)(2,1)S(1)}, bf16[256,256]{1,0:T(8,128)(2,1)S(1)}, u32[]{:S(2)}, u32[]{:S(2)}) collective-permute-start(bf16[256,256]{1,0:T(8,128)(2,1)S(1)} %get-tuple-element.62), channel_id=1, source_target_pairs={{0,3},{1,2},{2,1},{3,0},{32,33},{33,32},{34,35},{35,34},{4,7},{5,6... | collective-permute-start | bytes 393224 | tf_op jit(solution)/shard_map/ppermute | solution.py:335
  50.7 6.7 %collective-permute-start.11 = (bf16[256,256]{1,0:T(8,128)(2,1)S(1)}, bf16[256,256]{1,0:T(8,128)(2,1)S(1)}, u32[]{:S(2)}, u32[]{:S(2)}) collective-permute-start(bf16[256,256]{1,0:T(8,128)(2,1)S(1)} %get-tuple-element.64), channel_id=1, source_target_pairs={{0,3},{1,2},{2,1},{3,0},{32,33},{33,32},{34,35},{35,34},{4,7},{5,6... | collective-permute-start | bytes 393224 | tf_op jit(solution)/shard_map/ppermute | solution.py:335
  52.1 5.9 %collective-permute-start.8 = (bf16[256,256]{1,0:T(8,128)(2,1)S(1)}, bf16[256,256]{1,0:T(8,128)(2,1)S(1)}, u32[]{:S(2)}, u32[]{:S(2)}) collective-permute-start(bf16[256,256]{1,0:T(8,128)(2,1)S(1)} %get-tuple-element.61), channel_id=1, source_target_pairs={{0,1},{1,0},{2,3},{3,2},{32,35},{33,34},{34,33},{35,32},{4,5},{5,4... | collective-permute-start | bytes 393224 | tf_op jit(solution)/shard_map/ppermute | solution.py:335
